TPU v7x, 32 devices: a whole 2x2x4 slice. The times are simulated.
32 devices in a mesh: sec: 4 (over y, x), blk: 8 (over z, core).
Axes of the slice: x: 2, y: 2, z: 4, core: 2. Of those that a mesh axis runs over, the one named last changes fastest.
Arguments:
- velocity: bfloat16 [16, 3, 64, 512], P(None, None, ('sec', 'blk')), may hold values from -6 to 6
- geometry: float32 [9, 64, 512], P(None, ('sec', 'blk')), may hold values from -4 to 4
- mass: float32 [64, 512], P(('sec', 'blk')), may hold values from 0.5 to 2
- snapshots: bfloat16 [512, 3, 64, 512], P(None, None, ('sec', 'blk')), may hold values from -6 to 6
- eigvecs: float32 [512, 256], P('blk'), may hold values from -0.25 to 0.25
- mode_order: int32 [256], replicated, may hold values from 0 to 255, each once
- elem_map: int32 [64], P(('sec', 'blk')), may hold values from 0 to 1, as said below
Outputs:
- coefficients: float32 [16, 256], P('sec', 'blk')
Inputs may be any that keep to these rules, and one draw needn't show every extreme that they name: `elem_map`: each aligned run of 2 entries (the elements of one device) holds each of 0 to 1 once. `mode_order`: A permutation of the modes.
All inputs are finite; a program needn't handle non-finite values.
Results may differ from a plain program's by a relative error of at most 0.0075.
Values sent between devices are 32-bit elements; how exact they have to be, the bound alone decides.
No kernel may reach another device: no remote copies, remote signals or barrier semaphores. Data moves between devices by JAX's collectives and lax.ppermute only.
A program may use at most 64 MiB of HBM per device.

v0:
```python
import math

import jax
import jax.numpy as jnp
import numpy as np
from jax import lax
from jax.sharding import PartitionSpec as P

GLL_NODES = np.array(
    [
        -1.0,
        -0.8717401485096066,
        -0.5917001814331423,
        -0.2092992179024789,
        0.2092992179024789,
        0.5917001814331423,
        0.8717401485096066,
        1.0,
    ]
)
GLL_WEIGHTS = np.array(
    [
        1.0 / 28.0,
        0.2107042271435061,
        0.3411226924835044,
        0.4124587946587038,
        0.4124587946587038,
        0.3411226924835044,
        0.2107042271435061,
        1.0 / 28.0,
    ]
)


def legendre_seven(nodes):
    before = nodes * 0.0 + 1.0
    current = nodes * 1.0
    for order in range(1, 7):
        following = ((2.0 * order + 1.0) * nodes * current - order * before) / (order + 1.0)
        before = current
        current = following
    return current


def derivative_matrix():
    degree = 7
    values = legendre_seven(GLL_NODES)
    result = np.zeros((8, 8))
    for row_idx in range(8):
        for col_idx in range(8):
            if row_idx != col_idx:
                result[row_idx, col_idx] = values[row_idx] / (
                    values[col_idx] * (GLL_NODES[row_idx] - GLL_NODES[col_idx])
                )
    result[0, 0] = -degree * (degree + 1) / 4.0
    result[7, 7] = degree * (degree + 1) / 4.0
    return result.astype(np.float32)


def point_weights():
    cube = GLL_WEIGHTS[:, None, None] * GLL_WEIGHTS[None, :, None] * GLL_WEIGHTS[None, None, :]
    return cube.reshape(512).astype(np.float32)


def vorticity_weighted(velocity, geometry, mass):
    fields, components, elements, points = velocity.shape
    highest = lax.Precision.HIGHEST
    table = jnp.asarray(derivative_matrix())
    cube = velocity.astype(jnp.float32).reshape(fields, components, elements, 8, 8, 8)
    along_r = jnp.einsum("ai,scdijk->scdajk", table, cube, precision=highest).reshape(
        fields, components, elements, points
    )
    along_s = jnp.einsum("aj,scdijk->scdiak", table, cube, precision=highest).reshape(
        fields, components, elements, points
    )
    along_t = jnp.einsum("ak,scdijk->scdija", table, cube, precision=highest).reshape(
        fields, components, elements, points
    )

    def gradient(component, coord):
        return (
            geometry[coord] * along_r[:, component]
            + geometry[3 + coord] * along_s[:, component]
            + geometry[6 + coord] * along_t[:, component]
        )

    vorticity = jnp.stack(
        [
            gradient(2, 1) - gradient(1, 2),
            gradient(0, 2) - gradient(2, 0),
            gradient(1, 0) - gradient(0, 1),
        ],
        axis=1,
    )
    return (mass * jnp.asarray(point_weights()) * vorticity).astype(jnp.bfloat16)


def shards(velocity, geometry, mass, snapshots, eigvecs, mode_order, elem_map):
    highest = lax.Precision.HIGHEST
    weighted = vorticity_weighted(velocity, geometry, mass)
    fields, components, elements, points = weighted.shape
    slot_index = lax.broadcasted_iota(jnp.int32, (elements, elements), 0)
    onehot = (slot_index == elem_map[None, :]).astype(jnp.bfloat16)
    stored = jnp.einsum(
        "fe,scep->scfp", onehot, weighted, preferred_element_type=jnp.float32
    ).astype(jnp.bfloat16)
    stored_flat = stored.reshape(fields, components * elements * points)
    snap_flat = snapshots.reshape(snapshots.shape[0], components * elements * points)
    mode_count = eigvecs.shape[1]
    selector = (
        lax.broadcasted_iota(jnp.int32, (mode_count, mode_count), 0) == mode_order[None, :]
    ).astype(jnp.float32)
    ordered = jnp.dot(eigvecs, selector, precision=highest)
    factor = 0.25 / math.sqrt(elements * lax.axis_size("sec") * lax.axis_size("blk"))
    contracted = lax.dot_general(
        stored_flat, snap_flat, (((1,), (1,)), ((), ())), preferred_element_type=jnp.float32
    )
    whole_order = lax.all_gather(ordered, "blk", axis=0, tiled=True)
    share = jnp.dot(contracted, whole_order, precision=highest)
    sections = lax.axis_size("sec")
    blocks = lax.axis_size("blk")
    field_rows = fields // sections
    mode_cols = mode_count // blocks
    arranged = share.reshape(sections, field_rows, blocks, mode_cols).transpose(0, 2, 1, 3)
    arranged = arranged.reshape(sections * blocks * field_rows, mode_cols)
    reduced = lax.psum_scatter(arranged, ("sec", "blk"), scatter_dimension=0, tiled=True)
    return reduced * factor


def solution(mesh):
    placed = (
        P(None, None, ("sec", "blk"), None),
        P(None, ("sec", "blk"), None),
        P(("sec", "blk"), None),
        P(None, None, ("sec", "blk"), None),
        P("blk", None),
        P(),
        P(("sec", "blk")),
    )
    return jax.shard_map(
        shards, mesh=mesh, in_specs=placed, out_specs=P("sec", "blk"), check_vma=False
    )
```

profile of v0, /device:TPU:0, one launch (start us, length us, event | category | flops | bytes accessed | tf_op | source)
XLA Modules:
  0.0 80.5 jit_solution(12092791080624740874)
XLA Ops:
  0.0 1.0 %slice_bitcast_fusion.5 = (f32[2,512]{1,0:T(2,128)S(1)}, f32[2,512]{1,0:T(2,128)S(1)}, f32[2,512]{1,0:T(2,128)S(1)}, f32[2,512]{1,0:T(2,128)S(1)}, f32[2,512]{1,...) fusion(f32[9,2,512]{2,1,0:T(2,128)} %param.10), kind=kLoop, calls=%fused_computation.24 | loop fusion | bytes 73728 | tf_op jit(solution)/shard_map/mul | solution.py:82
  1.0 2.2 %copy.20 = bf16[16,3,2,512]{0,3,2,1:T(8,128)(2,1)} copy(bf16[16,3,2,512]{3,2,1,0:T(2,128)(2,1)} %param.9) | data formatting | bytes 196608 | tf_op args[0]
  3.1 2.1 %convolution_bitcast_fusion.1 = f32[16,3,2,8,8,8]{0,3,5,4,2,1:T(8,128)S(1)} fusion(f32[8,8,1,1,1,1]{1,0,5,4,3,2:T(8,128)} %constant.16, bf16[16,3,2,8,8,8]{0,5,4,3,2,1:T(8,128)(2,1)} %bitcast.62), kind=kOutput, calls=%fused_computation.3 | convolution fusion | flops 4718592 | bytes 295168 | tf_op jit(solution)/shard_map/ai,scdijk->scdajk/dot_general | solution.py:70
  5.3 0.3 copy.22
  5.6 0.8 %copy-done.4 = bf16[16,3,2,512]{0,3,2,1:T(8,128)(2,1)S(1)} copy-done((bf16[16,3,2,512]{0,3,2,1:T(8,128)(2,1)S(1)}, bf16[16,3,2,512]{0,3,2,1:T(8,128)(2,1)}, u32[]{:S(2)}) %copy-start.4) | copy-done | bytes 98328
  6.4 0.8 convolution_bitcast_fusion
  7.2 0.3 copy.24
  7.5 0.8 fusion.14
  8.3 0.4 copy-done.2
  8.7 0.8 copy-done.3
  9.4 1.7 %add_subtract_fusion.2 = f32[16,1,2,512]{0,3,2,1:T(8,128)} fusion(f32[16,3,2,512]{0,3,2,1:T(8,128)S(1)} %bitcast.59, f32[16,3,2,512]{0,3,2,1:T(8,128)S(1)} %bitcast.56, f32[16,3,2,512]{0,3,2,1:T(8,128)S(1)} %bitcast.53, f32[2,512]{1,0:T(2,128)S(1)} %get-tuple-element.7, f32[2,512]{1,0:T(2,128)S(1)} %get-tuple-element.8, f32[2,512]{1,0:T(2,128)S(1)} %get-tuple-element.5, ...), kind=kLoop, calls=%fused_computation.12 | loop fusion | flops 180224 | bytes 483328 | tf_op jit(solution)/shard_map/sub | solution.py:89
  11.1 1.2 %copy.25 = f32[16,1,2,512]{3,0,2,1:T(8,128)S(1)} copy(f32[16,1,2,512]{0,3,2,1:T(8,128)} %add_subtract_fusion.2) | data formatting | bytes 131072 | tf_op jit(solution)/shard_map/sub | solution.py:89
  12.3 3.1 %add_subtract_fusion.1 = f32[16,1,2,512]{0,3,2,1:T(8,128)} fusion(f32[16,3,2,512]{0,3,2,1:T(8,128)} %bitcast.60, f32[16,3,2,512]{0,3,2,1:T(8,128)} %bitcast.57, f32[16,3,2,512]{0,3,2,1:T(8,128)} %bitcast.54, f32[2,512]{1,0:T(2,128)S(1)} %get-tuple-element.12, f32[2,512]{1,0:T(2,128)S(1)} %get-tuple-element.13, f32[2,512]{1,0:T(2,128)S(1)} %get-tuple-element.6, ...), kind=kLoop, calls=%fused_computation.11 | loop fusion | flops 180224 | bytes 483328 | tf_op jit(solution)/shard_map/sub | solution.py:90
  15.4 1.2 %copy.26 = f32[16,1,2,512]{3,0,2,1:T(8,128)S(1)} copy(f32[16,1,2,512]{0,3,2,1:T(8,128)} %add_subtract_fusion.1) | data formatting | bytes 131072 | tf_op jit(solution)/shard_map/sub | solution.py:90
  16.6 3.1 %add_subtract_fusion = f32[16,1,2,512]{0,3,2,1:T(8,128)} fusion(f32[16,3,2,512]{0,3,2,1:T(8,128)} %bitcast.61, f32[16,3,2,512]{0,3,2,1:T(8,128)} %bitcast.58, f32[16,3,2,512]{0,3,2,1:T(8,128)} %bitcast.55, f32[2,512]{1,0:T(2,128)S(1)} %get-tuple-element.12, f32[2,512]{1,0:T(2,128)S(1)} %get-tuple-element.13, f32[2,512]{1,0:T(2,128)S(1)} %get-tuple-element.6, ...), kind=kLoop, calls=%fused_computation.10 | loop fusion | flops 180224 | bytes 483328 | tf_op jit(solution)/shard_map/sub | solution.py:91
  19.7 1.2 %copy.27 = f32[16,1,2,512]{3,0,2,1:T(8,128)S(1)} copy(f32[16,1,2,512]{0,3,2,1:T(8,128)} %add_subtract_fusion) | data formatting | bytes 131072 | tf_op jit(solution)/shard_map/sub | solution.py:91
  20.9 0.3 fusion.2
  21.2 0.9 %fusion.3 = f32[16,512]{1,0:T(8,128)S(1)} fusion(bf16[512,3,2,512]{3,2,1,0:T(2,128)(2,1)S(1)} %copy-done, bf16[16,3,2,512]{3,2,1,0:T(2,128)(2,1)S(1)} %fusion.2), kind=kOutput, calls=%fused_computation.7 | convolution fusion | flops 50331648 | bytes 3276800 | tf_op jit(solution)/shard_map/dot_general | solution.py:115
  22.1 0.2 convolution_bitcast_fusion.2
  22.4 16.6 %all_gather.3 = f32[512,256]{1,0:T(8,128)S(1)} all-gather(f32[64,256]{1,0:T(8,128)S(1)} %convolution_bitcast_fusion.2), channel_id=1, replica_groups=mesh['sec'=4,'blk'=8] {'blk'}, dimensions={0}, use_global_device_ids=true | all-gather | bytes 589824 | tf_op jit(solution)/shard_map/all_gather | solution.py:118
  39.0 0.3 fusion.15
  39.2 0.1 reshape.28
  39.4 40.5 %all-reduce = f32[128,32]{1,0:T(8,128)S(1)} all-reduce(f32[128,32]{1,0:T(8,128)S(1)} %bitcast.66), channel_id=2, replica_groups=mesh['sec'=4,'blk'=8] {'sec','blk'}, use_global_device_ids=true, to_apply=%region_0.0.clone | all-reduce | flops 4096 | bytes 32768
  79.9 0.6 dynamic-slice_multiply_fusion
  (22 shorter events, 0.1 us)
Async XLA Ops:
  0.0 21.2 %copy-start = (bf16[512,3,2,512]{3,2,1,0:T(2,128)(2,1)S(1)}, bf16[512,3,2,512]{3,2,1,0:T(2,128)(2,1)}, u32[]{:S(2)}) copy-start(bf16[512,3,2,512]{3,2,1,0:T(2,128)(2,1)} %param.12) | copy-start | bytes 9437188
  5.3 1.1 %copy-start.4 = (bf16[16,3,2,512]{0,3,2,1:T(8,128)(2,1)S(1)}, bf16[16,3,2,512]{0,3,2,1:T(8,128)(2,1)}, u32[]{:S(2)}) copy-start(bf16[16,3,2,512]{0,3,2,1:T(8,128)(2,1)} %copy.20) | copy-start | bytes 294916
  5.3 1.1 %copy-start.6 = (f32[8,8,1,1,1,1]{1,0,5,4,3,2:T(8,128)S(1)}, f32[8,8,1,1,1,1]{1,0,5,4,3,2:T(8,128)}, u32[]{:S(2)}) copy-start(f32[8,8,1,1,1,1]{1,0,5,4,3,2:T(8,128)} %constant.16) | copy-start | bytes 772
  5.6 2.7 %copy-start.1 = (f32[16,3,2,8,8,8]{0,5,4,3,2,1:T(8,128)}, f32[16,3,2,8,8,8]{0,5,4,3,2,1:T(8,128)S(1)}, u32[]{:S(2)}) copy-start(f32[16,3,2,8,8,8]{0,5,4,3,2,1:T(8,128)S(1)} %copy.22) | copy-start | bytes 589828
  7.5 1.2 %copy-start.2 = (f32[16,3,2,8,8,8]{0,5,4,3,2,1:T(8,128)}, f32[16,3,2,8,8,8]{0,5,4,3,2,1:T(8,128)S(1)}, u32[]{:S(2)}) copy-start(f32[16,3,2,8,8,8]{0,5,4,3,2,1:T(8,128)S(1)} %copy.24) | copy-start | bytes 589828
  8.3 1.1 %copy-start.3 = (f32[8,16,3,2,8,8]{1,0,5,4,3,2:T(8,128)}, f32[8,16,3,2,8,8]{1,0,5,4,3,2:T(8,128)S(1)}, u32[]{:S(2)}) copy-start(f32[8,16,3,2,8,8]{1,0,5,4,3,2:T(8,128)S(1)} %fusion.14) | copy-start | bytes 589828
  16.6 4.3 %copy-start.7 = (f32[2,512]{1,0:T(2,128)S(1)}, f32[2,512]{1,0:T(2,128)}, u32[]{:S(2)}) copy-start(f32[2,512]{1,0:T(2,128)} %param.11) | copy-start | bytes 12292
  16.6 4.3 %copy-start.8 = (f32[512]{0:T(512)S(1)}, f32[512]{0:T(512)}, u32[]{:S(2)}) copy-start(f32[512]{0:T(512)} %constant.7.clone) | copy-start | bytes 6148
  16.6 4.3 %copy-start.10 = (s32[2]{0:T(128)S(1)}, s32[2]{0:T(128)}, u32[]{:S(2)}) copy-start(s32[2]{0:T(128)} %param.15) | copy-start | bytes 28
  21.2 0.9 %copy-start.5 = (f32[64,256]{1,0:T(8,128)S(1)}, f32[64,256]{1,0:T(8,128)}, u32[]{:S(2)}) copy-start(f32[64,256]{1,0:T(8,128)} %param.13) | copy-start | bytes 196612
  21.2 0.9 %copy-start.9 = (s32[256]{0:T(256)S(1)}, s32[256]{0:T(256)}, u32[]{:S(2)}) copy-start(s32[256]{0:T(256)} %param.14) | copy-start | bytes 3076
where the time goes:
time: 80.9 us; the launch traced here: 80.5 us
  blocking collectives  57.1 us (71%)
  local copies, waits for them, and re-layouts  9.47 us (12%)
  other arithmetic  8.41 us (10%)
  matrix products  5.34 us (7%)
    unnamed x1, blocking collectives  40.5 us
    all_gather x1, blocking collectives, shards(): whole_order = lax.all_gather(ordered, 'blk', axis=0, tiled=True)  16.6 us
    unnamed x23, local copies, waits for them, and re-layouts  4.16 us
    sub x1, other arithmetic, vorticity_weighted(): gradient(1, 0) - gradient(0, 1)  3.08 us
    sub x1, other arithmetic, vorticity_weighted(): gradient(0, 2) - gradient(2, 0)  3.06 us
    dot_general x1, matrix products, vorticity_weighted(): jnp.einsum('ai,scdijk->scdajk', table, cube, precision=highest)  2.13 us
    sub x1, other arithmetic, vorticity_weighted(): gradient(2, 1) - gradient(1, 2)  1.66 us

commit v1 on v0

--- a/solution.py
+++ b/solution.py
@@ -95,6 +95,81 @@
     return (mass * jnp.asarray(point_weights()) * vorticity).astype(jnp.bfloat16)
 
 
+def exchange(block, ds, db):
+    sections, blocks = lax.axis_size("sec"), lax.axis_size("blk")
+    pairs = [
+        (s * blocks + b, (s ^ ds) * blocks + (b ^ db))
+        for s in range(sections)
+        for b in range(blocks)
+    ]
+    return lax.ppermute(block, ("sec", "blk"), pairs)
+
+
+def reduced_sums(partial):
+    sections, blocks = lax.axis_size("sec"), lax.axis_size("blk")
+    section = lax.axis_index("sec")
+    sums = partial + exchange(partial, 0, 1)
+    step = sections // 2
+    while step:
+        half = sums.shape[0] // 2
+        low, high = sums[:half], sums[half:]
+        upper = (section & step) != 0
+        sums = jnp.where(upper, high, low) + exchange(jnp.where(upper, low, high), step, 1)
+        step //= 2
+    step = 2
+    while step < blocks:
+        sums = sums + exchange(sums, 0, step | 1)
+        step *= 2
+    return sums
+
+
+def own_columns(eigvecs, mode_order):
+    blocks = lax.axis_size("blk")
+    block = lax.axis_index("blk")
+    mode_count = mode_order.shape[0]
+    cols = mode_count // blocks
+    relative = []
+    for place in range(blocks):
+        core, chip = place // (blocks // 2), place % (blocks // 2)
+        odd = bin(chip).count("1") & 1
+        relative.append(2 * chip + (core ^ odd))
+    wanted = jnp.take(
+        mode_order.reshape(blocks, cols), block ^ jnp.asarray(relative, jnp.int32), axis=0
+    ).reshape(mode_count)
+    selector = (
+        wanted[:, None] == lax.broadcasted_iota(jnp.int32, (mode_count, mode_count), 1)
+    ).astype(jnp.float32)
+    table = lax.dot_general(
+        selector, eigvecs, (((1,), (1,)), ((), ())), precision=lax.Precision.HIGHEST
+    )
+    half = mode_count // 2
+    keep, got = table[:half], exchange(table[half:], 0, 1)
+    odd = (block & 1) != 0
+    held = [
+        jnp.concatenate([jnp.where(odd, got, keep), jnp.where(odd, keep, got)], axis=1)
+    ]
+    step = blocks // 2
+    while step > 1:
+        half = held[0].shape[0] // 2
+        send = jnp.concatenate([part[half:] for part in held], axis=0)
+        got = exchange(send, 0, step | 1)
+        held = [part[:half] for part in held] + [
+            got[i * half : (i + 1) * half] for i in range(len(held))
+        ]
+        step //= 2
+    return held
+
+
+def pair_order():
+    blocks = lax.axis_size("blk")
+    order = [0]
+    step = blocks // 2
+    while step > 1:
+        order += [other ^ step for other in order]
+        step //= 2
+    return [other // 2 for other in order]
+
+
 def shards(velocity, geometry, mass, snapshots, eigvecs, mode_order, elem_map):
     highest = lax.Precision.HIGHEST
     weighted = vorticity_weighted(velocity, geometry, mass)
@@ -106,25 +181,23 @@
     ).astype(jnp.bfloat16)
     stored_flat = stored.reshape(fields, components * elements * points)
     snap_flat = snapshots.reshape(snapshots.shape[0], components * elements * points)
-    mode_count = eigvecs.shape[1]
-    selector = (
-        lax.broadcasted_iota(jnp.int32, (mode_count, mode_count), 0) == mode_order[None, :]
-    ).astype(jnp.float32)
-    ordered = jnp.dot(eigvecs, selector, precision=highest)
     factor = 0.25 / math.sqrt(elements * lax.axis_size("sec") * lax.axis_size("blk"))
     contracted = lax.dot_general(
         stored_flat, snap_flat, (((1,), (1,)), ((), ())), preferred_element_type=jnp.float32
     )
-    whole_order = lax.all_gather(ordered, "blk", axis=0, tiled=True)
-    share = jnp.dot(contracted, whole_order, precision=highest)
-    sections = lax.axis_size("sec")
-    blocks = lax.axis_size("blk")
-    field_rows = fields // sections
-    mode_cols = mode_count // blocks
-    arranged = share.reshape(sections, field_rows, blocks, mode_cols).transpose(0, 2, 1, 3)
-    arranged = arranged.reshape(sections * blocks * field_rows, mode_cols)
-    reduced = lax.psum_scatter(arranged, ("sec", "blk"), scatter_dimension=0, tiled=True)
-    return reduced * factor
+    columns = own_columns(eigvecs, mode_order)
+    sums = reduced_sums(contracted)
+    chips = lax.axis_size("blk") // 2
+    chip = lax.axis_index("blk") // 2
+    parts = jnp.take(
+        sums.reshape(sums.shape[0], chips, sums.shape[1] // chips),
+        chip ^ jnp.asarray(pair_order(), jnp.int32),
+        axis=1,
+    ).reshape(sums.shape)
+    share = lax.dot_general(
+        parts, jnp.concatenate(columns, axis=1), (((1,), (1,)), ((), ())), precision=highest
+    )
+    return share * factor
 
 
 def solution(mesh):

time: 80.9 us -> 37.3 us (0.46)
  blocking collectives: 57.1 us -> 0 us
  starting transfers between devices: 0 us -> 12.1 us
  waiting for transfers between devices: 0 us -> 4.81 us
  other arithmetic: 8.41 us -> 5.43 us
  local copies, waits for them, and re-layouts: 9.47 us -> 8.32 us
    unnamed x1 -> x0, blocking collectives: 40.5 us -> none
    all_gather x1 -> x0, blocking collectives: 16.6 us -> none  [shards(): whole_order = lax.all_gather(ordered, 'blk', axis=0, tiled=True)]
    ppermute x0 -> x8, starting transfers between devices: none -> 12.1 us  [exchange(): return lax.ppermute(block, ('sec', 'blk'), pairs)]
    ppermute x0 -> x8, waiting for transfers between devices: none -> 4.81 us  [exchange(): return lax.ppermute(block, ('sec', 'blk'), pairs)]
    unnamed x23, local copies, waits for them, and re-layouts: 4.16 us -> 2.28 us
    sub x1, other arithmetic: 3.08 us -> 1.68 us  [vorticity_weighted(): gradient(1, 0) - gradient(0, 1)]
    sub x1, other arithmetic: 3.06 us -> 1.69 us  [vorticity_weighted(): gradient(0, 2) - gradient(2, 0)]
    dot_general x1, matrix products: 0.76 us -> 1.98 us  [vorticity_weighted(): jnp.einsum('aj,scdijk->scdiak', table, cube, precision=highest)]
  transfers between devices with their start and end apart: 0 -> 8, of which waited for: 0 -> 4; matrix products, arithmetic and copies ran while one was open for 0% -> 6% of each run, Pallas kernels for 0% -> 0%
where the time goes in v1:
time: 37.3 us; the launch traced here: 36.9 us
  starting transfers between devices  12.1 us (32%)
  local copies, waits for them, and re-layouts  8.32 us (22%)
  matrix products  6.02 us (16%)
  other arithmetic  5.43 us (15%)
  waiting for transfers between devices  4.81 us (13%)
    ppermute x8, starting transfers between devices, exchange(): return lax.ppermute(block, ('sec', 'blk'), pairs)  12.1 us
    ppermute x8, waiting for transfers between devices, exchange(): return lax.ppermute(block, ('sec', 'blk'), pairs)  4.81 us
    unnamed x23, local copies, waits for them, and re-layouts  2.28 us
    dot_general x1, matrix products, vorticity_weighted(): jnp.einsum('aj,scdijk->scdiak', table, cube, precision=highest)  1.98 us
    sub x1, other arithmetic, vorticity_weighted(): gradient(2, 1) - gradient(1, 2)  1.69 us
    sub x1, other arithmetic, vorticity_weighted(): gradient(0, 2) - gradient(2, 0)  1.69 us
    sub x1, other arithmetic, vorticity_weighted(): gradient(1, 0) - gradient(0, 1)  1.68 us
    sub x1, local copies, waits for them, and re-layouts, vorticity_weighted(): gradient(2, 1) - gradient(1, 2)  1.24 us
  transfers between devices with their start and end apart: 8, of which 4 were waited for; matrix products, arithmetic and copies ran while one was open for 6% of the time, Pallas kernels for 0%

profile of v1, /device:TPU:0, one launch (start us, length us, event | category | flops | bytes accessed | tf_op | source)
XLA Modules:
  0.0 36.9 jit_solution(13670140863739870242)
XLA Ops:
  0.0 2.2 %copy.23 = bf16[16,3,2,512]{0,3,2,1:T(8,128)(2,1)} copy(bf16[16,3,2,512]{3,2,1,0:T(2,128)(2,1)} %param.11) | data formatting | bytes 196608 | tf_op args[0]
  2.2 2.0 %convolution_bitcast_fusion = f32[16,3,2,8,8,8]{0,4,5,3,2,1:T(8,128)S(1)} fusion(f32[8,8,1,1,1,1]{1,0,5,4,3,2:T(8,128)} %constant.74, bf16[16,3,2,8,8,8]{0,5,4,3,2,1:T(8,128)(2,1)} %bitcast.65), kind=kOutput, calls=%fused_computation.4 | convolution fusion | flops 4718592 | bytes 295168 | tf_op jit(solution)/shard_map/aj,scdijk->scdiak/dot_general | solution.py:73
  4.2 1.0 %convolution_bitcast_fusion.1 = f32[16,3,2,8,8,8]{0,3,5,4,2,1:T(8,128)S(1)} fusion(f32[8,8,1,1,1,1]{1,0,5,4,3,2:T(8,128)S(1)} %copy-done.3, bf16[16,3,2,8,8,8]{0,5,4,3,2,1:T(8,128)(2,1)S(1)} %bitcast.66), kind=kOutput, calls=%fused_computation.5 | convolution fusion | flops 4718592 | bytes 295168 | tf_op jit(solution)/shard_map/ai,scdijk->scdajk/dot_general | solution.py:70
  5.2 0.8 %fusion.31 = f32[8,16,3,2,8,8]{1,0,5,4,3,2:T(8,128)S(1)} fusion(f32[8,8,1,1,1,1]{1,0,5,4,3,2:T(8,128)S(1)} %copy-done.3, bf16[16,3,2,8,8,8]{0,5,4,3,2,1:T(8,128)(2,1)S(1)} %bitcast.67), kind=kOutput, calls=%fused_computation.73 | convolution fusion | flops 4718592 | bytes 295168 | tf_op jit(solution)/shard_map/ak,scdijk->scdija/dot_general | solution.py:76
  6.7 1.7 %add_subtract_fusion.2 = f32[16,1,2,512]{0,3,2,1:T(8,128)} fusion(f32[16,3,2,512]{0,3,2,1:T(8,128)S(1)} %bitcast.56, f32[16,3,2,512]{0,3,2,1:T(8,128)S(1)} %bitcast.59, f32[16,3,2,512]{0,3,2,1:T(8,128)S(1)} %bitcast.62, f32[2,512]{1,0:T(2,128)S(1)} %get-tuple-element.17, f32[2,512]{1,0:T(2,128)S(1)} %get-tuple-element.18, ...), kind=kLoop, calls=%fused_computation.14 | loop fusion | flops 180224 | bytes 483328 | tf_op jit(solution)/shard_map/sub | solution.py:89
  8.4 1.7 %add_subtract_fusion.1 = f32[16,1,2,512]{0,3,2,1:T(8,128)} fusion(f32[16,3,2,512]{0,3,2,1:T(8,128)S(1)} %bitcast.57, f32[16,3,2,512]{0,3,2,1:T(8,128)S(1)} %bitcast.60, f32[16,3,2,512]{0,3,2,1:T(8,128)S(1)} %bitcast.63, f32[2,512]{1,0:T(2,128)S(1)} %get-tuple-element.22, f32[2,512]{1,0:T(2,128)S(1)} %get-tuple-element.23, ...), kind=kLoop, calls=%fused_computation.13 | loop fusion | flops 180224 | bytes 483328 | tf_op jit(solution)/shard_map/sub | solution.py:90
  10.0 1.7 %add_subtract_fusion = f32[16,1,2,512]{0,3,2,1:T(8,128)} fusion(f32[16,3,2,512]{0,3,2,1:T(8,128)S(1)} %bitcast.58, f32[16,3,2,512]{0,3,2,1:T(8,128)S(1)} %bitcast.61, f32[16,3,2,512]{0,3,2,1:T(8,128)S(1)} %bitcast.64, f32[2,512]{1,0:T(2,128)S(1)} %get-tuple-element.22, f32[2,512]{1,0:T(2,128)S(1)} %get-tuple-element.23, f32[2,512]{1,0:T(2,128)S(1)} %get-tuple-element.16, ...), kind=kLoop, calls=%fused_computation.12 | loop fusion | flops 180224 | bytes 483328 | tf_op jit(solution)/shard_map/sub | solution.py:91
  11.7 1.2 %copy.28 = f32[16,1,2,512]{3,0,2,1:T(8,128)S(1)} copy(f32[16,1,2,512]{0,3,2,1:T(8,128)} %add_subtract_fusion.2) | data formatting | bytes 131072 | tf_op jit(solution)/shard_map/sub | solution.py:89
  13.0 1.2 %copy.29 = f32[16,1,2,512]{3,0,2,1:T(8,128)S(1)} copy(f32[16,1,2,512]{0,3,2,1:T(8,128)} %add_subtract_fusion.1) | data formatting | bytes 131072 | tf_op jit(solution)/shard_map/sub | solution.py:90
  14.2 1.2 %copy.30 = f32[16,1,2,512]{3,0,2,1:T(8,128)S(1)} copy(f32[16,1,2,512]{0,3,2,1:T(8,128)} %add_subtract_fusion) | data formatting | bytes 131072 | tf_op jit(solution)/shard_map/sub | solution.py:91
  15.8 0.9 %fusion.3 = f32[16,512]{1,0:T(8,128)S(1)} fusion(bf16[512,3,2,512]{3,2,1,0:T(2,128)(2,1)S(1)} %copy-done, bf16[16,3,2,512]{3,2,1,0:T(2,128)(2,1)S(1)} %fusion.2), kind=kOutput, calls=%fused_computation.8 | convolution fusion | flops 50331648 | bytes 3276800 | tf_op jit(solution)/shard_map/dot_general | solution.py:185
  17.3 0.6 %gather_fusion.1 = s32[8,32]{1,0:T(8,128)S(1)} fusion(s32[8,32]{1,0:T(8,128)S(1)} %reshape.54, s32[1024]{0:T(1024)S(1)} %pad_clamp_fusion), kind=kCustom, calls=%fused_computation.1 | custom fusion | bytes 2080 | tf_op jit(solution)/shard_map/jit(_take)/gather | solution.py:136
  18.6 2.7 %collective-permute-start.1 = (f32[8,512]{1,0:T(8,128)S(1)}, f32[8,512]{1,0:T(8,128)S(1)}, u32[]{:S(2)}, u32[]{:S(2)}) collective-permute-start(f32[8,512]{1,0:T(8,128)S(1)} %slice_select_fusion.2), channel_id=1, source_target_pairs={{0,17},{1,16},{2,19},{3,18},{4,21},{5,20},{6,23},{7,22},{8,25},{9,... | collective-permute-start | bytes 49160 | tf_op jit(solution)/shard_map/ppermute | solution.py:105
  21.3 1.4 %collective-permute-done.1 = f32[8,512]{1,0:T(8,128)S(1)} collective-permute-done((f32[8,512]{1,0:T(8,128)S(1)}, f32[8,512]{1,0:T(8,128)S(1)}, u32[]{:S(2)}, u32[]{:S(2)}) %collective-permute-start.1) | collective-permute-done | bytes 16416 | tf_op jit(solution)/shard_map/ppermute | solution.py:105
  22.7 1.8 %collective-permute-start.2 = (f32[4,512]{1,0:T(4,128)S(1)}, f32[4,512]{1,0:T(4,128)S(1)}, u32[]{:S(2)}, u32[]{:S(2)}) collective-permute-start(f32[4,512]{1,0:T(4,128)S(1)} %slice_select_fusion.3), channel_id=1, source_target_pairs={{0,9},{1,8},{2,11},{3,10},{4,13},{5,12},{6,15},{7,14},{8,1},{9,0},... | collective-permute-start | bytes 24584 | tf_op jit(solution)/shard_map/ppermute | solution.py:105
  24.7 2.7 %collective-permute-start.6 = (f32[64,128]{0,1:T(8,128)S(1)}, f32[64,128]{0,1:T(8,128)S(1)}, u32[]{:S(2)}, u32[]{:S(2)}) collective-permute-start(f32[64,128]{0,1:T(8,128)S(1)} %fusion.13), channel_id=1, source_target_pairs={{0,5},{1,4},{2,7},{3,6},{4,1},{5,0},{6,3},{7,2},{8,13},{9,12},{10,... | collective-permute-start | bytes 98312 | tf_op jit(solution)/shard_map/ppermute | solution.py:105
  27.3 1.3 %collective-permute-start.3 = (f32[4,512]{1,0:T(4,128)S(1)}, f32[4,512]{1,0:T(4,128)S(1)}, u32[]{:S(2)}, u32[]{:S(2)}) collective-permute-start(f32[4,512]{1,0:T(4,128)S(1)} %select_add_fusion.1), channel_id=1, source_target_pairs={{0,3},{1,2},{2,1},{3,0},{4,7},{5,6},{6,5},{7,4},{8,11},{9,10},{10,... | collective-permute-start | bytes 24584 | tf_op jit(solution)/shard_map/ppermute | solution.py:105
  28.7 1.8 %collective-permute-done.3 = f32[4,512]{1,0:T(4,128)S(1)} collective-permute-done((f32[4,512]{1,0:T(4,128)S(1)}, f32[4,512]{1,0:T(4,128)S(1)}, u32[]{:S(2)}, u32[]{:S(2)}) %collective-permute-start.3) | collective-permute-done | bytes 8224 | tf_op jit(solution)/shard_map/ppermute | solution.py:105
  30.5 1.4 %collective-permute-start.4 = (f32[4,512]{1,0:T(4,128)S(1)}, f32[4,512]{1,0:T(4,128)S(1)}, u32[]{:S(2)}, u32[]{:S(2)}) collective-permute-start(f32[4,512]{1,0:T(4,128)S(1)} %add.88), channel_id=1, source_target_pairs={{0,5},{1,4},{2,7},{3,6},{4,1},{5,0},{6,3},{7,2},{8,13},{9,12},{10,... | collective-permute-start | bytes 24584 | tf_op jit(solution)/shard_map/ppermute | solution.py:105
  32.0 1.7 %collective-permute-start.7 = (f32[64,128]{0,1:T(8,128)S(1)}, f32[64,128]{0,1:T(8,128)S(1)}, u32[]{:S(2)}, u32[]{:S(2)}) collective-permute-start(f32[64,128]{0,1:T(8,128)S(1)} %fusion.15), channel_id=1, source_target_pairs={{0,3},{1,2},{2,1},{3,0},{4,7},{5,6},{6,5},{7,4},{8,11},{9,10},{10,... | collective-permute-start | bytes 98312 | tf_op jit(solution)/shard_map/ppermute | solution.py:105
  33.8 0.7 %collective-permute-done.4 = f32[4,512]{1,0:T(4,128)S(1)} collective-permute-done((f32[4,512]{1,0:T(4,128)S(1)}, f32[4,512]{1,0:T(4,128)S(1)}, u32[]{:S(2)}, u32[]{:S(2)}) %collective-permute-start.4) | collective-permute-done | bytes 8224 | tf_op jit(solution)/shard_map/ppermute | solution.py:105
  34.5 0.6 %gather_fusion = f32[4,4,128]{2,1,0:T(4,128)S(1)} fusion(f32[4,4,128]{2,0,1:T(4,128)S(1)} %add_bitcast_fusion, s32[1024]{0:T(1024)S(1)} %pad_clamp_fusion.1), kind=kCustom, calls=%fused_computation | custom fusion | bytes 16400 | tf_op jit(solution)/shard_map/jit(_take)/gather | solution.py:192
  35.0 0.9 %collective-permute-done.7 = f32[64,128]{0,1:T(8,128)S(1)} collective-permute-done((f32[64,128]{0,1:T(8,128)S(1)}, f32[64,128]{0,1:T(8,128)S(1)}, u32[]{:S(2)}, u32[]{:S(2)}) %collective-permute-start.7) | collective-permute-done | bytes 32800 | tf_op jit(solution)/shard_map/ppermute | solution.py:105
  36.2 0.8 %convolution_multiply_fusion = f32[4,32]{1,0:T(4,128)} fusion(f32[32,128]{1,0:T(8,128)S(1)} %copy.38, f32[32,128]{1,0:T(8,128)S(1)} %copy.37, f32[32,128]{1,0:T(8,128)S(1)} %copy.36, f32[32,128]{1,0:T(8,128)S(1)} %copy.35, f32[4,4,128]{2,1,0:T(4,128)S(1)} %gather_fusion, pred[512]{0:T(512)(128)(4,1)S(1)} %broadcast_bitcast_fusion), kind=kOutput, calls=%fused_computation.9 | convolution fusion | flops 837760 | bytes 74752 | tf_op jit(solution)/shard_map/dot_general | solution.py:197
  (61 shorter events, 2.9 us)
Async XLA Ops:
  0.0 15.7 %copy-start = (bf16[512,3,2,512]{3,2,1,0:T(2,128)(2,1)S(1)}, bf16[512,3,2,512]{3,2,1,0:T(2,128)(2,1)}, u32[]{:S(2)}) copy-start(bf16[512,3,2,512]{3,2,1,0:T(2,128)(2,1)} %param.14) | copy-start | bytes 9437188
  0.0 4.2 %copy-start.3 = (f32[8,8,1,1,1,1]{1,0,5,4,3,2:T(8,128)S(1)}, f32[8,8,1,1,1,1]{1,0,5,4,3,2:T(8,128)}, u32[]{:S(2)}) copy-start(f32[8,8,1,1,1,1]{1,0,5,4,3,2:T(8,128)} %constant.74) | copy-start | bytes 772
  2.2 2.0 %copy-start.1 = (bf16[16,3,2,512]{0,3,2,1:T(8,128)(2,1)S(1)}, bf16[16,3,2,512]{0,3,2,1:T(8,128)(2,1)}, u32[]{:S(2)}) copy-start(bf16[16,3,2,512]{0,3,2,1:T(8,128)(2,1)} %copy.23) | copy-start | bytes 294916
  5.2 0.8 %copy-start.4 = (f32[9,2,512]{2,1,0:T(2,128)S(1)}, f32[9,2,512]{2,1,0:T(2,128)}, u32[]{:S(2)}) copy-start(f32[9,2,512]{2,1,0:T(2,128)} %param.12) | copy-start | bytes 110596
  11.7 3.7 %copy-start.5 = (f32[2,512]{1,0:T(2,128)S(1)}, f32[2,512]{1,0:T(2,128)}, u32[]{:S(2)}) copy-start(f32[2,512]{1,0:T(2,128)} %param.13) | copy-start | bytes 12292
  11.7 3.7 %copy-start.6 = (f32[512]{0:T(512)S(1)}, f32[512]{0:T(512)}, u32[]{:S(2)}) copy-start(f32[512]{0:T(512)} %constant.66.clone) | copy-start | bytes 6148
  11.7 3.7 %copy-start.10 = (s32[2]{0:T(128)S(1)}, s32[2]{0:T(128)}, u32[]{:S(2)}) copy-start(s32[2]{0:T(128)} %param.17) | copy-start | bytes 28
  15.7 1.4 %copy-start.9 = (s32[8]{0:T(128)S(1)}, s32[8]{0:T(128)}, u32[]{:S(2)}) copy-start(s32[8]{0:T(128)} %constant.67.clone) | copy-start | bytes 100
  15.7 1.4 %copy-start.7 = (s32[256]{0:T(256)S(1)}, s32[256]{0:T(256)}, u32[]{:S(2)}) copy-start(s32[256]{0:T(256)} %param.16) | copy-start | bytes 3076
  15.8 2.2 %copy-start.2 = (f32[64,256]{1,0:T(8,128)S(1)}, f32[64,256]{1,0:T(8,128)}, u32[]{:S(2)}) copy-start(f32[64,256]{1,0:T(8,128)} %param.15) | copy-start | bytes 196612
  15.8 2.7 %copy-start.8 = (s32[4]{0:T(128)S(1)}, s32[4]{0:T(128)}, u32[]{:S(2)}) copy-start(s32[4]{0:T(128)} %constant.68.clone) | copy-start | bytes 52
  16.7 1.9 %collective-permute-start = (f32[16,512]{1,0:T(8,128)S(1)}, f32[16,512]{1,0:T(8,128)S(1)}, u32[]{:S(2)}, u32[]{:S(2)}) collective-permute-start(f32[16,512]{1,0:T(8,128)S(1)} %fusion.3), channel_id=1, source_target_pairs={{0,1},{1,0},{2,3},{3,2},{4,5},{5,4},{6,7},{7,6},{8,9},{9,8},{10,11... | collective-permute-start | bytes 98312 | tf_op jit(solution)/shard_map/ppermute | solution.py:105
  18.4 2.9 %collective-permute-start.5 = (f32[128,64]{0,1:T(8,128)S(1)}, f32[128,64]{0,1:T(8,128)S(1)}, u32[]{:S(2)}, u32[]{:S(2)}) collective-permute-start(f32[128,64]{0,1:T(8,128)S(1)} %slice.162), channel_id=1, source_target_pairs={{0,1},{1,0},{2,3},{3,2},{4,5},{5,4},{6,7},{7,6},{8,9},{9,8},{10,11... | collective-permute-start | bytes 98312 | tf_op jit(solution)/shard_map/ppermute | solution.py:105
  18.6 4.1 %collective-permute-start.1 = (f32[8,512]{1,0:T(8,128)S(1)}, f32[8,512]{1,0:T(8,128)S(1)}, u32[]{:S(2)}, u32[]{:S(2)}) collective-permute-start(f32[8,512]{1,0:T(8,128)S(1)} %slice_select_fusion.2), channel_id=1, source_target_pairs={{0,17},{1,16},{2,19},{3,18},{4,21},{5,20},{6,23},{7,22},{8,25},{9,... | collective-permute-start | bytes 49160 | tf_op jit(solution)/shard_map/ppermute | solution.py:105
  22.7 4.6 %collective-permute-start.2 = (f32[4,512]{1,0:T(4,128)S(1)}, f32[4,512]{1,0:T(4,128)S(1)}, u32[]{:S(2)}, u32[]{:S(2)}) collective-permute-start(f32[4,512]{1,0:T(4,128)S(1)} %slice_select_fusion.3), channel_id=1, source_target_pairs={{0,9},{1,8},{2,11},{3,10},{4,13},{5,12},{6,15},{7,14},{8,1},{9,0},... | collective-permute-start | bytes 24584 | tf_op jit(solution)/shard_map/ppermute | solution.py:105
  24.7 7.2 %collective-permute-start.6 = (f32[64,128]{0,1:T(8,128)S(1)}, f32[64,128]{0,1:T(8,128)S(1)}, u32[]{:S(2)}, u32[]{:S(2)}) collective-permute-start(f32[64,128]{0,1:T(8,128)S(1)} %fusion.13), channel_id=1, source_target_pairs={{0,5},{1,4},{2,7},{3,6},{4,1},{5,0},{6,3},{7,2},{8,13},{9,12},{10,... | collective-permute-start | bytes 98312 | tf_op jit(solution)/shard_map/ppermute | solution.py:105
  27.3 3.1 %collective-permute-start.3 = (f32[4,512]{1,0:T(4,128)S(1)}, f32[4,512]{1,0:T(4,128)S(1)}, u32[]{:S(2)}, u32[]{:S(2)}) collective-permute-start(f32[4,512]{1,0:T(4,128)S(1)} %select_add_fusion.1), channel_id=1, source_target_pairs={{0,3},{1,2},{2,1},{3,0},{4,7},{5,6},{6,5},{7,4},{8,11},{9,10},{10,... | collective-permute-start | bytes 24584 | tf_op jit(solution)/shard_map/ppermute | solution.py:105
  30.5 4.0 %collective-permute-start.4 = (f32[4,512]{1,0:T(4,128)S(1)}, f32[4,512]{1,0:T(4,128)S(1)}, u32[]{:S(2)}, u32[]{:S(2)}) collective-permute-start(f32[4,512]{1,0:T(4,128)S(1)} %add.88), channel_id=1, source_target_pairs={{0,5},{1,4},{2,7},{3,6},{4,1},{5,0},{6,3},{7,2},{8,13},{9,12},{10,... | collective-permute-start | bytes 24584 | tf_op jit(solution)/shard_map/ppermute | solution.py:105
  32.0 3.9 %collective-permute-start.7 = (f32[64,128]{0,1:T(8,128)S(1)}, f32[64,128]{0,1:T(8,128)S(1)}, u32[]{:S(2)}, u32[]{:S(2)}) collective-permute-start(f32[64,128]{0,1:T(8,128)S(1)} %fusion.15), channel_id=1, source_target_pairs={{0,3},{1,2},{2,1},{3,0},{4,7},{5,6},{6,5},{7,4},{8,11},{9,10},{10,... | collective-permute-start | bytes 98312 | tf_op jit(solution)/shard_map/ppermute | solution.py:105

commit v2 on v1

--- a/solution.py
+++ b/solution.py
@@ -2,9 +2,14 @@
 
 import jax
 import jax.numpy as jnp
+import ml_dtypes
 import numpy as np
 from jax import lax
+from jax.experimental import pallas as pl
+from jax.experimental.pallas import tpu as pltpu
 from jax.sharding import PartitionSpec as P
+
+LANES = 128
 
 GLL_NODES = np.array(
     [
@@ -62,37 +67,89 @@
     return cube.reshape(512).astype(np.float32)
 
 
-def vorticity_weighted(velocity, geometry, mass):
+def along_tables(points):
+    table = derivative_matrix()
+    side = table.shape[0]
+    lanes = np.arange(LANES)
+    per_block = LANES // (side * side)
+    r_rows = np.zeros((points // LANES * side, LANES), np.float32)
+    for block in range(points // LANES):
+        for node in range(side):
+            r_rows[block * side + node] = table[block * per_block + lanes // (side * side), node]
+    i, j, k = lanes // (side * side), lanes // side % side, lanes % side
+    along_s = table[j[None, :], j[:, None]] * (i[None, :] == i[:, None]) * (k[None, :] == k[:, None])
+    along_t = table[k[None, :], k[:, None]] * (i[None, :] == i[:, None]) * (j[None, :] == j[:, None])
+    both = np.concatenate([along_s, along_t], axis=1).astype(np.float32)
+    high = both.astype(ml_dtypes.bfloat16)
+    low = (both - high.astype(np.float32)).astype(ml_dtypes.bfloat16)
+    return r_rows, np.concatenate([high, low], axis=0)
+
+
+def vorticity_kernel(map_ref, velocity_ref, geometry_ref, mass_ref, point_ref, r_ref, st_ref, out_ref):
+    components, elements, fields, points = velocity_ref.shape
+    blocks = points // LANES
+    side = r_ref.shape[0] // blocks
+    lane = lax.broadcasted_iota(jnp.int32, (fields, LANES), 1)
+    lower = lane < LANES // 2
+    for elem in range(elements):
+        packed = [
+            [velocity_ref[c, elem, :, b * LANES : (b + 1) * LANES] for b in range(blocks)]
+            for c in range(components)
+        ]
+        stacked = jnp.concatenate([packed[c][b] for c in range(components) for b in range(blocks)], axis=0)
+        along_st = jnp.dot(
+            jnp.concatenate([stacked, stacked], axis=1), st_ref[...], preferred_element_type=jnp.float32
+        )
+        along_r = []
+        for c in range(components):
+            nodes = []
+            for b in range(blocks):
+                own = packed[c][b].astype(jnp.float32)
+                other = pltpu.roll(own, LANES // 2, 1)
+                nodes += [jnp.where(lower, own, other), jnp.where(lower, other, own)]
+            for b in range(blocks):
+                total = r_ref[b * side : b * side + 1, :] * nodes[0]
+                for node in range(1, side):
+                    total += r_ref[b * side + node : b * side + node + 1, :] * nodes[node]
+                along_r.append(total)
+        slot = map_ref[elem]
+        for b in range(blocks):
+            lanes = slice(b * LANES, (b + 1) * LANES)
+            weight = mass_ref[elem : elem + 1, lanes] * point_ref[:, lanes]
+            factors = [weight * geometry_ref[n, elem : elem + 1, lanes] for n in range(9)]
+
+            def gradient(component, coord):
+                row = (component * blocks + b) * fields
+                part = along_st[row : row + fields]
+                return (
+                    factors[coord] * along_r[component * blocks + b]
+                    + factors[3 + coord] * part[:, :LANES]
+                    + factors[6 + coord] * part[:, LANES:]
+                )
+
+            for c in range(components):
+                after, last = (c + 1) % 3, (c + 2) % 3
+                out_ref[c, slot, :, lanes] = (gradient(last, after) - gradient(after, last)).astype(jnp.bfloat16)
+
+
+def stored_vorticity(velocity, geometry, mass, elem_map):
     fields, components, elements, points = velocity.shape
-    highest = lax.Precision.HIGHEST
-    table = jnp.asarray(derivative_matrix())
-    cube = velocity.astype(jnp.float32).reshape(fields, components, elements, 8, 8, 8)
-    along_r = jnp.einsum("ai,scdijk->scdajk", table, cube, precision=highest).reshape(
-        fields, components, elements, points
-    )
-    along_s = jnp.einsum("aj,scdijk->scdiak", table, cube, precision=highest).reshape(
-        fields, components, elements, points
-    )
-    along_t = jnp.einsum("ak,scdijk->scdija", table, cube, precision=highest).reshape(
-        fields, components, elements, points
-    )
-
-    def gradient(component, coord):
-        return (
-            geometry[coord] * along_r[:, component]
-            + geometry[3 + coord] * along_s[:, component]
-            + geometry[6 + coord] * along_t[:, component]
-        )
-
-    vorticity = jnp.stack(
-        [
-            gradient(2, 1) - gradient(1, 2),
-            gradient(0, 2) - gradient(2, 0),
-            gradient(1, 0) - gradient(0, 1),
-        ],
-        axis=1,
-    )
-    return (mass * jnp.asarray(point_weights()) * vorticity).astype(jnp.bfloat16)
+    r_rows, st = along_tables(points)
+    vmem = pl.BlockSpec(memory_space=pltpu.VMEM)
+    return pl.pallas_call(
+        vorticity_kernel,
+        out_shape=jax.ShapeDtypeStruct((components, elements, fields, points), jnp.bfloat16),
+        in_specs=[pl.BlockSpec(memory_space=pltpu.SMEM)] + [vmem] * 6,
+        out_specs=vmem,
+    )(
+        elem_map,
+        velocity.transpose(1, 2, 0, 3),
+        geometry,
+        mass,
+        jnp.asarray(point_weights()).reshape(1, points),
+        jnp.asarray(r_rows),
+        jnp.asarray(st),
+    )
 
 
 def exchange(block, ds, db):
@@ -172,18 +229,14 @@
 
 def shards(velocity, geometry, mass, snapshots, eigvecs, mode_order, elem_map):
     highest = lax.Precision.HIGHEST
-    weighted = vorticity_weighted(velocity, geometry, mass)
-    fields, components, elements, points = weighted.shape
-    slot_index = lax.broadcasted_iota(jnp.int32, (elements, elements), 0)
-    onehot = (slot_index == elem_map[None, :]).astype(jnp.bfloat16)
-    stored = jnp.einsum(
-        "fe,scep->scfp", onehot, weighted, preferred_element_type=jnp.float32
-    ).astype(jnp.bfloat16)
-    stored_flat = stored.reshape(fields, components * elements * points)
-    snap_flat = snapshots.reshape(snapshots.shape[0], components * elements * points)
+    stored = stored_vorticity(velocity, geometry, mass, elem_map)
+    components, elements, fields, points = stored.shape
     factor = 0.25 / math.sqrt(elements * lax.axis_size("sec") * lax.axis_size("blk"))
     contracted = lax.dot_general(
-        stored_flat, snap_flat, (((1,), (1,)), ((), ())), preferred_element_type=jnp.float32
+        stored,
+        snapshots,
+        (((0, 1, 3), (1, 2, 3)), ((), ())),
+        preferred_element_type=jnp.float32,
     )
     columns = own_columns(eigvecs, mode_order)
     sums = reduced_sums(contracted)

time: 37.3 us -> 29.6 us (0.79)
  other arithmetic: 5.43 us -> 1.14 us
  local copies, waits for them, and re-layouts: 8.32 us -> 4.13 us
  matrix products: 6.02 us -> 3.76 us
  Pallas kernels: 0 us -> 2.01 us
  waiting for transfers between devices: 4.81 us -> 6.25 us
    sub x3 -> x0, other arithmetic: 5.06 us -> none  [the longest x1 1.69 us: vorticity_weighted(): gradient(2, 1) - gradient(1, 2)]
    sub x3 -> x0, local copies, waits for them, and re-layouts: 3.67 us -> none  [the longest x1 1.24 us: vorticity_weighted(): gradient(2, 1) - gradient(1, 2)]
    dot_general x5 -> x1, matrix products: 4.89 us -> 1.8 us  [shards(): lax.dot_general(stored, snapshots, (((0, 1, 3), (1, 2, 3)), ((), ())), pr...]
    pallas_call x0 -> x1, Pallas kernels: none -> 2.01 us  [stored_vorticity(): pl.pallas_call(vorticity_kernel, out_shape=jax.ShapeDtypeStruct((componen...]
    ppermute x8, waiting for transfers between devices: 4.81 us -> 6.25 us  [exchange(): return lax.ppermute(block, ('sec', 'blk'), pairs)]
    dot_general x1, matrix products: 0.35 us -> 1.18 us  [own_columns(): lax.dot_general(selector, eigvecs, (((1,), (1,)), ((), ())), precision=la...]
    reshape x1, local copies, waits for them, and re-layouts: 0.08 us -> 0.91 us  [own_columns(): mode_order.reshape(blocks, cols)]
    and x1, other arithmetic: 0.01 us -> 0.81 us  [own_columns(): jnp.take(mode_order.reshape(blocks, cols), block ^ jnp.asarray(relative,...]
  transfers between devices with their start and end apart: 8 -> 8, of which waited for: 4 -> 5; matrix products, arithmetic and copies ran while one was open for 6% -> 15% of each run, Pallas kernels for 0% -> 7%
where the time goes in v2:
time: 29.6 us; the launch traced here: 29.4 us
  starting transfers between devices  12 us (41%)
  waiting for transfers between devices  6.25 us (21%)
  local copies, waits for them, and re-layouts  4.13 us (14%)
  matrix products  3.76 us (13%)
  Pallas kernels  2.01 us (7%)
  other arithmetic  1.14 us (4%)
    ppermute x8, starting transfers between devices, exchange(): return lax.ppermute(block, ('sec', 'blk'), pairs)  12 us
    ppermute x8, waiting for transfers between devices, exchange(): return lax.ppermute(block, ('sec', 'blk'), pairs)  6.25 us
    pallas_call x1, Pallas kernels, stored_vorticity(): pl.pallas_call(vorticity_kernel, out_shape=jax.ShapeDtypeStruct((componen...  2.01 us
    dot_general x1, matrix products, shards(): lax.dot_general(stored, snapshots, (((0, 1, 3), (1, 2, 3)), ((), ())), pr...  1.8 us
    unnamed x5, local copies, waits for them, and re-layouts  1.54 us
    dot_general x1, matrix products, own_columns(): lax.dot_general(selector, eigvecs, (((1,), (1,)), ((), ())), precision=la...  1.18 us
    reshape x1, local copies, waits for them, and re-layouts, own_columns(): mode_order.reshape(blocks, cols)  0.91 us
    and x1, other arithmetic, own_columns(): jnp.take(mode_order.reshape(blocks, cols), block ^ jnp.asarray(relative,...  0.81 us
  transfers between devices with their start and end apart: 8, of which 5 were waited for; matrix products, arithmetic and copies ran while one was open for 15% of the time, Pallas kernels for 7%

profile of v2, /device:TPU:0, one launch (start us, length us, event | category | flops | bytes accessed | tf_op | source)
XLA Modules:
  0.0 29.4 jit_solution(7236500230236808464)
XLA Ops:
  0.0 0.8 %compare_and_fusion = (pred[8]{0:T(512)(128)(4,1)S(1)}, s32[8]{0:T(128)S(1)}) fusion(s32[8]{0:T(128)} %constant.70.clone, s32[]{:T(128)S(6)} %axis_index.26), kind=kLoop, calls=%fused_computation.41 | loop fusion | flops 56 | bytes 76 | tf_op jit(solution)/shard_map/jit(_take)/and | solution.py:193
  0.8 0.9 %reshape.37 = s32[8,32]{1,0:T(8,128)S(1)} reshape(s32[256]{0:T(256)} %param.17) | data formatting | bytes 2048 | tf_op jit(solution)/shard_map/reshape | solution.py:194
  1.7 0.6 %gather_fusion.1 = s32[8,32]{1,0:T(8,128)S(1)} fusion(s32[8,32]{1,0:T(8,128)S(1)} %reshape.37, s32[1024]{0:T(1024)S(1)} %pad_clamp_fusion), kind=kCustom, calls=%fused_computation.1 | custom fusion | bytes 2080 | tf_op jit(solution)/shard_map/jit(_take)/gather | solution.py:193
  2.4 0.1 select_n.79
  2.4 1.2 %fusion.5 = f32[256,64]{0,1:T(8,128)S(1)} fusion(f32[64,256]{1,0:T(8,128)} %param.16, s32[256]{0:T(256)S(1)} %select_n.79), kind=kOutput, calls=%fused_computation.7 | convolution fusion | flops 50397184 | bytes 132096 | tf_op jit(solution)/shard_map/dot_general | solution.py:199
  3.6 0.5 %collective-permute-start.5 = (f32[128,64]{0,1:T(8,128)S(1)}, f32[128,64]{0,1:T(8,128)S(1)}, u32[]{:S(2)}, u32[]{:S(2)}) collective-permute-start(f32[128,64]{0,1:T(8,128)S(1)} %slice.63), channel_id=1, source_target_pairs={{0,1},{1,0},{2,3},{3,2},{4,5},{5,4},{6,7},{7,6},{8,9},{9,8},{10,11... | collective-permute-start | bytes 98312 | tf_op jit(solution)/shard_map/ppermute | solution.py:162
  4.2 1.5 %copy.31 = bf16[16,3,2,512]{3,0,2,1:T(8,128)(2,1)} copy(bf16[16,3,2,512]{3,2,1,0:T(2,128)(2,1)} %param.12) | data formatting | bytes 196608 | tf_op args[0]
  5.7 2.0 %shard_map.118 = bf16[3,2,16,512]{3,2,1,0:T(8,128)(2,1)} custom-call(s32[2]{0:T(128)} %map_ref.1, bf16[3,2,16,512]{3,2,1,0:T(8,128)(2,1)} %bitcast.18, f32[9,2,512]{2,1,0:T(2,128)} %geometry_ref.1, f32[2,512]{1,0:T(2,128)} %mass_ref.1, f32[1,512]{1,0:T(1,128)} %constant.77.point_ref, f32[32,128]{1,0:T(8,128)} %constant.68.clone.r_ref, ...), custom_call_target="tpu_custom_call" | custom-call | tf_op jit(solution)/shard_map/pallas_call | solution.py:139
  7.7 1.8 %fusion.2 = f32[16,512]{1,0:T(8,128)S(1)} fusion(bf16[3,2,16,512]{3,2,1,0:T(8,128)(2,1)} %shard_map.118, bf16[512,3,2,512]{3,2,1,0:T(2,128)(2,1)S(1)} %copy-done), kind=kOutput, calls=%fused_computation.4 | convolution fusion | flops 50331648 | bytes 3276800 | tf_op jit(solution)/shard_map/dot_general | solution.py:235
  9.7 1.1 %collective-permute-done = f32[16,512]{1,0:T(8,128)S(1)} collective-permute-done((f32[16,512]{1,0:T(8,128)S(1)}, f32[16,512]{1,0:T(8,128)S(1)}, u32[]{:S(2)}, u32[]{:S(2)}) %collective-permute-start) | collective-permute-done | bytes 32800 | tf_op jit(solution)/shard_map/ppermute | solution.py:162
  10.8 2.7 %collective-permute-start.1 = (f32[8,512]{1,0:T(8,128)S(1)}, f32[8,512]{1,0:T(8,128)S(1)}, u32[]{:S(2)}, u32[]{:S(2)}) collective-permute-start(f32[8,512]{1,0:T(8,128)S(1)} %slice_select_fusion.2), channel_id=1, source_target_pairs={{0,17},{1,16},{2,19},{3,18},{4,21},{5,20},{6,23},{7,22},{8,25},{9,... | collective-permute-start | bytes 49160 | tf_op jit(solution)/shard_map/ppermute | solution.py:162
  13.5 1.4 %collective-permute-done.1 = f32[8,512]{1,0:T(8,128)S(1)} collective-permute-done((f32[8,512]{1,0:T(8,128)S(1)}, f32[8,512]{1,0:T(8,128)S(1)}, u32[]{:S(2)}, u32[]{:S(2)}) %collective-permute-start.1) | collective-permute-done | bytes 16416 | tf_op jit(solution)/shard_map/ppermute | solution.py:162
  14.9 1.8 %collective-permute-start.2 = (f32[4,512]{1,0:T(4,128)S(1)}, f32[4,512]{1,0:T(4,128)S(1)}, u32[]{:S(2)}, u32[]{:S(2)}) collective-permute-start(f32[4,512]{1,0:T(4,128)S(1)} %slice_select_fusion.3), channel_id=1, source_target_pairs={{0,9},{1,8},{2,11},{3,10},{4,13},{5,12},{6,15},{7,14},{8,1},{9,0},... | collective-permute-start | bytes 24584 | tf_op jit(solution)/shard_map/ppermute | solution.py:162
  16.7 2.4 %collective-permute-start.6 = (f32[64,128]{0,1:T(8,128)S(1)}, f32[64,128]{0,1:T(8,128)S(1)}, u32[]{:S(2)}, u32[]{:S(2)}) collective-permute-start(f32[64,128]{0,1:T(8,128)S(1)} %fusion.7), channel_id=1, source_target_pairs={{0,5},{1,4},{2,7},{3,6},{4,1},{5,0},{6,3},{7,2},{8,13},{9,12},{10,... | collective-permute-start | bytes 98312 | tf_op jit(solution)/shard_map/ppermute | solution.py:162
  19.1 1.6 %collective-permute-start.3 = (f32[4,512]{1,0:T(4,128)S(1)}, f32[4,512]{1,0:T(4,128)S(1)}, u32[]{:S(2)}, u32[]{:S(2)}) collective-permute-start(f32[4,512]{1,0:T(4,128)S(1)} %select_add_fusion.1), channel_id=1, source_target_pairs={{0,3},{1,2},{2,1},{3,0},{4,7},{5,6},{6,5},{7,4},{8,11},{9,10},{10,... | collective-permute-start | bytes 24584 | tf_op jit(solution)/shard_map/ppermute | solution.py:162
  20.8 1.5 %collective-permute-done.3 = f32[4,512]{1,0:T(4,128)S(1)} collective-permute-done((f32[4,512]{1,0:T(4,128)S(1)}, f32[4,512]{1,0:T(4,128)S(1)}, u32[]{:S(2)}, u32[]{:S(2)}) %collective-permute-start.3) | collective-permute-done | bytes 8224 | tf_op jit(solution)/shard_map/ppermute | solution.py:162
  22.3 1.7 %collective-permute-start.4 = (f32[4,512]{1,0:T(4,128)S(1)}, f32[4,512]{1,0:T(4,128)S(1)}, u32[]{:S(2)}, u32[]{:S(2)}) collective-permute-start(f32[4,512]{1,0:T(4,128)S(1)} %add.28), channel_id=1, source_target_pairs={{0,5},{1,4},{2,7},{3,6},{4,1},{5,0},{6,3},{7,2},{8,13},{9,12},{10,... | collective-permute-start | bytes 24584 | tf_op jit(solution)/shard_map/ppermute | solution.py:162
  24.0 0.1 fusion.21
  24.1 0.1 fusion.9
  24.3 1.3 %collective-permute-start.7 = (f32[64,128]{0,1:T(8,128)S(1)}, f32[64,128]{0,1:T(8,128)S(1)}, u32[]{:S(2)}, u32[]{:S(2)}) collective-permute-start(f32[64,128]{0,1:T(8,128)S(1)} %fusion.9), channel_id=1, source_target_pairs={{0,3},{1,2},{2,1},{3,0},{4,7},{5,6},{6,5},{7,4},{8,11},{9,10},{10,... | collective-permute-start | bytes 98312 | tf_op jit(solution)/shard_map/ppermute | solution.py:162
  25.6 0.7 %collective-permute-done.4 = f32[4,512]{1,0:T(4,128)S(1)} collective-permute-done((f32[4,512]{1,0:T(4,128)S(1)}, f32[4,512]{1,0:T(4,128)S(1)}, u32[]{:S(2)}, u32[]{:S(2)}) %collective-permute-start.4) | collective-permute-done | bytes 8224 | tf_op jit(solution)/shard_map/ppermute | solution.py:162
  26.3 0.6 %gather_fusion = f32[4,4,128]{2,1,0:T(4,128)S(1)} fusion(f32[4,4,128]{2,0,1:T(4,128)S(1)} %add_bitcast_fusion, s32[1024]{0:T(1024)S(1)} %pad_clamp_fusion.1), kind=kCustom, calls=%fused_computation | custom fusion | bytes 16400 | tf_op jit(solution)/shard_map/jit(_take)/gather | solution.py:245
  26.8 1.6 %collective-permute-done.7 = f32[64,128]{0,1:T(8,128)S(1)} collective-permute-done((f32[64,128]{0,1:T(8,128)S(1)}, f32[64,128]{0,1:T(8,128)S(1)}, u32[]{:S(2)}, u32[]{:S(2)}) %collective-permute-start.7) | collective-permute-done | bytes 32800 | tf_op jit(solution)/shard_map/ppermute | solution.py:162
  28.6 0.8 %convolution_multiply_fusion = f32[4,32]{1,0:T(4,128)} fusion(f32[32,128]{1,0:T(8,128)S(1)} %copy.24, f32[32,128]{1,0:T(8,128)S(1)} %copy.23, f32[32,128]{1,0:T(8,128)S(1)} %copy.22, f32[32,128]{1,0:T(8,128)S(1)} %copy.21, f32[4,4,128]{2,1,0:T(4,128)S(1)} %gather_fusion, pred[512]{0:T(512)(128)(4,1)S(1)} %broadcast_bitcast_fusion), kind=kOutput, calls=%fused_computation.5 | convolution fusion | flops 837760 | bytes 74752 | tf_op jit(solution)/shard_map/dot_general | solution.py:250
  (29 shorter events, 0.7 us)
Async XLA Ops:
  0.0 7.7 %copy-start = (bf16[512,3,2,512]{3,2,1,0:T(2,128)(2,1)S(1)}, bf16[512,3,2,512]{3,2,1,0:T(2,128)(2,1)}, u32[]{:S(2)}) copy-start(bf16[512,3,2,512]{3,2,1,0:T(2,128)(2,1)} %param.15) | copy-start | bytes 9437188
  0.0 9.6 %copy-start.1 = (s32[4]{0:T(128)S(1)}, s32[4]{0:T(128)}, u32[]{:S(2)}) copy-start(s32[4]{0:T(128)} %constant.71.clone) | copy-start | bytes 52
  3.6 9.8 %collective-permute-start.5 = (f32[128,64]{0,1:T(8,128)S(1)}, f32[128,64]{0,1:T(8,128)S(1)}, u32[]{:S(2)}, u32[]{:S(2)}) collective-permute-start(f32[128,64]{0,1:T(8,128)S(1)} %slice.63), channel_id=1, source_target_pairs={{0,1},{1,0},{2,3},{3,2},{4,5},{5,4},{6,7},{7,6},{8,9},{9,8},{10,11... | collective-permute-start | bytes 98312 | tf_op jit(solution)/shard_map/ppermute | solution.py:162
  9.5 1.2 %collective-permute-start = (f32[16,512]{1,0:T(8,128)S(1)}, f32[16,512]{1,0:T(8,128)S(1)}, u32[]{:S(2)}, u32[]{:S(2)}) collective-permute-start(f32[16,512]{1,0:T(8,128)S(1)} %fusion.2), channel_id=1, source_target_pairs={{0,1},{1,0},{2,3},{3,2},{4,5},{5,4},{6,7},{7,6},{8,9},{9,8},{10,11... | collective-permute-start | bytes 98312 | tf_op jit(solution)/shard_map/ppermute | solution.py:162
  10.8 4.1 %collective-permute-start.1 = (f32[8,512]{1,0:T(8,128)S(1)}, f32[8,512]{1,0:T(8,128)S(1)}, u32[]{:S(2)}, u32[]{:S(2)}) collective-permute-start(f32[8,512]{1,0:T(8,128)S(1)} %slice_select_fusion.2), channel_id=1, source_target_pairs={{0,17},{1,16},{2,19},{3,18},{4,21},{5,20},{6,23},{7,22},{8,25},{9,... | collective-permute-start | bytes 49160 | tf_op jit(solution)/shard_map/ppermute | solution.py:162
  14.9 4.2 %collective-permute-start.2 = (f32[4,512]{1,0:T(4,128)S(1)}, f32[4,512]{1,0:T(4,128)S(1)}, u32[]{:S(2)}, u32[]{:S(2)}) collective-permute-start(f32[4,512]{1,0:T(4,128)S(1)} %slice_select_fusion.3), channel_id=1, source_target_pairs={{0,9},{1,8},{2,11},{3,10},{4,13},{5,12},{6,15},{7,14},{8,1},{9,0},... | collective-permute-start | bytes 24584 | tf_op jit(solution)/shard_map/ppermute | solution.py:162
  16.7 7.3 %collective-permute-start.6 = (f32[64,128]{0,1:T(8,128)S(1)}, f32[64,128]{0,1:T(8,128)S(1)}, u32[]{:S(2)}, u32[]{:S(2)}) collective-permute-start(f32[64,128]{0,1:T(8,128)S(1)} %fusion.7), channel_id=1, source_target_pairs={{0,5},{1,4},{2,7},{3,6},{4,1},{5,0},{6,3},{7,2},{8,13},{9,12},{10,... | collective-permute-start | bytes 98312 | tf_op jit(solution)/shard_map/ppermute | solution.py:162
  19.1 3.1 %collective-permute-start.3 = (f32[4,512]{1,0:T(4,128)S(1)}, f32[4,512]{1,0:T(4,128)S(1)}, u32[]{:S(2)}, u32[]{:S(2)}) collective-permute-start(f32[4,512]{1,0:T(4,128)S(1)} %select_add_fusion.1), channel_id=1, source_target_pairs={{0,3},{1,2},{2,1},{3,0},{4,7},{5,6},{6,5},{7,4},{8,11},{9,10},{10,... | collective-permute-start | bytes 24584 | tf_op jit(solution)/shard_map/ppermute | solution.py:162
  22.3 4.0 %collective-permute-start.4 = (f32[4,512]{1,0:T(4,128)S(1)}, f32[4,512]{1,0:T(4,128)S(1)}, u32[]{:S(2)}, u32[]{:S(2)}) collective-permute-start(f32[4,512]{1,0:T(4,128)S(1)} %add.28), channel_id=1, source_target_pairs={{0,5},{1,4},{2,7},{3,6},{4,1},{5,0},{6,3},{7,2},{8,13},{9,12},{10,... | collective-permute-start | bytes 24584 | tf_op jit(solution)/shard_map/ppermute | solution.py:162
  24.3 4.1 %collective-permute-start.7 = (f32[64,128]{0,1:T(8,128)S(1)}, f32[64,128]{0,1:T(8,128)S(1)}, u32[]{:S(2)}, u32[]{:S(2)}) collective-permute-start(f32[64,128]{0,1:T(8,128)S(1)} %fusion.9), channel_id=1, source_target_pairs={{0,3},{1,2},{2,1},{3,0},{4,7},{5,6},{6,5},{7,4},{8,11},{9,10},{10,... | collective-permute-start | bytes 98312 | tf_op jit(solution)/shard_map/ppermute | solution.py:162

commit v3 on v2

--- a/solution.py
+++ b/solution.py
@@ -85,70 +85,168 @@
     return r_rows, np.concatenate([high, low], axis=0)
 
 
-def vorticity_kernel(map_ref, velocity_ref, geometry_ref, mass_ref, point_ref, r_ref, st_ref, out_ref):
-    components, elements, fields, points = velocity_ref.shape
+def pair_rows(rows, height):
+    elements = rows.shape[0]
+    turn = lax.broadcasted_iota(jnp.int32, (height, LANES), 0) % elements
+    spread = jnp.broadcast_to(rows[0:1], (height, LANES))
+    for elem in range(1, elements):
+        spread = jnp.where(turn == elem, rows[elem : elem + 1], spread)
+    return spread
+
+
+def partial_kernel(
+    map_ref,
+    velocity_hbm,
+    geometry_hbm,
+    mass_hbm,
+    point_hbm,
+    r_hbm,
+    st_hbm,
+    snapshots_hbm,
+    out_ref,
+    velocity_ref,
+    geometry_ref,
+    mass_ref,
+    point_ref,
+    r_ref,
+    st_ref,
+    snapshots_ref,
+    product_ref,
+    turned_ref,
+    semaphores,
+):
+    fields, components, elements, points = velocity_hbm.shape
+    snaps = snapshots_hbm.shape[0]
     blocks = points // LANES
-    side = r_ref.shape[0] // blocks
-    lane = lax.broadcasted_iota(jnp.int32, (fields, LANES), 1)
-    lower = lane < LANES // 2
-    for elem in range(elements):
-        packed = [
-            [velocity_ref[c, elem, :, b * LANES : (b + 1) * LANES] for b in range(blocks)]
-            for c in range(components)
-        ]
-        stacked = jnp.concatenate([packed[c][b] for c in range(components) for b in range(blocks)], axis=0)
-        along_st = jnp.dot(
-            jnp.concatenate([stacked, stacked], axis=1), st_ref[...], preferred_element_type=jnp.float32
+    side = r_hbm.shape[0] // blocks
+    rows = fields * elements
+    chunks = [(c, b) for c in range(components) for b in range(blocks)]
+    small = [
+        (geometry_hbm, geometry_ref),
+        (mass_hbm, mass_ref),
+        (point_hbm, point_ref),
+        (r_hbm, r_ref),
+        (st_hbm, st_ref),
+    ]
+    for n, (c, b) in enumerate(chunks):
+        small.append((velocity_hbm.at[:, c, :, pl.ds(b * LANES, LANES)], velocity_ref.at[n]))
+    large = [
+        (snapshots_hbm.at[:, c, :, pl.ds(b * LANES, LANES)], snapshots_ref.at[n])
+        for n, (c, b) in enumerate(chunks)
+    ]
+    copies = [
+        pltpu.make_async_copy(source, target, semaphores.at[n])
+        for n, (source, target) in enumerate(small + large)
+    ]
+    for copy in copies:
+        copy.start()
+    for copy in copies[: len(small)]:
+        copy.wait()
+
+    packed = [velocity_ref.at[n].reshape(rows, LANES)[...] for n in range(len(chunks))]
+    stacked = jnp.concatenate(packed, axis=0)
+    along_st = jnp.dot(
+        jnp.concatenate([stacked, stacked], axis=1), st_ref[...], preferred_element_type=jnp.float32
+    )
+    lower = lax.broadcasted_iota(jnp.int32, (rows, LANES), 1) < LANES // 2
+    along_r = []
+    for c in range(components):
+        nodes = []
+        for b in range(blocks):
+            own = packed[c * blocks + b].astype(jnp.float32)
+            other = pltpu.roll(own, LANES // 2, 1)
+            nodes += [jnp.where(lower, own, other), jnp.where(lower, other, own)]
+        for b in range(blocks):
+            total = r_ref[b * side : b * side + 1, :] * nodes[0]
+            for node in range(1, side):
+                total += r_ref[b * side + node : b * side + node + 1, :] * nodes[node]
+            along_r.append(total)
+
+    weighted = [None] * len(chunks)
+    for b in range(blocks):
+        lanes = slice(b * LANES, (b + 1) * LANES)
+        weight = mass_ref[:, lanes] * point_ref[:, lanes]
+        factors = [pair_rows(weight * geometry_ref[n, :, lanes], rows) for n in range(9)]
+
+        def gradient(component, coord):
+            row = (component * blocks + b) * rows
+            part = along_st[row : row + rows]
+            return (
+                factors[coord] * along_r[component * blocks + b]
+                + factors[3 + coord] * part[:, :LANES]
+                + factors[6 + coord] * part[:, LANES:]
+            )
+
+        for c in range(components):
+            after, last = (c + 1) % 3, (c + 2) % 3
+            weighted[c * blocks + b] = (gradient(last, after) - gradient(after, last)).astype(jnp.bfloat16)
+    weighted = jnp.concatenate(weighted, axis=1)
+
+    for copy in copies[len(small) :]:
+        copy.wait()
+    height = snaps * elements
+    step = min(height, 256)
+    for start in range(0, height, step):
+        part = jnp.concatenate(
+            [snapshots_ref.at[n].reshape(height, LANES)[start : start + step] for n in range(len(chunks))], axis=1
         )
-        along_r = []
-        for c in range(components):
-            nodes = []
-            for b in range(blocks):
-                own = packed[c][b].astype(jnp.float32)
-                other = pltpu.roll(own, LANES // 2, 1)
-                nodes += [jnp.where(lower, own, other), jnp.where(lower, other, own)]
-            for b in range(blocks):
-                total = r_ref[b * side : b * side + 1, :] * nodes[0]
-                for node in range(1, side):
-                    total += r_ref[b * side + node : b * side + node + 1, :] * nodes[node]
-                along_r.append(total)
-        slot = map_ref[elem]
-        for b in range(blocks):
-            lanes = slice(b * LANES, (b + 1) * LANES)
-            weight = mass_ref[elem : elem + 1, lanes] * point_ref[:, lanes]
-            factors = [weight * geometry_ref[n, elem : elem + 1, lanes] for n in range(9)]
-
-            def gradient(component, coord):
-                row = (component * blocks + b) * fields
-                part = along_st[row : row + fields]
-                return (
-                    factors[coord] * along_r[component * blocks + b]
-                    + factors[3 + coord] * part[:, :LANES]
-                    + factors[6 + coord] * part[:, LANES:]
-                )
-
-            for c in range(components):
-                after, last = (c + 1) % 3, (c + 2) % 3
-                out_ref[c, slot, :, lanes] = (gradient(last, after) - gradient(after, last)).astype(jnp.bfloat16)
-
-
-def stored_vorticity(velocity, geometry, mass, elem_map):
+        product_ref[start : start + step, :rows] = lax.dot_general(
+            part, weighted, (((1,), (1,)), ((), ())), preferred_element_type=jnp.float32
+        )
+    turn = lax.broadcasted_iota(jnp.int32, (snaps, rows), 1) % elements
+    chosen = jnp.zeros((snaps, rows), jnp.float32)
+    for slot in range(elements):
+        here = product_ref[pl.ds(slot, snaps, stride=elements), :][:, :rows]
+        for elem in range(elements):
+            chosen = jnp.where((turn == elem) & (map_ref[elem] == slot), here, chosen)
+    for n in range(snaps // LANES):
+        turned_ref[n * rows : (n + 1) * rows, :] = chosen[n * LANES : (n + 1) * LANES, :].T
+    for n in range(snaps // LANES):
+        total = turned_ref[pl.ds(n * rows, fields, stride=elements), :]
+        for elem in range(1, elements):
+            total += turned_ref[pl.ds(n * rows + elem, fields, stride=elements), :]
+        out_ref[:, n * LANES : (n + 1) * LANES] = total
+
+
+def partial_sums(velocity, geometry, mass, snapshots, elem_map):
     fields, components, elements, points = velocity.shape
+    snaps = snapshots.shape[0]
     r_rows, st = along_tables(points)
-    vmem = pl.BlockSpec(memory_space=pltpu.VMEM)
+    chunks = components * (points // LANES)
+    rows = fields * elements
+    anywhere = pl.BlockSpec(memory_space=pltpu.HBM)
     return pl.pallas_call(
-        vorticity_kernel,
-        out_shape=jax.ShapeDtypeStruct((components, elements, fields, points), jnp.bfloat16),
-        in_specs=[pl.BlockSpec(memory_space=pltpu.SMEM)] + [vmem] * 6,
-        out_specs=vmem,
+        partial_kernel,
+        out_shape=jax.ShapeDtypeStruct((fields, snaps), jnp.float32),
+        in_specs=[pl.BlockSpec(memory_space=pltpu.SMEM)] + [anywhere] * 7,
+        out_specs=pl.BlockSpec(memory_space=pltpu.VMEM),
+        scratch_shapes=[
+            pltpu.VMEM((chunks, fields, elements, LANES), jnp.bfloat16),
+            pltpu.VMEM(geometry.shape, jnp.float32),
+            pltpu.VMEM(mass.shape, jnp.float32),
+            pltpu.VMEM((1, points), jnp.float32),
+            pltpu.VMEM(r_rows.shape, jnp.float32),
+            pltpu.VMEM(st.shape, jnp.bfloat16),
+            pltpu.VMEM((chunks, snaps, elements, LANES), jnp.bfloat16),
+            pltpu.VMEM((snaps * elements, LANES), jnp.float32),
+            pltpu.VMEM((snaps // LANES * rows, LANES), jnp.float32),
+            pltpu.SemaphoreType.DMA((5 + 2 * chunks,)),
+        ],
+        compiler_params=pltpu.CompilerParams(vmem_limit_bytes=40 * 1024 * 1024),
     )(
         elem_map,
-        velocity.transpose(1, 2, 0, 3),
-        geometry,
-        mass,
-        jnp.asarray(point_weights()).reshape(1, points),
-        jnp.asarray(r_rows),
-        jnp.asarray(st),
+        *[
+            pltpu.with_memory_space_constraint(array, pltpu.HBM)
+            for array in (
+                velocity,
+                geometry,
+                mass,
+                jnp.asarray(point_weights()).reshape(1, points),
+                jnp.asarray(r_rows),
+                jnp.asarray(st),
+                snapshots,
+            )
+        ],
     )
 
 
@@ -229,15 +327,9 @@
 
 def shards(velocity, geometry, mass, snapshots, eigvecs, mode_order, elem_map):
     highest = lax.Precision.HIGHEST
-    stored = stored_vorticity(velocity, geometry, mass, elem_map)
-    components, elements, fields, points = stored.shape
+    elements = velocity.shape[2]
     factor = 0.25 / math.sqrt(elements * lax.axis_size("sec") * lax.axis_size("blk"))
-    contracted = lax.dot_general(
-        stored,
-        snapshots,
-        (((0, 1, 3), (1, 2, 3)), ((), ())),
-        preferred_element_type=jnp.float32,
-    )
+    contracted = partial_sums(velocity, geometry, mass, snapshots, elem_map)
     columns = own_columns(eigvecs, mode_order)
     sums = reduced_sums(contracted)
     chips = lax.axis_size("blk") // 2

time: 29.6 us -> 25.7 us (0.87)
  matrix products: 3.76 us -> 1.12 us
  Pallas kernels: 2.01 us -> 4.43 us
  local copies, waits for them, and re-layouts: 4.13 us -> 2.47 us
  waiting for transfers between devices: 6.25 us -> 4.87 us
  other arithmetic: 1.14 us -> 0.34 us
    pallas_call x1, Pallas kernels: 2.01 us -> 4.43 us  [partial_sums(): pl.pallas_call(partial_kernel, out_shape=jax.ShapeDtypeStruct((fields, sn...]
    dot_general x1 -> x0, matrix products: 1.8 us -> none  [shards(): lax.dot_general(stored, snapshots, (((0, 1, 3), (1, 2, 3)), ((), ())), pr...]
    ppermute x8, waiting for transfers between devices: 6.25 us -> 4.87 us  [exchange(): return lax.ppermute(block, ('sec', 'blk'), pairs)]
    dot_general x1, matrix products: 1.18 us -> 0.35 us  [own_columns(): lax.dot_general(selector, eigvecs, (((1,), (1,)), ((), ())), precision=la...]
    unnamed x5 -> x10, local copies, waits for them, and re-layouts: 1.54 us -> 0.71 us
    reshape x1, local copies, waits for them, and re-layouts: 0.91 us -> 0.08 us  [own_columns(): mode_order.reshape(blocks, cols)]
    and x1, other arithmetic: 0.81 us -> 0.01 us  [own_columns(): jnp.take(mode_order.reshape(blocks, cols), block ^ jnp.asarray(relative,...]
  transfers between devices with their start and end apart: 8 -> 8, of which waited for: 5 -> 4; matrix products, arithmetic and copies ran while one was open for 15% -> 9% of each run, Pallas kernels for 7% -> 0%
where the time goes in v3:
time: 25.7 us; the launch traced here: 25.5 us
  starting transfers between devices  12.1 us (47%)
  waiting for transfers between devices  4.87 us (19%)
  Pallas kernels  4.43 us (17%)
  local copies, waits for them, and re-layouts  2.47 us (10%)
  matrix products  1.12 us (4%)
  other arithmetic  0.34 us (1%)
    ppermute x8, starting transfers between devices, exchange(): return lax.ppermute(block, ('sec', 'blk'), pairs)  12.1 us
    ppermute x8, waiting for transfers between devices, exchange(): return lax.ppermute(block, ('sec', 'blk'), pairs)  4.87 us
    pallas_call x1, Pallas kernels, partial_sums(): pl.pallas_call(partial_kernel, out_shape=jax.ShapeDtypeStruct((fields, sn...  4.43 us
    dot_general x1, matrix products, shards(): lax.dot_general(parts, jnp.concatenate(columns, axis=1), (((1,), (1,)), (...  0.78 us
    unnamed x10, local copies, waits for them, and re-layouts  0.71 us
    gather x1, local copies, waits for them, and re-layouts, shards(): jnp.take(sums.reshape(sums.shape[0], chips, sums.shape[1] // chips), chip...  0.57 us
    gather x1, local copies, waits for them, and re-layouts, own_columns(): jnp.take(mode_order.reshape(blocks, cols), block ^ jnp.asarray(relative,...  0.56 us
  transfers between devices with their start and end apart: 8, of which 4 were waited for; matrix products, arithmetic and copies ran while one was open for 9% of the time, Pallas kernels for 0%

profile of v3, /device:TPU:0, one launch (start us, length us, event | category | flops | bytes accessed | tf_op | source)
XLA Modules:
  0.0 25.5 jit_solution(1962859852865887889)
XLA Ops:
  0.0 0.7 %copy-done.1 = s32[2]{0:T(128)S(1)} copy-done((s32[2]{0:T(128)S(1)}, s32[2]{0:T(128)}, u32[]{:S(2)}) %copy-start.1) | copy-done | bytes 32
  0.7 4.4 %shard_map.118 = f32[16,512]{1,0:T(8,128)S(1)} custom-call(s32[2]{0:T(128)S(1)} %copy-done.1, bf16[16,3,2,512]{3,2,1,0:T(2,128)(2,1)} %velocity_hbm.1, f32[9,2,512]{2,1,0:T(2,128)} %geometry_hbm.1, f32[2,512]{1,0:T(2,128)} %mass_hbm.1, f32[1,512]{1,0:T(1,128)} %constant.77.point_hbm, f32[32,128]{1,0:T(8,128)} %constant.68.clone.r_hbm, ...), custom_call_target="tpu_custom_call" | custom-call | tf_op jit(solution)/shard_map/pallas_call | solution.py:218
  5.1 0.5 %collective-permute-start = (f32[16,512]{1,0:T(8,128)S(1)}, f32[16,512]{1,0:T(8,128)S(1)}, u32[]{:S(2)}, u32[]{:S(2)}) collective-permute-start(f32[16,512]{1,0:T(8,128)S(1)} %shard_map.118), channel_id=1, source_target_pairs={{0,1},{1,0},{2,3},{3,2},{4,5},{5,4},{6,7},{7,6},{8,9},{9,8},{10,11... | collective-permute-start | bytes 98312 | tf_op jit(solution)/shard_map/ppermute | solution.py:260
  5.7 0.1 reshape.37
  5.8 0.6 %gather_fusion.1 = s32[8,32]{1,0:T(8,128)S(1)} fusion(s32[8,32]{1,0:T(8,128)S(1)} %reshape.37, s32[1024]{0:T(1024)S(1)} %pad_clamp_fusion), kind=kCustom, calls=%fused_computation.1 | custom fusion | bytes 2080 | tf_op jit(solution)/shard_map/jit(_take)/gather | solution.py:291
  6.4 0.1 select_n.79
  6.5 0.3 %fusion = f32[256,64]{0,1:T(8,128)S(1)} fusion(f32[64,256]{1,0:T(8,128)S(1)} %copy-done, s32[256]{0:T(256)S(1)} %select_n.79), kind=kOutput, calls=%fused_computation.4 | convolution fusion | flops 50397184 | bytes 132096 | tf_op jit(solution)/shard_map/dot_general | solution.py:297
  6.9 0.1 collective-permute-start.5
  7.1 2.7 %collective-permute-start.1 = (f32[8,512]{1,0:T(8,128)S(1)}, f32[8,512]{1,0:T(8,128)S(1)}, u32[]{:S(2)}, u32[]{:S(2)}) collective-permute-start(f32[8,512]{1,0:T(8,128)S(1)} %slice_select_fusion.2), channel_id=1, source_target_pairs={{0,17},{1,16},{2,19},{3,18},{4,21},{5,20},{6,23},{7,22},{8,25},{9,... | collective-permute-start | bytes 49160 | tf_op jit(solution)/shard_map/ppermute | solution.py:260
  9.8 1.4 %collective-permute-done.1 = f32[8,512]{1,0:T(8,128)S(1)} collective-permute-done((f32[8,512]{1,0:T(8,128)S(1)}, f32[8,512]{1,0:T(8,128)S(1)}, u32[]{:S(2)}, u32[]{:S(2)}) %collective-permute-start.1) | collective-permute-done | bytes 16416 | tf_op jit(solution)/shard_map/ppermute | solution.py:260
  11.2 1.8 %collective-permute-start.2 = (f32[4,512]{1,0:T(4,128)S(1)}, f32[4,512]{1,0:T(4,128)S(1)}, u32[]{:S(2)}, u32[]{:S(2)}) collective-permute-start(f32[4,512]{1,0:T(4,128)S(1)} %slice_select_fusion.3), channel_id=1, source_target_pairs={{0,9},{1,8},{2,11},{3,10},{4,13},{5,12},{6,15},{7,14},{8,1},{9,0},... | collective-permute-start | bytes 24584 | tf_op jit(solution)/shard_map/ppermute | solution.py:260
  13.1 0.1 fusion.2
  13.2 2.7 %collective-permute-start.6 = (f32[64,128]{0,1:T(8,128)S(1)}, f32[64,128]{0,1:T(8,128)S(1)}, u32[]{:S(2)}, u32[]{:S(2)}) collective-permute-start(f32[64,128]{0,1:T(8,128)S(1)} %fusion.2), channel_id=1, source_target_pairs={{0,5},{1,4},{2,7},{3,6},{4,1},{5,0},{6,3},{7,2},{8,13},{9,12},{10,... | collective-permute-start | bytes 98312 | tf_op jit(solution)/shard_map/ppermute | solution.py:260
  15.8 1.3 %collective-permute-start.3 = (f32[4,512]{1,0:T(4,128)S(1)}, f32[4,512]{1,0:T(4,128)S(1)}, u32[]{:S(2)}, u32[]{:S(2)}) collective-permute-start(f32[4,512]{1,0:T(4,128)S(1)} %select_add_fusion.1), channel_id=1, source_target_pairs={{0,3},{1,2},{2,1},{3,0},{4,7},{5,6},{6,5},{7,4},{8,11},{9,10},{10,... | collective-permute-start | bytes 24584 | tf_op jit(solution)/shard_map/ppermute | solution.py:260
  17.2 1.8 %collective-permute-done.3 = f32[4,512]{1,0:T(4,128)S(1)} collective-permute-done((f32[4,512]{1,0:T(4,128)S(1)}, f32[4,512]{1,0:T(4,128)S(1)}, u32[]{:S(2)}, u32[]{:S(2)}) %collective-permute-start.3) | collective-permute-done | bytes 8224 | tf_op jit(solution)/shard_map/ppermute | solution.py:260
  19.0 1.4 %collective-permute-start.4 = (f32[4,512]{1,0:T(4,128)S(1)}, f32[4,512]{1,0:T(4,128)S(1)}, u32[]{:S(2)}, u32[]{:S(2)}) collective-permute-start(f32[4,512]{1,0:T(4,128)S(1)} %add.28), channel_id=1, source_target_pairs={{0,5},{1,4},{2,7},{3,6},{4,1},{5,0},{6,3},{7,2},{8,13},{9,12},{10,... | collective-permute-start | bytes 24584 | tf_op jit(solution)/shard_map/ppermute | solution.py:260
  20.3 0.1 fusion.16
  20.4 0.1 fusion.4
  20.6 1.6 %collective-permute-start.7 = (f32[64,128]{0,1:T(8,128)S(1)}, f32[64,128]{0,1:T(8,128)S(1)}, u32[]{:S(2)}, u32[]{:S(2)}) collective-permute-start(f32[64,128]{0,1:T(8,128)S(1)} %fusion.4), channel_id=1, source_target_pairs={{0,3},{1,2},{2,1},{3,0},{4,7},{5,6},{6,5},{7,4},{8,11},{9,10},{10,... | collective-permute-start | bytes 98312 | tf_op jit(solution)/shard_map/ppermute | solution.py:260
  22.2 0.7 %collective-permute-done.4 = f32[4,512]{1,0:T(4,128)S(1)} collective-permute-done((f32[4,512]{1,0:T(4,128)S(1)}, f32[4,512]{1,0:T(4,128)S(1)}, u32[]{:S(2)}, u32[]{:S(2)}) %collective-permute-start.4) | collective-permute-done | bytes 8224 | tf_op jit(solution)/shard_map/ppermute | solution.py:260
  23.0 0.6 %gather_fusion = f32[4,4,128]{2,1,0:T(4,128)S(1)} fusion(f32[4,4,128]{2,0,1:T(4,128)S(1)} %add_bitcast_fusion, s32[1024]{0:T(1024)S(1)} %pad_clamp_fusion.1), kind=kCustom, calls=%fused_computation | custom fusion | bytes 16400 | tf_op jit(solution)/shard_map/jit(_take)/gather | solution.py:337
  23.5 0.9 %collective-permute-done.7 = f32[64,128]{0,1:T(8,128)S(1)} collective-permute-done((f32[64,128]{0,1:T(8,128)S(1)}, f32[64,128]{0,1:T(8,128)S(1)}, u32[]{:S(2)}, u32[]{:S(2)}) %collective-permute-start.7) | collective-permute-done | bytes 32800 | tf_op jit(solution)/shard_map/ppermute | solution.py:260
  24.5 0.1 fusion.17
  24.7 0.8 %convolution_multiply_fusion = f32[4,32]{1,0:T(4,128)} fusion(f32[32,128]{1,0:T(8,128)S(1)} %copy.18, f32[32,128]{1,0:T(8,128)S(1)} %copy.17, f32[32,128]{1,0:T(8,128)S(1)} %copy.16, f32[32,128]{1,0:T(8,128)S(1)} %copy.15, f32[4,4,128]{2,1,0:T(4,128)S(1)} %gather_fusion, pred[512]{0:T(512)(128)(4,1)S(1)} %broadcast_bitcast_fusion), kind=kOutput, calls=%fused_computation.2 | convolution fusion | flops 837760 | bytes 74752 | tf_op jit(solution)/shard_map/dot_general | solution.py:342
  (33 shorter events, 0.5 us)
Async XLA Ops:
  0.0 6.5 %copy-start = (f32[64,256]{1,0:T(8,128)S(1)}, f32[64,256]{1,0:T(8,128)}, u32[]{:S(2)}) copy-start(f32[64,256]{1,0:T(8,128)} %param.16) | copy-start | bytes 196612
  0.0 5.7 %copy-start.4 = (s32[8]{0:T(128)S(1)}, s32[8]{0:T(128)}, u32[]{:S(2)}) copy-start(s32[8]{0:T(128)} %constant.70.clone) | copy-start | bytes 100
  0.0 7.0 %copy-start.3 = (s32[4]{0:T(128)S(1)}, s32[4]{0:T(128)}, u32[]{:S(2)}) copy-start(s32[4]{0:T(128)} %constant.71.clone) | copy-start | bytes 52
  0.0 0.7 %copy-start.1 = (s32[2]{0:T(128)S(1)}, s32[2]{0:T(128)}, u32[]{:S(2)}) copy-start(s32[2]{0:T(128)} %map_ref.1) | copy-start | bytes 28
  0.7 5.0 %copy-start.2 = (s32[256]{0:T(256)S(1)}, s32[256]{0:T(256)}, u32[]{:S(2)}) copy-start(s32[256]{0:T(256)} %param.17) | copy-start | bytes 3076
  5.1 1.9 %collective-permute-start = (f32[16,512]{1,0:T(8,128)S(1)}, f32[16,512]{1,0:T(8,128)S(1)}, u32[]{:S(2)}, u32[]{:S(2)}) collective-permute-start(f32[16,512]{1,0:T(8,128)S(1)} %shard_map.118), channel_id=1, source_target_pairs={{0,1},{1,0},{2,3},{3,2},{4,5},{5,4},{6,7},{7,6},{8,9},{9,8},{10,11... | collective-permute-start | bytes 98312 | tf_op jit(solution)/shard_map/ppermute | solution.py:260
  6.9 2.9 %collective-permute-start.5 = (f32[128,64]{0,1:T(8,128)S(1)}, f32[128,64]{0,1:T(8,128)S(1)}, u32[]{:S(2)}, u32[]{:S(2)}) collective-permute-start(f32[128,64]{0,1:T(8,128)S(1)} %slice.63), channel_id=1, source_target_pairs={{0,1},{1,0},{2,3},{3,2},{4,5},{5,4},{6,7},{7,6},{8,9},{9,8},{10,11... | collective-permute-start | bytes 98312 | tf_op jit(solution)/shard_map/ppermute | solution.py:260
  7.1 4.1 %collective-permute-start.1 = (f32[8,512]{1,0:T(8,128)S(1)}, f32[8,512]{1,0:T(8,128)S(1)}, u32[]{:S(2)}, u32[]{:S(2)}) collective-permute-start(f32[8,512]{1,0:T(8,128)S(1)} %slice_select_fusion.2), channel_id=1, source_target_pairs={{0,17},{1,16},{2,19},{3,18},{4,21},{5,20},{6,23},{7,22},{8,25},{9,... | collective-permute-start | bytes 49160 | tf_op jit(solution)/shard_map/ppermute | solution.py:260
  11.2 4.6 %collective-permute-start.2 = (f32[4,512]{1,0:T(4,128)S(1)}, f32[4,512]{1,0:T(4,128)S(1)}, u32[]{:S(2)}, u32[]{:S(2)}) collective-permute-start(f32[4,512]{1,0:T(4,128)S(1)} %slice_select_fusion.3), channel_id=1, source_target_pairs={{0,9},{1,8},{2,11},{3,10},{4,13},{5,12},{6,15},{7,14},{8,1},{9,0},... | collective-permute-start | bytes 24584 | tf_op jit(solution)/shard_map/ppermute | solution.py:260
  13.2 7.2 %collective-permute-start.6 = (f32[64,128]{0,1:T(8,128)S(1)}, f32[64,128]{0,1:T(8,128)S(1)}, u32[]{:S(2)}, u32[]{:S(2)}) collective-permute-start(f32[64,128]{0,1:T(8,128)S(1)} %fusion.2), channel_id=1, source_target_pairs={{0,5},{1,4},{2,7},{3,6},{4,1},{5,0},{6,3},{7,2},{8,13},{9,12},{10,... | collective-permute-start | bytes 98312 | tf_op jit(solution)/shard_map/ppermute | solution.py:260
  15.8 3.1 %collective-permute-start.3 = (f32[4,512]{1,0:T(4,128)S(1)}, f32[4,512]{1,0:T(4,128)S(1)}, u32[]{:S(2)}, u32[]{:S(2)}) collective-permute-start(f32[4,512]{1,0:T(4,128)S(1)} %select_add_fusion.1), channel_id=1, source_target_pairs={{0,3},{1,2},{2,1},{3,0},{4,7},{5,6},{6,5},{7,4},{8,11},{9,10},{10,... | collective-permute-start | bytes 24584 | tf_op jit(solution)/shard_map/ppermute | solution.py:260
  19.0 4.0 %collective-permute-start.4 = (f32[4,512]{1,0:T(4,128)S(1)}, f32[4,512]{1,0:T(4,128)S(1)}, u32[]{:S(2)}, u32[]{:S(2)}) collective-permute-start(f32[4,512]{1,0:T(4,128)S(1)} %add.28), channel_id=1, source_target_pairs={{0,5},{1,4},{2,7},{3,6},{4,1},{5,0},{6,3},{7,2},{8,13},{9,12},{10,... | collective-permute-start | bytes 24584 | tf_op jit(solution)/shard_map/ppermute | solution.py:260
  20.6 3.9 %collective-permute-start.7 = (f32[64,128]{0,1:T(8,128)S(1)}, f32[64,128]{0,1:T(8,128)S(1)}, u32[]{:S(2)}, u32[]{:S(2)}) collective-permute-start(f32[64,128]{0,1:T(8,128)S(1)} %fusion.4), channel_id=1, source_target_pairs={{0,3},{1,2},{2,1},{3,0},{4,7},{5,6},{6,5},{7,4},{8,11},{9,10},{10,... | collective-permute-start | bytes 98312 | tf_op jit(solution)/shard_map/ppermute | solution.py:260

commit v4 on v3

v4 whole, which is shorter than its diff:
```python
import functools
import math

import jax
import jax.numpy as jnp
import ml_dtypes
import numpy as np
from jax import lax
from jax.experimental import pallas as pl
from jax.experimental.pallas import tpu as pltpu
from jax.sharding import PartitionSpec as P

LANES = 128

GLL_NODES = np.array(
    [
        -1.0,
        -0.8717401485096066,
        -0.5917001814331423,
        -0.2092992179024789,
        0.2092992179024789,
        0.5917001814331423,
        0.8717401485096066,
        1.0,
    ]
)
GLL_WEIGHTS = np.array(
    [
        1.0 / 28.0,
        0.2107042271435061,
        0.3411226924835044,
        0.4124587946587038,
        0.4124587946587038,
        0.3411226924835044,
        0.2107042271435061,
        1.0 / 28.0,
    ]
)


def legendre_seven(nodes):
    before = nodes * 0.0 + 1.0
    current = nodes * 1.0
    for order in range(1, 7):
        following = ((2.0 * order + 1.0) * nodes * current - order * before) / (order + 1.0)
        before = current
        current = following
    return current


def derivative_matrix():
    degree = 7
    values = legendre_seven(GLL_NODES)
    result = np.zeros((8, 8))
    for row_idx in range(8):
        for col_idx in range(8):
            if row_idx != col_idx:
                result[row_idx, col_idx] = values[row_idx] / (
                    values[col_idx] * (GLL_NODES[row_idx] - GLL_NODES[col_idx])
                )
    result[0, 0] = -degree * (degree + 1) / 4.0
    result[7, 7] = degree * (degree + 1) / 4.0
    return result.astype(np.float32)


def point_weights():
    cube = GLL_WEIGHTS[:, None, None] * GLL_WEIGHTS[None, :, None] * GLL_WEIGHTS[None, None, :]
    return cube.reshape(512).astype(np.float32)


def along_tables(points):
    table = derivative_matrix()
    side = table.shape[0]
    lanes = np.arange(LANES)
    per_block = LANES // (side * side)
    r_rows = np.zeros((points // LANES * side, LANES), np.float32)
    for block in range(points // LANES):
        for node in range(side):
            r_rows[block * side + node] = table[block * per_block + lanes // (side * side), node]
    i, j, k = lanes // (side * side), lanes // side % side, lanes % side
    along_s = table[j[None, :], j[:, None]] * (i[None, :] == i[:, None]) * (k[None, :] == k[:, None])
    along_t = table[k[None, :], k[:, None]] * (i[None, :] == i[:, None]) * (j[None, :] == j[:, None])
    both = np.concatenate([along_s, along_t], axis=1).astype(np.float32)
    high = both.astype(ml_dtypes.bfloat16)
    low = (both - high.astype(np.float32)).astype(ml_dtypes.bfloat16)
    return r_rows, np.concatenate([high, low], axis=0)


def pair_rows(rows, height):
    elements = rows.shape[0]
    turn = lax.broadcasted_iota(jnp.int32, (height, LANES), 0) % elements
    spread = jnp.broadcast_to(rows[0:1], (height, LANES))
    for elem in range(1, elements):
        spread = jnp.where(turn == elem, rows[elem : elem + 1], spread)
    return spread


def parity(chip):
    return bin(chip).count("1") & 1


def odd_block(block, blocks):
    odd, rest = block & 1, blocks // 2
    while rest > 1:
        block = block >> 1
        odd = odd ^ (block & 1)
        rest //= 2
    return odd


def partial_kernel(
    blocks,
    map_hbm,
    order_hbm,
    velocity_hbm,
    geometry_hbm,
    mass_hbm,
    point_hbm,
    r_hbm,
    st_hbm,
    eigvecs_hbm,
    snapshots_hbm,
    out_ref,
    keep_ref,
    map_ref,
    order_ref,
    velocity_ref,
    geometry_ref,
    mass_ref,
    point_ref,
    r_ref,
    st_ref,
    eigvecs_ref,
    snapshots_ref,
    product_ref,
    turned_ref,
    columns_ref,
    semaphores,
):
    fields, components, elements, points = velocity_hbm.shape
    snaps = snapshots_hbm.shape[0]
    own, mode_count = eigvecs_hbm.shape
    parts = points // LANES
    side = r_hbm.shape[0] // parts
    rows = fields * elements
    chunks = [(c, p) for c in range(components) for p in range(parts)]
    small = [
        (velocity_hbm.at[:, c, :, pl.ds(p * LANES, LANES)], velocity_ref.at[n])
        for n, (c, p) in enumerate(chunks)
    ]
    small += [
        (st_hbm, st_ref),
        (r_hbm, r_ref),
        (geometry_hbm, geometry_ref),
        (mass_hbm, mass_ref),
        (point_hbm, point_ref),
    ]
    large = [
        (map_hbm, map_ref),
        (order_hbm, order_ref),
        (eigvecs_hbm, eigvecs_ref),
    ]
    large += [
        (snapshots_hbm.at[:, c, :, pl.ds(p * LANES, LANES)], snapshots_ref.at[n])
        for n, (c, p) in enumerate(chunks)
    ]
    copies = [
        pltpu.make_async_copy(source, target, semaphores.at[n])
        for n, (source, target) in enumerate(small + large)
    ]
    for copy in copies:
        copy.start()
    for copy in copies[: len(small)]:
        copy.wait()

    packed = [velocity_ref.at[n].reshape(rows, LANES)[...] for n in range(len(chunks))]
    stacked = jnp.concatenate(packed, axis=0)
    along_st = jnp.dot(
        jnp.concatenate([stacked, stacked], axis=1), st_ref[...], preferred_element_type=jnp.float32
    )
    lower = lax.broadcasted_iota(jnp.int32, (rows, LANES), 1) < LANES // 2
    along_r = []
    for c in range(components):
        nodes = []
        for p in range(parts):
            here = packed[c * parts + p].astype(jnp.float32)
            other = pltpu.roll(here, LANES // 2, 1)
            nodes += [jnp.where(lower, here, other), jnp.where(lower, other, here)]
        for p in range(parts):
            total = r_ref[p * side : p * side + 1, :] * nodes[0]
            for node in range(1, side):
                total += r_ref[p * side + node : p * side + node + 1, :] * nodes[node]
            along_r.append(total)

    weighted = [None] * len(chunks)
    for p in range(parts):
        lanes = slice(p * LANES, (p + 1) * LANES)
        weight = mass_ref[:, lanes] * point_ref[:, lanes]
        factors = [pair_rows(weight * geometry_ref[n, :, lanes], rows) for n in range(9)]

        def gradient(component, coord):
            row = (component * parts + p) * rows
            part = along_st[row : row + rows]
            return (
                factors[coord] * along_r[component * parts + p]
                + factors[3 + coord] * part[:, :LANES]
                + factors[6 + coord] * part[:, LANES:]
            )

        for c in range(components):
            after, last = (c + 1) % 3, (c + 2) % 3
            weighted[c * parts + p] = (gradient(last, after) - gradient(after, last)).astype(jnp.bfloat16)
    weighted = jnp.concatenate(weighted, axis=1)

    for copy in copies[len(small) : len(small) + 3]:
        copy.wait()
    selector = (
        lax.broadcasted_iota(jnp.int32, (mode_count, mode_count), 0) == order_ref[...]
    ).astype(jnp.bfloat16)
    rest = eigvecs_ref[...]
    ordered = jnp.zeros(rest.shape, jnp.float32)
    for _ in range(3):
        piece = rest.astype(jnp.bfloat16)
        ordered += jnp.dot(piece, selector, preferred_element_type=jnp.float32)
        rest = rest - piece.astype(jnp.float32)
    columns_ref[...] = ordered.T
    cols, chips = mode_count // blocks, blocks // 2
    odd = odd_block(lax.axis_index("blk"), blocks)
    half = mode_count // 4
    first = fields * chips
    for chip in range(chips):
        even = parity(chip)
        keep = columns_ref[pl.ds((2 * chip + (even ^ odd)) * cols, cols), :]
        send = columns_ref[pl.ds((2 * chip + (even ^ 1 ^ odd)) * cols, cols), :]
        keep_ref[chip * cols : (chip + 1) * cols, :] = keep
        row, lane = chip * cols % half, chip * cols // half * own
        out_ref[first + row : first + row + cols, lane : lane + own] = send

    for copy in copies[len(small) + 3 :]:
        copy.wait()
    height = snaps * elements
    step = min(height, 256)
    for start in range(0, height, step):
        part = jnp.concatenate(
            [snapshots_ref.at[n].reshape(height, LANES)[start : start + step] for n in range(len(chunks))], axis=1
        )
        product_ref[start : start + step, :rows] = lax.dot_general(
            part, weighted, (((1,), (1,)), ((), ())), preferred_element_type=jnp.float32
        )
    turn = lax.broadcasted_iota(jnp.int32, (snaps, rows), 1) % elements
    chosen = jnp.zeros((snaps, rows), jnp.float32)
    for slot in range(elements):
        here = product_ref[pl.ds(slot, snaps, stride=elements), :][:, :rows]
        for elem in range(elements):
            chosen = jnp.where((turn == elem) & (map_ref[elem] == slot), here, chosen)
    for n in range(snaps // LANES):
        turned_ref[n * rows : (n + 1) * rows, :] = chosen[n * LANES : (n + 1) * LANES, :].T
    pair = 2 * own
    for n in range(snaps // LANES):
        total = turned_ref[pl.ds(n * rows, fields, stride=elements), :]
        for elem in range(1, elements):
            total += turned_ref[pl.ds(n * rows + elem, fields, stride=elements), :]
        for chip in range(n * LANES // pair, (n + 1) * LANES // pair):
            lane = chip * pair - n * LANES
            out_ref[pl.ds(chip, fields, stride=chips), :] = total[:, lane : lane + pair]


def partial_sums(velocity, geometry, mass, snapshots, eigvecs, mode_order, elem_map):
    fields, components, elements, points = velocity.shape
    snaps = snapshots.shape[0]
    own, mode_count = eigvecs.shape
    blocks = snaps // own
    r_rows, st = along_tables(points)
    chunks = components * (points // LANES)
    rows = fields * elements
    vmem = pl.BlockSpec(memory_space=pltpu.VMEM)
    return pl.pallas_call(
        functools.partial(partial_kernel, blocks),
        out_shape=(
            jax.ShapeDtypeStruct((fields * blocks // 2 + mode_count // 4, 2 * own), jnp.float32),
            jax.ShapeDtypeStruct((mode_count // 2, own), jnp.float32),
        ),
        in_specs=[pl.BlockSpec(memory_space=pltpu.HBM)] * 10,
        out_specs=(vmem, vmem),
        scratch_shapes=[
            pltpu.SMEM(elem_map.shape, jnp.int32),
            pltpu.VMEM((1, mode_count), jnp.int32),
            pltpu.VMEM((chunks, fields, elements, LANES), jnp.bfloat16),
            pltpu.VMEM(geometry.shape, jnp.float32),
            pltpu.VMEM(mass.shape, jnp.float32),
            pltpu.VMEM((1, points), jnp.float32),
            pltpu.VMEM(r_rows.shape, jnp.float32),
            pltpu.VMEM(st.shape, jnp.bfloat16),
            pltpu.VMEM(eigvecs.shape, jnp.float32),
            pltpu.VMEM((chunks, snaps, elements, LANES), jnp.bfloat16),
            pltpu.VMEM((snaps * elements, LANES), jnp.float32),
            pltpu.VMEM((snaps // LANES * rows, LANES), jnp.float32),
            pltpu.VMEM((mode_count, own), jnp.float32),
            pltpu.SemaphoreType.DMA((8 + 2 * chunks,)),
        ],
        compiler_params=pltpu.CompilerParams(vmem_limit_bytes=40 * 1024 * 1024),
    )(
        *[
            pltpu.with_memory_space_constraint(array, pltpu.HBM)
            for array in (
                elem_map,
                mode_order.reshape(1, mode_count),
                velocity,
                geometry,
                mass,
                jnp.asarray(point_weights()).reshape(1, points),
                jnp.asarray(r_rows),
                jnp.asarray(st),
                eigvecs,
                snapshots,
            )
        ]
    )


def exchange(block, ds, db):
    sections, blocks = lax.axis_size("sec"), lax.axis_size("blk")
    pairs = [
        (s * blocks + b, (s ^ ds) * blocks + (b ^ db))
        for s in range(sections)
        for b in range(blocks)
    ]
    return lax.ppermute(block, ("sec", "blk"), pairs)


def share_kernel(factor, chips, sums_ref, got_ref, held_ref, out_ref, total_ref):
    count = sums_ref.shape[0]
    fields, cols = out_ref.shape
    total_ref[...] = sums_ref[...] + got_ref[:count, :]
    chip = lax.axis_index("blk") // 2
    left = jnp.concatenate(
        [total_ref[pl.ds(chip ^ n, fields, stride=chips), :] for n in range(chips)], axis=1
    )
    right = [ref[start + n * cols : start + (n + 1) * cols, :] for ref, start in ((held_ref, 0), (got_ref, count)) for n in range(chips // 2)]
    out_ref[...] = factor * lax.dot_general(
        left,
        jnp.concatenate(right, axis=1),
        (((1,), (1,)), ((), ())),
        precision=lax.Precision.HIGHEST,
        preferred_element_type=jnp.float32,
    )


def shards(velocity, geometry, mass, snapshots, eigvecs, mode_order, elem_map):
    sections, blocks = lax.axis_size("sec"), lax.axis_size("blk")
    section, block = lax.axis_index("sec"), lax.axis_index("blk")
    fields, _, elements, _ = velocity.shape
    own, mode_count = eigvecs.shape
    chips, cols, pair = blocks // 2, mode_count // blocks, 2 * own
    factor = 0.25 / math.sqrt(elements * sections * blocks)

    packet, keep = partial_sums(velocity, geometry, mass, snapshots, eigvecs, mode_order, elem_map)
    got = exchange(packet, 0, 1)
    count = fields * chips
    sums = packet[:count] + got[:count]
    arrived = jnp.concatenate([got[count:, :own], got[count:, own:]], axis=0)
    second = (block & 1) != 0
    held = jnp.concatenate(
        [jnp.where(second, arrived, keep), jnp.where(second, keep, arrived)], axis=1
    ).reshape(chips, 1, cols, pair)

    step = sections // 2
    while step:
        count //= 2
        upper = (section & step) != 0
        low, high = sums[:count], sums[count:]
        sums = jnp.where(upper, high, low) + exchange(jnp.where(upper, low, high), step, 1)
        step //= 2

    step = 1
    while step < chips:
        halves = held.reshape((held.shape[0] // 2, 2) + held.shape[1:])
        upper = (block & (2 * step)) != 0
        held = jnp.where(upper, halves[:, 1], halves[:, 0])
        send = jnp.where(upper, halves[:, 0], halves[:, 1])
        got = exchange(jnp.concatenate([sums, send.reshape(-1, pair)], axis=0), 0, (2 * step) | 1)
        step *= 2
        if step < chips:
            held = jnp.concatenate([held, got[count:].reshape(held.shape)], axis=1)
            sums = sums + got[:count]

    held = held.reshape(-1, pair)
    if pair % LANES:
        total = (sums + got[:count]).reshape(count // chips, chips, pair)
        order = (block // 2) ^ jnp.arange(chips, dtype=jnp.int32)
        return factor * lax.dot_general(
            jnp.take(total, order, axis=1),
            jnp.concatenate([held, got[count:]], axis=0).reshape(chips, cols, pair),
            (((1, 2), (0, 2)), ((), ())),
            precision=lax.Precision.HIGHEST,
        )
    vmem = pl.BlockSpec(memory_space=pltpu.VMEM)
    return pl.pallas_call(
        functools.partial(share_kernel, factor, chips),
        out_shape=jax.ShapeDtypeStruct((count // chips, cols), jnp.float32),
        in_specs=[vmem] * 3,
        out_specs=vmem,
        scratch_shapes=[pltpu.VMEM((count, pair), jnp.float32)],
    )(*[pltpu.with_memory_space_constraint(array, pltpu.VMEM) for array in (sums, got, held)])


def solution(mesh):
    placed = (
        P(None, None, ("sec", "blk"), None),
        P(None, ("sec", "blk"), None),
        P(("sec", "blk"), None),
        P(None, None, ("sec", "blk"), None),
        P("blk", None),
        P(),
        P(("sec", "blk")),
    )
    return jax.shard_map(
        shards, mesh=mesh, in_specs=placed, out_specs=P("sec", "blk"), check_vma=False
    )
```

time: 25.7 us -> 22.1 us (0.86)
  local copies, waits for them, and re-layouts: 2.47 us -> 0.08 us
  starting transfers between devices: 12.1 us -> 9.73 us
  waiting for transfers between devices: 4.87 us -> 6.91 us
  matrix products: 1.12 us -> 0 us
  Pallas kernels: 4.43 us -> 4.7 us
    ppermute x8 -> x5, starting transfers between devices: 12.1 us -> 9.73 us  [exchange(): return lax.ppermute(block, ('sec', 'blk'), pairs)]
    ppermute x8 -> x5, waiting for transfers between devices: 4.87 us -> 6.91 us  [exchange(): return lax.ppermute(block, ('sec', 'blk'), pairs)]
    gather x2 -> x0, local copies, waits for them, and re-layouts: 1.13 us -> none  [the longest x1 0.57 us: shards(): jnp.take(sums.reshape(sums.shape[0], chips, sums.shape[1] // chips), chip...]
    dot_general x2 -> x0, matrix products: 1.12 us -> none  [the longest x1 0.78 us: shards(): lax.dot_general(parts, jnp.concatenate(columns, axis=1), (((1,), (1,)), (...]
    unnamed x10 -> x0, local copies, waits for them, and re-layouts: 0.71 us -> none
    slice x7 -> x2, local copies, waits for them, and re-layouts: 0.4 us -> 0.08 us  [the longest x1 0.07 us: shards(): arrived = jnp.concatenate([got[count:, :own], got[count:, own:]], axis=0)]
    pallas_call x1 -> x2, Pallas kernels: 4.43 us -> 4.7 us  [the longest x1 3.94 us: partial_sums(): pl.pallas_call(functools.partial(partial_kernel, blocks), out_shape=(jax....]
  transfers between devices with their start and end apart: 8 -> 5, of which waited for: 4 -> 5; matrix products, arithmetic and copies ran while one was open for 9% -> 1% of each run, Pallas kernels for 0% -> 0%
where the time goes in v4:
time: 22.1 us; the launch traced here: 21.6 us
  starting transfers between devices  9.73 us (44%)
  waiting for transfers between devices  6.91 us (31%)
  Pallas kernels  4.7 us (21%)
    ppermute x5, starting transfers between devices, exchange(): return lax.ppermute(block, ('sec', 'blk'), pairs)  9.73 us
    ppermute x5, waiting for transfers between devices, exchange(): return lax.ppermute(block, ('sec', 'blk'), pairs)  6.91 us
    pallas_call x1, Pallas kernels, partial_sums(): pl.pallas_call(functools.partial(partial_kernel, blocks), out_shape=(jax....  3.94 us
    pallas_call x1, Pallas kernels, shards(): pl.pallas_call(functools.partial(share_kernel, factor, chips), out_shape=...  0.76 us
  transfers between devices with their start and end apart: 5, of which 5 were waited for; matrix products, arithmetic and copies ran while one was open for 1% of the time, Pallas kernels for 0%

profile of v4, /device:TPU:0, one launch (start us, length us, event | category | flops | bytes accessed | tf_op | source)
XLA Modules:
  0.0 21.6 jit_solution(7457344037271655775)
XLA Ops:
  0.0 3.9 %shard_map.100 = (f32[128,128]{1,0:T(8,128)S(1)}, f32[128,64]{1,0:T(8,128)S(1)}) custom-call(s32[2]{0:T(128)} %map_hbm.1, s32[1,256]{1,0:T(1,128)} %bitcast.29, bf16[16,3,2,512]{3,2,1,0:T(2,128)(2,1)} %velocity_hbm.1, f32[9,2,512]{2,1,0:T(2,128)} %geometry_hbm.1, f32[2,512]{1,0:T(2,128)} %mass_hbm.1, f32[1,512]{1,0:T(1,128)} %constant.30.point_hbm, ...), custom_call_target="tpu_custom_call" | custom-call | tf_op jit(solution)/shard_map/pallas_call | solution.py:277
  3.9 0.5 %collective-permute-start = (f32[128,128]{1,0:T(8,128)S(1)}, f32[128,128]{1,0:T(8,128)S(1)}, u32[]{:S(2)}, u32[]{:S(2)}) collective-permute-start(f32[128,128]{1,0:T(8,128)S(1)} %get-tuple-element.7), channel_id=1, source_target_pairs={{0,1},{1,0},{2,3},{3,2},{4,5},{5,4},{6,7},{7,6},{8,9},{9,8},{10,11... | collective-permute-start | bytes 196616 | tf_op jit(solution)/shard_map/ppermute | solution.py:328
  4.5 0.9 %collective-permute-done = f32[128,128]{1,0:T(8,128)S(1)} collective-permute-done((f32[128,128]{1,0:T(8,128)S(1)}, f32[128,128]{1,0:T(8,128)S(1)}, u32[]{:S(2)}, u32[]{:S(2)}) %collective-permute-start) | collective-permute-done | bytes 65568 | tf_op jit(solution)/shard_map/ppermute | solution.py:328
  5.4 2.7 %collective-permute-start.1 = (f32[32,128]{1,0:T(8,128)S(1)}, f32[32,128]{1,0:T(8,128)S(1)}, u32[]{:S(2)}, u32[]{:S(2)}) collective-permute-start(f32[32,128]{1,0:T(8,128)S(1)} %slice_select_fusion.2), channel_id=1, source_target_pairs={{0,17},{1,16},{2,19},{3,18},{4,21},{5,20},{6,23},{7,22},{8,25},{9,... | collective-permute-start | bytes 49160 | tf_op jit(solution)/shard_map/ppermute | solution.py:328
  8.1 0.1 fusion.3
  8.2 0.1 pad_maximum_fusion.1
  8.3 1.3 %collective-permute-done.1 = f32[32,128]{1,0:T(8,128)S(1)} collective-permute-done((f32[32,128]{1,0:T(8,128)S(1)}, f32[32,128]{1,0:T(8,128)S(1)}, u32[]{:S(2)}, u32[]{:S(2)}) %collective-permute-start.1) | collective-permute-done | bytes 16416 | tf_op jit(solution)/shard_map/ppermute | solution.py:328
  9.5 1.8 %collective-permute-start.2 = (f32[16,128]{1,0:T(8,128)S(1)}, f32[16,128]{1,0:T(8,128)S(1)}, u32[]{:S(2)}, u32[]{:S(2)}) collective-permute-start(f32[16,128]{1,0:T(8,128)S(1)} %slice_select_fusion.3), channel_id=1, source_target_pairs={{0,9},{1,8},{2,11},{3,10},{4,13},{5,12},{6,15},{7,14},{8,1},{9,0},... | collective-permute-start | bytes 24584 | tf_op jit(solution)/shard_map/ppermute | solution.py:328
  11.3 1.4 %collective-permute-done.2 = f32[16,128]{1,0:T(8,128)S(1)} collective-permute-done((f32[16,128]{1,0:T(8,128)S(1)}, f32[16,128]{1,0:T(8,128)S(1)}, u32[]{:S(2)}, u32[]{:S(2)}) %collective-permute-start.2) | collective-permute-done | bytes 8224 | tf_op jit(solution)/shard_map/ppermute | solution.py:328
  12.7 1.8 %collective-permute-start.3 = (f32[80,128]{1,0:T(8,128)S(1)}, f32[80,128]{1,0:T(8,128)S(1)}, u32[]{:S(2)}, u32[]{:S(2)}) collective-permute-start(f32[80,128]{1,0:T(8,128)S(1)} %pad_maximum_fusion.2), channel_id=1, source_target_pairs={{0,3},{1,2},{2,1},{3,0},{4,7},{5,6},{6,5},{7,4},{8,11},{9,10},{10,... | collective-permute-start | bytes 122888 | tf_op jit(solution)/shard_map/ppermute | solution.py:328
  14.5 1.7 %collective-permute-done.3 = f32[80,128]{1,0:T(8,128)S(1)} collective-permute-done((f32[80,128]{1,0:T(8,128)S(1)}, f32[80,128]{1,0:T(8,128)S(1)}, u32[]{:S(2)}, u32[]{:S(2)}) %collective-permute-start.3) | collective-permute-done | bytes 40992 | tf_op jit(solution)/shard_map/ppermute | solution.py:328
  16.3 2.9 %collective-permute-start.4 = (f32[80,128]{1,0:T(8,128)S(1)}, f32[80,128]{1,0:T(8,128)S(1)}, u32[]{:S(2)}, u32[]{:S(2)}) collective-permute-start(f32[80,128]{1,0:T(8,128)S(1)} %pad_maximum_fusion.3), channel_id=1, source_target_pairs={{0,5},{1,4},{2,7},{3,6},{4,1},{5,0},{6,3},{7,2},{8,13},{9,12},{10,... | collective-permute-start | bytes 122888 | tf_op jit(solution)/shard_map/ppermute | solution.py:328
  19.2 1.7 %collective-permute-done.4.got_ref = f32[80,128]{1,0:T(8,128)S(1)} collective-permute-done((f32[80,128]{1,0:T(8,128)S(1)}, f32[80,128]{1,0:T(8,128)S(1)}, u32[]{:S(2)}, u32[]{:S(2)}) %collective-permute-start.4) | collective-permute-done | bytes 40992 | tf_op jit(solution)/shard_map/ppermute | solution.py:328
  20.9 0.8 %shard_map.101 = f32[4,32]{1,0:T(4,128)} custom-call(f32[16,128]{1,0:T(8,128)S(1)} %slice_add_fusion.1.sums_ref, f32[80,128]{1,0:T(8,128)S(1)} %collective-permute-done.4.got_ref, f32[64,128]{1,0:T(8,128)S(1)} %bitcast.24), custom_call_target="tpu_custom_call" | custom-call | tf_op jit(solution)/shard_map/pallas_call | solution.py:398
  (13 shorter events, 0.1 us)
Async XLA Ops:
  3.9 1.4 %collective-permute-start = (f32[128,128]{1,0:T(8,128)S(1)}, f32[128,128]{1,0:T(8,128)S(1)}, u32[]{:S(2)}, u32[]{:S(2)}) collective-permute-start(f32[128,128]{1,0:T(8,128)S(1)} %get-tuple-element.7), channel_id=1, source_target_pairs={{0,1},{1,0},{2,3},{3,2},{4,5},{5,4},{6,7},{7,6},{8,9},{9,8},{10,11... | collective-permute-start | bytes 196616 | tf_op jit(solution)/shard_map/ppermute | solution.py:328
  5.4 4.1 %collective-permute-start.1 = (f32[32,128]{1,0:T(8,128)S(1)}, f32[32,128]{1,0:T(8,128)S(1)}, u32[]{:S(2)}, u32[]{:S(2)}) collective-permute-start(f32[32,128]{1,0:T(8,128)S(1)} %slice_select_fusion.2), channel_id=1, source_target_pairs={{0,17},{1,16},{2,19},{3,18},{4,21},{5,20},{6,23},{7,22},{8,25},{9,... | collective-permute-start | bytes 49160 | tf_op jit(solution)/shard_map/ppermute | solution.py:328
  9.5 3.1 %collective-permute-start.2 = (f32[16,128]{1,0:T(8,128)S(1)}, f32[16,128]{1,0:T(8,128)S(1)}, u32[]{:S(2)}, u32[]{:S(2)}) collective-permute-start(f32[16,128]{1,0:T(8,128)S(1)} %slice_select_fusion.3), channel_id=1, source_target_pairs={{0,9},{1,8},{2,11},{3,10},{4,13},{5,12},{6,15},{7,14},{8,1},{9,0},... | collective-permute-start | bytes 24584 | tf_op jit(solution)/shard_map/ppermute | solution.py:328
  12.7 3.5 %collective-permute-start.3 = (f32[80,128]{1,0:T(8,128)S(1)}, f32[80,128]{1,0:T(8,128)S(1)}, u32[]{:S(2)}, u32[]{:S(2)}) collective-permute-start(f32[80,128]{1,0:T(8,128)S(1)} %pad_maximum_fusion.2), channel_id=1, source_target_pairs={{0,3},{1,2},{2,1},{3,0},{4,7},{5,6},{6,5},{7,4},{8,11},{9,10},{10,... | collective-permute-start | bytes 122888 | tf_op jit(solution)/shard_map/ppermute | solution.py:328
  16.3 4.6 %collective-permute-start.4 = (f32[80,128]{1,0:T(8,128)S(1)}, f32[80,128]{1,0:T(8,128)S(1)}, u32[]{:S(2)}, u32[]{:S(2)}) collective-permute-start(f32[80,128]{1,0:T(8,128)S(1)} %pad_maximum_fusion.3), channel_id=1, source_target_pairs={{0,5},{1,4},{2,7},{3,6},{4,1},{5,0},{6,3},{7,2},{8,13},{9,12},{10,... | collective-permute-start | bytes 122888 | tf_op jit(solution)/shard_map/ppermute | solution.py:328

commit v5 on v4

--- a/solution.py
+++ b/solution.py
@@ -3,7 +3,6 @@
 
 import jax
 import jax.numpy as jnp
-import ml_dtypes
 import numpy as np
 from jax import lax
 from jax.experimental import pallas as pl
@@ -73,17 +72,18 @@
     side = table.shape[0]
     lanes = np.arange(LANES)
     per_block = LANES // (side * side)
-    r_rows = np.zeros((points // LANES * side, LANES), np.float32)
-    for block in range(points // LANES):
-        for node in range(side):
-            r_rows[block * side + node] = table[block * per_block + lanes // (side * side), node]
     i, j, k = lanes // (side * side), lanes // side % side, lanes % side
     along_s = table[j[None, :], j[:, None]] * (i[None, :] == i[:, None]) * (k[None, :] == k[:, None])
     along_t = table[k[None, :], k[:, None]] * (i[None, :] == i[:, None]) * (j[None, :] == j[:, None])
-    both = np.concatenate([along_s, along_t], axis=1).astype(np.float32)
-    high = both.astype(ml_dtypes.bfloat16)
-    low = (both - high.astype(np.float32)).astype(ml_dtypes.bfloat16)
-    return r_rows, np.concatenate([high, low], axis=0)
+    along_r = [table[p * per_block + i, node] for p in range(points // LANES) for node in range(side)]
+    return np.concatenate(
+        [along_s, along_t, np.stack(along_r), point_weights().reshape(-1, LANES)], axis=0
+    ).astype(np.float32)
+
+
+def halves_of(values):
+    high = values.astype(jnp.bfloat16)
+    return high, (values - high.astype(jnp.float32)).astype(jnp.bfloat16)
 
 
 def pair_rows(rows, height):
@@ -115,9 +115,7 @@
     velocity_hbm,
     geometry_hbm,
     mass_hbm,
-    point_hbm,
-    r_hbm,
-    st_hbm,
+    table_hbm,
     eigvecs_hbm,
     snapshots_hbm,
     out_ref,
@@ -127,13 +125,10 @@
     velocity_ref,
     geometry_ref,
     mass_ref,
-    point_ref,
-    r_ref,
-    st_ref,
+    table_ref,
     eigvecs_ref,
     snapshots_ref,
     product_ref,
-    turned_ref,
     columns_ref,
     semaphores,
 ):
@@ -141,26 +136,18 @@
     snaps = snapshots_hbm.shape[0]
     own, mode_count = eigvecs_hbm.shape
     parts = points // LANES
-    side = r_hbm.shape[0] // parts
     rows = fields * elements
     chunks = [(c, p) for c in range(components) for p in range(parts)]
     small = [
-        (velocity_hbm.at[:, c, :, pl.ds(p * LANES, LANES)], velocity_ref.at[n])
-        for n, (c, p) in enumerate(chunks)
-    ]
-    small += [
-        (st_hbm, st_ref),
-        (r_hbm, r_ref),
+        (velocity_hbm, velocity_ref),
+        (table_hbm, table_ref),
         (geometry_hbm, geometry_ref),
         (mass_hbm, mass_ref),
-        (point_hbm, point_ref),
-    ]
-    large = [
-        (map_hbm, map_ref),
         (order_hbm, order_ref),
         (eigvecs_hbm, eigvecs_ref),
-    ]
-    large += [
+        (map_hbm, map_ref),
+    ]
+    large = [
         (snapshots_hbm.at[:, c, :, pl.ds(p * LANES, LANES)], snapshots_ref.at[n])
         for n, (c, p) in enumerate(chunks)
     ]
@@ -173,11 +160,18 @@
     for copy in copies[: len(small)]:
         copy.wait()
 
-    packed = [velocity_ref.at[n].reshape(rows, LANES)[...] for n in range(len(chunks))]
+    packed = [
+        velocity_ref[:, c, :, p * LANES : (p + 1) * LANES].reshape(rows, LANES) for c, p in chunks
+    ]
     stacked = jnp.concatenate(packed, axis=0)
+    st_high, st_low = halves_of(jnp.concatenate([table_ref[:LANES, :], table_ref[LANES : 2 * LANES, :]], axis=1))
     along_st = jnp.dot(
-        jnp.concatenate([stacked, stacked], axis=1), st_ref[...], preferred_element_type=jnp.float32
-    )
+        jnp.concatenate([stacked, stacked], axis=1),
+        jnp.concatenate([st_high, st_low], axis=0),
+        preferred_element_type=jnp.float32,
+    )
+    point_row = table_hbm.shape[0] - parts
+    side = (point_row - 2 * LANES) // parts
     lower = lax.broadcasted_iota(jnp.int32, (rows, LANES), 1) < LANES // 2
     along_r = []
     for c in range(components):
@@ -187,15 +181,16 @@
             other = pltpu.roll(here, LANES // 2, 1)
             nodes += [jnp.where(lower, here, other), jnp.where(lower, other, here)]
         for p in range(parts):
-            total = r_ref[p * side : p * side + 1, :] * nodes[0]
+            first = 2 * LANES + p * side
+            total = table_ref[first : first + 1, :] * nodes[0]
             for node in range(1, side):
-                total += r_ref[p * side + node : p * side + node + 1, :] * nodes[node]
+                total += table_ref[first + node : first + node + 1, :] * nodes[node]
             along_r.append(total)
 
     weighted = [None] * len(chunks)
     for p in range(parts):
         lanes = slice(p * LANES, (p + 1) * LANES)
-        weight = mass_ref[:, lanes] * point_ref[:, lanes]
+        weight = mass_ref[:, lanes] * table_ref[point_row + p : point_row + p + 1, :]
         factors = [pair_rows(weight * geometry_ref[n, :, lanes], rows) for n in range(9)]
 
         def gradient(component, coord):
@@ -210,20 +205,13 @@
         for c in range(components):
             after, last = (c + 1) % 3, (c + 2) % 3
             weighted[c * parts + p] = (gradient(last, after) - gradient(after, last)).astype(jnp.bfloat16)
-    weighted = jnp.concatenate(weighted, axis=1)
-
-    for copy in copies[len(small) : len(small) + 3]:
-        copy.wait()
+
     selector = (
         lax.broadcasted_iota(jnp.int32, (mode_count, mode_count), 0) == order_ref[...]
     ).astype(jnp.bfloat16)
-    rest = eigvecs_ref[...]
-    ordered = jnp.zeros(rest.shape, jnp.float32)
-    for _ in range(3):
-        piece = rest.astype(jnp.bfloat16)
-        ordered += jnp.dot(piece, selector, preferred_element_type=jnp.float32)
-        rest = rest - piece.astype(jnp.float32)
-    columns_ref[...] = ordered.T
+    columns_ref[...] = sum(
+        jnp.dot(piece, selector, preferred_element_type=jnp.float32) for piece in halves_of(eigvecs_ref[...])
+    ).T
     cols, chips = mode_count // blocks, blocks // 2
     odd = odd_block(lax.axis_index("blk"), blocks)
     half = mode_count // 4
@@ -236,32 +224,50 @@
         row, lane = chip * cols % half, chip * cols // half * own
         out_ref[first + row : first + row + cols, lane : lane + own] = send
 
-    for copy in copies[len(small) + 3 :]:
-        copy.wait()
-    height = snaps * elements
-    step = min(height, 256)
-    for start in range(0, height, step):
-        part = jnp.concatenate(
-            [snapshots_ref.at[n].reshape(height, LANES)[start : start + step] for n in range(len(chunks))], axis=1
-        )
-        product_ref[start : start + step, :rows] = lax.dot_general(
-            part, weighted, (((1,), (1,)), ((), ())), preferred_element_type=jnp.float32
-        )
-    turn = lax.broadcasted_iota(jnp.int32, (snaps, rows), 1) % elements
-    chosen = jnp.zeros((snaps, rows), jnp.float32)
-    for slot in range(elements):
-        here = product_ref[pl.ds(slot, snaps, stride=elements), :][:, :rows]
-        for elem in range(elements):
-            chosen = jnp.where((turn == elem) & (map_ref[elem] == slot), here, chosen)
-    for n in range(snaps // LANES):
-        turned_ref[n * rows : (n + 1) * rows, :] = chosen[n * LANES : (n + 1) * LANES, :].T
+    width = LANES * elements
+    spans = snaps // LANES
+    adder = (
+        lax.broadcasted_iota(jnp.int32, (width, LANES), 0) // elements
+        == lax.broadcasted_iota(jnp.int32, (width, LANES), 1)
+    ).astype(jnp.bfloat16)
+    slot = lax.broadcasted_iota(jnp.int32, (fields, LANES), 1) % elements
+    for c in range(components):
+        group = range(c * parts, (c + 1) * parts)
+        for n in group:
+            copies[len(small) + n].wait()
+        values = jnp.concatenate([weighted[n] for n in group], axis=1)
+        for span in range(spans):
+            part = jnp.concatenate(
+                [
+                    snapshots_ref.at[n].reshape(snaps * elements, LANES)[span * width : (span + 1) * width]
+                    for n in group
+                ],
+                axis=1,
+            )
+            product = lax.dot_general(values, part, (((1,), (1,)), ((), ())), preferred_element_type=jnp.float32)
+            for piece in range(elements):
+                place = slice((span * elements + piece) * rows, (span * elements + piece + 1) * rows)
+                added = product[:, piece * LANES : (piece + 1) * LANES]
+                product_ref[place, :] = added + product_ref[place, :] if c else added
+    matched = []
+    for block in range(spans * elements):
+        chosen = product_ref[pl.ds(block * rows, fields, stride=elements), :]
+        for elem in range(1, elements):
+            here = product_ref[pl.ds(block * rows + elem, fields, stride=elements), :]
+            chosen = jnp.where(slot == map_ref[elem], here, chosen)
+        matched.append(halves_of(chosen))
+    matched = [
+        jnp.concatenate([matched[span * elements + piece][part] for piece in range(elements)], axis=1)
+        for span in range(spans)
+        for part in range(2)
+    ]
+    totals = jnp.dot(jnp.concatenate(matched, axis=0), adder, preferred_element_type=jnp.float32)
     pair = 2 * own
-    for n in range(snaps // LANES):
-        total = turned_ref[pl.ds(n * rows, fields, stride=elements), :]
-        for elem in range(1, elements):
-            total += turned_ref[pl.ds(n * rows + elem, fields, stride=elements), :]
-        for chip in range(n * LANES // pair, (n + 1) * LANES // pair):
-            lane = chip * pair - n * LANES
+    for span in range(spans):
+        row = 2 * span * fields
+        total = totals[row : row + fields] + totals[row + fields : row + 2 * fields]
+        for lane in range(0, LANES, pair):
+            chip = (span * LANES + lane) // pair
             out_ref[pl.ds(chip, fields, stride=chips), :] = total[:, lane : lane + pair]
 
 
@@ -270,9 +276,8 @@
     snaps = snapshots.shape[0]
     own, mode_count = eigvecs.shape
     blocks = snaps // own
-    r_rows, st = along_tables(points)
+    table = along_tables(points)
     chunks = components * (points // LANES)
-    rows = fields * elements
     vmem = pl.BlockSpec(memory_space=pltpu.VMEM)
     return pl.pallas_call(
         functools.partial(partial_kernel, blocks),
@@ -280,23 +285,20 @@
             jax.ShapeDtypeStruct((fields * blocks // 2 + mode_count // 4, 2 * own), jnp.float32),
             jax.ShapeDtypeStruct((mode_count // 2, own), jnp.float32),
         ),
-        in_specs=[pl.BlockSpec(memory_space=pltpu.HBM)] * 10,
+        in_specs=[pl.BlockSpec(memory_space=pltpu.HBM)] * 8,
         out_specs=(vmem, vmem),
         scratch_shapes=[
             pltpu.SMEM(elem_map.shape, jnp.int32),
             pltpu.VMEM((1, mode_count), jnp.int32),
-            pltpu.VMEM((chunks, fields, elements, LANES), jnp.bfloat16),
+            pltpu.VMEM(velocity.shape, jnp.bfloat16),
             pltpu.VMEM(geometry.shape, jnp.float32),
             pltpu.VMEM(mass.shape, jnp.float32),
-            pltpu.VMEM((1, points), jnp.float32),
-            pltpu.VMEM(r_rows.shape, jnp.float32),
-            pltpu.VMEM(st.shape, jnp.bfloat16),
+            pltpu.VMEM(table.shape, jnp.float32),
             pltpu.VMEM(eigvecs.shape, jnp.float32),
             pltpu.VMEM((chunks, snaps, elements, LANES), jnp.bfloat16),
-            pltpu.VMEM((snaps * elements, LANES), jnp.float32),
-            pltpu.VMEM((snaps // LANES * rows, LANES), jnp.float32),
+            pltpu.VMEM((snaps * elements // LANES * fields * elements, LANES), jnp.float32),
             pltpu.VMEM((mode_count, own), jnp.float32),
-            pltpu.SemaphoreType.DMA((8 + 2 * chunks,)),
+            pltpu.SemaphoreType.DMA((7 + chunks,)),
         ],
         compiler_params=pltpu.CompilerParams(vmem_limit_bytes=40 * 1024 * 1024),
     )(
@@ -308,9 +310,7 @@
                 velocity,
                 geometry,
                 mass,
-                jnp.asarray(point_weights()).reshape(1, points),
-                jnp.asarray(r_rows),
-                jnp.asarray(st),
+                jnp.asarray(table),
                 eigvecs,
                 snapshots,
             )

time: 22.1 us -> 21.5 us (0.973)
  Pallas kernels: 4.7 us -> 4.17 us
    pallas_call x1, Pallas kernels: 3.94 us -> 3.41 us  [partial_sums(): pl.pallas_call(functools.partial(partial_kernel, blocks), out_shape=(jax....]
where the time goes in v5:
time: 21.5 us; the launch traced here: 21.1 us
  starting transfers between devices  9.73 us (45%)
  waiting for transfers between devices  6.91 us (32%)
  Pallas kernels  4.17 us (19%)
    ppermute x5, starting transfers between devices, exchange(): return lax.ppermute(block, ('sec', 'blk'), pairs)  9.73 us
    ppermute x5, waiting for transfers between devices, exchange(): return lax.ppermute(block, ('sec', 'blk'), pairs)  6.91 us
    pallas_call x1, Pallas kernels, partial_sums(): pl.pallas_call(functools.partial(partial_kernel, blocks), out_shape=(jax....  3.41 us
    pallas_call x1, Pallas kernels, shards(): pl.pallas_call(functools.partial(share_kernel, factor, chips), out_shape=...  0.76 us
  transfers between devices with their start and end apart: 5, of which 5 were waited for; matrix products, arithmetic and copies ran while one was open for 1% of the time, Pallas kernels for 0%

profile of v5, /device:TPU:0, one launch (start us, length us, event | category | flops | bytes accessed | tf_op | source)
XLA Modules:
  0.0 21.1 jit_solution(15039616925036515983)
XLA Ops:
  0.0 3.4 %shard_map.82 = (f32[128,128]{1,0:T(8,128)S(1)}, f32[128,64]{1,0:T(8,128)S(1)}) custom-call(s32[2]{0:T(128)} %map_hbm.1, s32[1,256]{1,0:T(1,128)} %bitcast.29, bf16[16,3,2,512]{3,2,1,0:T(2,128)(2,1)} %velocity_hbm.1, f32[9,2,512]{2,1,0:T(2,128)} %geometry_hbm.1, f32[2,512]{1,0:T(2,128)} %mass_hbm.1, f32[292,128]{1,0:T(8,128)} %constant.18.clone.table_hbm, ...), custom_call_target="tpu_custom_call" | custom-call | tf_op jit(solution)/shard_map/pallas_call | solution.py:282
  3.4 0.5 %collective-permute-start = (f32[128,128]{1,0:T(8,128)S(1)}, f32[128,128]{1,0:T(8,128)S(1)}, u32[]{:S(2)}, u32[]{:S(2)}) collective-permute-start(f32[128,128]{1,0:T(8,128)S(1)} %get-tuple-element.7), channel_id=1, source_target_pairs={{0,1},{1,0},{2,3},{3,2},{4,5},{5,4},{6,7},{7,6},{8,9},{9,8},{10,11... | collective-permute-start | bytes 196616 | tf_op jit(solution)/shard_map/ppermute | solution.py:328
  3.9 0.9 %collective-permute-done = f32[128,128]{1,0:T(8,128)S(1)} collective-permute-done((f32[128,128]{1,0:T(8,128)S(1)}, f32[128,128]{1,0:T(8,128)S(1)}, u32[]{:S(2)}, u32[]{:S(2)}) %collective-permute-start) | collective-permute-done | bytes 65568 | tf_op jit(solution)/shard_map/ppermute | solution.py:328
  4.9 2.7 %collective-permute-start.1 = (f32[32,128]{1,0:T(8,128)S(1)}, f32[32,128]{1,0:T(8,128)S(1)}, u32[]{:S(2)}, u32[]{:S(2)}) collective-permute-start(f32[32,128]{1,0:T(8,128)S(1)} %slice_select_fusion.2), channel_id=1, source_target_pairs={{0,17},{1,16},{2,19},{3,18},{4,21},{5,20},{6,23},{7,22},{8,25},{9,... | collective-permute-start | bytes 49160 | tf_op jit(solution)/shard_map/ppermute | solution.py:328
  7.5 0.1 fusion.3
  7.6 0.1 pad_maximum_fusion.1
  7.7 1.3 %collective-permute-done.1 = f32[32,128]{1,0:T(8,128)S(1)} collective-permute-done((f32[32,128]{1,0:T(8,128)S(1)}, f32[32,128]{1,0:T(8,128)S(1)}, u32[]{:S(2)}, u32[]{:S(2)}) %collective-permute-start.1) | collective-permute-done | bytes 16416 | tf_op jit(solution)/shard_map/ppermute | solution.py:328
  9.0 1.8 %collective-permute-start.2 = (f32[16,128]{1,0:T(8,128)S(1)}, f32[16,128]{1,0:T(8,128)S(1)}, u32[]{:S(2)}, u32[]{:S(2)}) collective-permute-start(f32[16,128]{1,0:T(8,128)S(1)} %slice_select_fusion.3), channel_id=1, source_target_pairs={{0,9},{1,8},{2,11},{3,10},{4,13},{5,12},{6,15},{7,14},{8,1},{9,0},... | collective-permute-start | bytes 24584 | tf_op jit(solution)/shard_map/ppermute | solution.py:328
  10.8 1.4 %collective-permute-done.2 = f32[16,128]{1,0:T(8,128)S(1)} collective-permute-done((f32[16,128]{1,0:T(8,128)S(1)}, f32[16,128]{1,0:T(8,128)S(1)}, u32[]{:S(2)}, u32[]{:S(2)}) %collective-permute-start.2) | collective-permute-done | bytes 8224 | tf_op jit(solution)/shard_map/ppermute | solution.py:328
  12.2 1.8 %collective-permute-start.3 = (f32[80,128]{1,0:T(8,128)S(1)}, f32[80,128]{1,0:T(8,128)S(1)}, u32[]{:S(2)}, u32[]{:S(2)}) collective-permute-start(f32[80,128]{1,0:T(8,128)S(1)} %pad_maximum_fusion.2), channel_id=1, source_target_pairs={{0,3},{1,2},{2,1},{3,0},{4,7},{5,6},{6,5},{7,4},{8,11},{9,10},{10,... | collective-permute-start | bytes 122888 | tf_op jit(solution)/shard_map/ppermute | solution.py:328
  14.0 1.7 %collective-permute-done.3 = f32[80,128]{1,0:T(8,128)S(1)} collective-permute-done((f32[80,128]{1,0:T(8,128)S(1)}, f32[80,128]{1,0:T(8,128)S(1)}, u32[]{:S(2)}, u32[]{:S(2)}) %collective-permute-start.3) | collective-permute-done | bytes 40992 | tf_op jit(solution)/shard_map/ppermute | solution.py:328
  15.7 2.9 %collective-permute-start.4 = (f32[80,128]{1,0:T(8,128)S(1)}, f32[80,128]{1,0:T(8,128)S(1)}, u32[]{:S(2)}, u32[]{:S(2)}) collective-permute-start(f32[80,128]{1,0:T(8,128)S(1)} %pad_maximum_fusion.3), channel_id=1, source_target_pairs={{0,5},{1,4},{2,7},{3,6},{4,1},{5,0},{6,3},{7,2},{8,13},{9,12},{10,... | collective-permute-start | bytes 122888 | tf_op jit(solution)/shard_map/ppermute | solution.py:328
  18.7 1.7 %collective-permute-done.4.got_ref = f32[80,128]{1,0:T(8,128)S(1)} collective-permute-done((f32[80,128]{1,0:T(8,128)S(1)}, f32[80,128]{1,0:T(8,128)S(1)}, u32[]{:S(2)}, u32[]{:S(2)}) %collective-permute-start.4) | collective-permute-done | bytes 40992 | tf_op jit(solution)/shard_map/ppermute | solution.py:328
  20.4 0.8 %shard_map.83 = f32[4,32]{1,0:T(4,128)} custom-call(f32[16,128]{1,0:T(8,128)S(1)} %slice_add_fusion.1.sums_ref, f32[80,128]{1,0:T(8,128)S(1)} %collective-permute-done.4.got_ref, f32[64,128]{1,0:T(8,128)S(1)} %bitcast.24), custom_call_target="tpu_custom_call" | custom-call | tf_op jit(solution)/shard_map/pallas_call | solution.py:398
  (13 shorter events, 0.1 us)
Async XLA Ops:
  3.4 1.4 %collective-permute-start = (f32[128,128]{1,0:T(8,128)S(1)}, f32[128,128]{1,0:T(8,128)S(1)}, u32[]{:S(2)}, u32[]{:S(2)}) collective-permute-start(f32[128,128]{1,0:T(8,128)S(1)} %get-tuple-element.7), channel_id=1, source_target_pairs={{0,1},{1,0},{2,3},{3,2},{4,5},{5,4},{6,7},{7,6},{8,9},{9,8},{10,11... | collective-permute-start | bytes 196616 | tf_op jit(solution)/shard_map/ppermute | solution.py:328
  4.9 4.1 %collective-permute-start.1 = (f32[32,128]{1,0:T(8,128)S(1)}, f32[32,128]{1,0:T(8,128)S(1)}, u32[]{:S(2)}, u32[]{:S(2)}) collective-permute-start(f32[32,128]{1,0:T(8,128)S(1)} %slice_select_fusion.2), channel_id=1, source_target_pairs={{0,17},{1,16},{2,19},{3,18},{4,21},{5,20},{6,23},{7,22},{8,25},{9,... | collective-permute-start | bytes 49160 | tf_op jit(solution)/shard_map/ppermute | solution.py:328
  9.0 3.1 %collective-permute-start.2 = (f32[16,128]{1,0:T(8,128)S(1)}, f32[16,128]{1,0:T(8,128)S(1)}, u32[]{:S(2)}, u32[]{:S(2)}) collective-permute-start(f32[16,128]{1,0:T(8,128)S(1)} %slice_select_fusion.3), channel_id=1, source_target_pairs={{0,9},{1,8},{2,11},{3,10},{4,13},{5,12},{6,15},{7,14},{8,1},{9,0},... | collective-permute-start | bytes 24584 | tf_op jit(solution)/shard_map/ppermute | solution.py:328
  12.2 3.5 %collective-permute-start.3 = (f32[80,128]{1,0:T(8,128)S(1)}, f32[80,128]{1,0:T(8,128)S(1)}, u32[]{:S(2)}, u32[]{:S(2)}) collective-permute-start(f32[80,128]{1,0:T(8,128)S(1)} %pad_maximum_fusion.2), channel_id=1, source_target_pairs={{0,3},{1,2},{2,1},{3,0},{4,7},{5,6},{6,5},{7,4},{8,11},{9,10},{10,... | collective-permute-start | bytes 122888 | tf_op jit(solution)/shard_map/ppermute | solution.py:328
  15.7 4.6 %collective-permute-start.4 = (f32[80,128]{1,0:T(8,128)S(1)}, f32[80,128]{1,0:T(8,128)S(1)}, u32[]{:S(2)}, u32[]{:S(2)}) collective-permute-start(f32[80,128]{1,0:T(8,128)S(1)} %pad_maximum_fusion.3), channel_id=1, source_target_pairs={{0,5},{1,4},{2,7},{3,6},{4,1},{5,0},{6,3},{7,2},{8,13},{9,12},{10,... | collective-permute-start | bytes 122888 | tf_op jit(solution)/shard_map/ppermute | solution.py:328

commit v6 on v5

--- a/solution.py
+++ b/solution.py
@@ -108,7 +108,7 @@
     return odd
 
 
-def partial_kernel(
+def stored_kernel(
     blocks,
     map_hbm,
     order_hbm,
@@ -117,8 +117,8 @@
     mass_hbm,
     table_hbm,
     eigvecs_hbm,
-    snapshots_hbm,
-    out_ref,
+    stored_ref,
+    send_ref,
     keep_ref,
     map_ref,
     order_ref,
@@ -127,13 +127,10 @@
     mass_ref,
     table_ref,
     eigvecs_ref,
-    snapshots_ref,
-    product_ref,
     columns_ref,
     semaphores,
 ):
     fields, components, elements, points = velocity_hbm.shape
-    snaps = snapshots_hbm.shape[0]
     own, mode_count = eigvecs_hbm.shape
     parts = points // LANES
     rows = fields * elements
@@ -147,17 +144,13 @@
         (eigvecs_hbm, eigvecs_ref),
         (map_hbm, map_ref),
     ]
-    large = [
-        (snapshots_hbm.at[:, c, :, pl.ds(p * LANES, LANES)], snapshots_ref.at[n])
-        for n, (c, p) in enumerate(chunks)
-    ]
     copies = [
         pltpu.make_async_copy(source, target, semaphores.at[n])
-        for n, (source, target) in enumerate(small + large)
+        for n, (source, target) in enumerate(small)
     ]
     for copy in copies:
         copy.start()
-    for copy in copies[: len(small)]:
+    for copy in copies:
         copy.wait()
 
     packed = [
@@ -187,7 +180,8 @@
                 total += table_ref[first + node : first + node + 1, :] * nodes[node]
             along_r.append(total)
 
-    weighted = [None] * len(chunks)
+    straight = map_ref[0] == 0
+    first_row = lax.broadcasted_iota(jnp.int32, (rows, LANES), 0) % elements == 0
     for p in range(parts):
         lanes = slice(p * LANES, (p + 1) * LANES)
         weight = mass_ref[:, lanes] * table_ref[point_row + p : point_row + p + 1, :]
@@ -204,7 +198,10 @@
 
         for c in range(components):
             after, last = (c + 1) % 3, (c + 2) % 3
-            weighted[c * parts + p] = (gradient(last, after) - gradient(after, last)).astype(jnp.bfloat16)
+            values = gradient(last, after) - gradient(after, last)
+            turned = jnp.where(first_row, pltpu.roll(values, rows - 1, 0), pltpu.roll(values, 1, 0))
+            values = jnp.where(straight, values, turned).astype(jnp.bfloat16)
+            stored_ref[:, c, :, lanes] = values.reshape(fields, elements, LANES)
 
     selector = (
         lax.broadcasted_iota(jnp.int32, (mode_count, mode_count), 0) == order_ref[...]
@@ -215,78 +212,30 @@
     cols, chips = mode_count // blocks, blocks // 2
     odd = odd_block(lax.axis_index("blk"), blocks)
     half = mode_count // 4
-    first = fields * chips
     for chip in range(chips):
         even = parity(chip)
         keep = columns_ref[pl.ds((2 * chip + (even ^ odd)) * cols, cols), :]
         send = columns_ref[pl.ds((2 * chip + (even ^ 1 ^ odd)) * cols, cols), :]
         keep_ref[chip * cols : (chip + 1) * cols, :] = keep
         row, lane = chip * cols % half, chip * cols // half * own
-        out_ref[first + row : first + row + cols, lane : lane + own] = send
-
-    width = LANES * elements
-    spans = snaps // LANES
-    adder = (
-        lax.broadcasted_iota(jnp.int32, (width, LANES), 0) // elements
-        == lax.broadcasted_iota(jnp.int32, (width, LANES), 1)
-    ).astype(jnp.bfloat16)
-    slot = lax.broadcasted_iota(jnp.int32, (fields, LANES), 1) % elements
-    for c in range(components):
-        group = range(c * parts, (c + 1) * parts)
-        for n in group:
-            copies[len(small) + n].wait()
-        values = jnp.concatenate([weighted[n] for n in group], axis=1)
-        for span in range(spans):
-            part = jnp.concatenate(
-                [
-                    snapshots_ref.at[n].reshape(snaps * elements, LANES)[span * width : (span + 1) * width]
-                    for n in group
-                ],
-                axis=1,
-            )
-            product = lax.dot_general(values, part, (((1,), (1,)), ((), ())), preferred_element_type=jnp.float32)
-            for piece in range(elements):
-                place = slice((span * elements + piece) * rows, (span * elements + piece + 1) * rows)
-                added = product[:, piece * LANES : (piece + 1) * LANES]
-                product_ref[place, :] = added + product_ref[place, :] if c else added
-    matched = []
-    for block in range(spans * elements):
-        chosen = product_ref[pl.ds(block * rows, fields, stride=elements), :]
-        for elem in range(1, elements):
-            here = product_ref[pl.ds(block * rows + elem, fields, stride=elements), :]
-            chosen = jnp.where(slot == map_ref[elem], here, chosen)
-        matched.append(halves_of(chosen))
-    matched = [
-        jnp.concatenate([matched[span * elements + piece][part] for piece in range(elements)], axis=1)
-        for span in range(spans)
-        for part in range(2)
-    ]
-    totals = jnp.dot(jnp.concatenate(matched, axis=0), adder, preferred_element_type=jnp.float32)
-    pair = 2 * own
-    for span in range(spans):
-        row = 2 * span * fields
-        total = totals[row : row + fields] + totals[row + fields : row + 2 * fields]
-        for lane in range(0, LANES, pair):
-            chip = (span * LANES + lane) // pair
-            out_ref[pl.ds(chip, fields, stride=chips), :] = total[:, lane : lane + pair]
-
-
-def partial_sums(velocity, geometry, mass, snapshots, eigvecs, mode_order, elem_map):
+        send_ref[row : row + cols, lane : lane + own] = send
+
+
+def stored_vorticity(velocity, geometry, mass, eigvecs, mode_order, elem_map):
     fields, components, elements, points = velocity.shape
-    snaps = snapshots.shape[0]
     own, mode_count = eigvecs.shape
-    blocks = snaps // own
+    blocks = lax.axis_size("blk")
     table = along_tables(points)
-    chunks = components * (points // LANES)
     vmem = pl.BlockSpec(memory_space=pltpu.VMEM)
     return pl.pallas_call(
-        functools.partial(partial_kernel, blocks),
+        functools.partial(stored_kernel, blocks),
         out_shape=(
-            jax.ShapeDtypeStruct((fields * blocks // 2 + mode_count // 4, 2 * own), jnp.float32),
-            jax.ShapeDtypeStruct((mode_count // 2, own), jnp.float32),
+            pltpu.VMEM(velocity.shape, jnp.bfloat16),
+            pltpu.VMEM((mode_count // 4, 2 * own), jnp.float32),
+            pltpu.VMEM((mode_count // 2, own), jnp.float32),
         ),
-        in_specs=[pl.BlockSpec(memory_space=pltpu.HBM)] * 8,
-        out_specs=(vmem, vmem),
+        in_specs=[pl.BlockSpec(memory_space=pltpu.HBM)] * 7,
+        out_specs=(vmem,) * 3,
         scratch_shapes=[
             pltpu.SMEM(elem_map.shape, jnp.int32),
             pltpu.VMEM((1, mode_count), jnp.int32),
@@ -295,12 +244,9 @@
             pltpu.VMEM(mass.shape, jnp.float32),
             pltpu.VMEM(table.shape, jnp.float32),
             pltpu.VMEM(eigvecs.shape, jnp.float32),
-            pltpu.VMEM((chunks, snaps, elements, LANES), jnp.bfloat16),
-            pltpu.VMEM((snaps * elements // LANES * fields * elements, LANES), jnp.float32),
             pltpu.VMEM((mode_count, own), jnp.float32),
-            pltpu.SemaphoreType.DMA((7 + chunks,)),
+            pltpu.SemaphoreType.DMA((7,)),
         ],
-        compiler_params=pltpu.CompilerParams(vmem_limit_bytes=40 * 1024 * 1024),
     )(
         *[
             pltpu.with_memory_space_constraint(array, pltpu.HBM)
@@ -312,7 +258,6 @@
                 mass,
                 jnp.asarray(table),
                 eigvecs,
-                snapshots,
             )
         ]
     )
@@ -354,10 +299,16 @@
     chips, cols, pair = blocks // 2, mode_count // blocks, 2 * own
     factor = 0.25 / math.sqrt(elements * sections * blocks)
 
-    packet, keep = partial_sums(velocity, geometry, mass, snapshots, eigvecs, mode_order, elem_map)
-    got = exchange(packet, 0, 1)
+    stored, send, keep = stored_vorticity(velocity, geometry, mass, eigvecs, mode_order, elem_map)
+    sums = lax.dot_general(
+        stored.reshape(fields, -1),
+        snapshots.reshape(snapshots.shape[0], -1),
+        (((1,), (1,)), ((), ())),
+        preferred_element_type=jnp.float32,
+    ).reshape(-1, pair)
     count = fields * chips
-    sums = packet[:count] + got[:count]
+    got = exchange(jnp.concatenate([sums, send], axis=0), 0, 1)
+    sums = sums + got[:count]
     arrived = jnp.concatenate([got[count:, :own], got[count:, own:]], axis=0)
     second = (block & 1) != 0
     held = jnp.concatenate(

time: 21.5 us -> 21.2 us (0.986)
  the two profiles are of different devices: /device:TPU:0 before, /device:TPU:31 now
where the time goes in v6:
time: 21.2 us; the launch traced here: 21 us
  waiting for transfers between devices  14.3 us (67%)
  starting transfers between devices  2.65 us (12%)
  Pallas kernels  2.55 us (12%)
  matrix products  0.91 us (4%)
  local copies, waits for them, and re-layouts  0.37 us (2%)
    ppermute x5, waiting for transfers between devices, exchange(): return lax.ppermute(block, ('sec', 'blk'), pairs)  14.3 us
    ppermute x5, starting transfers between devices, exchange(): return lax.ppermute(block, ('sec', 'blk'), pairs)  2.65 us
    pallas_call x1, Pallas kernels, stored_vorticity(): pl.pallas_call(functools.partial(stored_kernel, blocks), out_shape=(pltpu...  1.79 us
    dot_general x1, matrix products, shards(): lax.dot_general(stored.reshape(fields, -1), snapshots.reshape(snapshots.s...  0.91 us
    pallas_call x1, Pallas kernels, shards(): pl.pallas_call(functools.partial(share_kernel, factor, chips), out_shape=...  0.76 us
  transfers between devices with their start and end apart: 5, of which 5 were waited for; matrix products, arithmetic and copies ran while one was open for 1% of the time, Pallas kernels for 0%

profile of v6, /device:TPU:31, one launch (start us, length us, event | category | flops | bytes accessed | tf_op | source)
XLA Modules:
  0.0 21.0 jit_solution(3323628449671782454)
XLA Ops:
  0.0 0.0 copy-start
  0.0 1.8 %shard_map.82 = (bf16[16,3,2,512]{3,2,1,0:T(2,128)(2,1)S(1)}, f32[64,128]{1,0:T(8,128)S(1)}, f32[128,64]{1,0:T(8,128)S(1)}) custom-call(s32[2]{0:T(128)} %map_hbm.1, s32[1,256]{1,0:T(1,128)} %bitcast.33, bf16[16,3,2,512]{3,2,1,0:T(2,128)(2,1)} %velocity_hbm.1, f32[9,2,512]{2,1,0:T(2,128)} %geometry_hbm.1, f32[2,512]{1,0:T(2,128)} %mass_hbm.1, ...), custom_call_target="tpu_custom_call" | custom-call | tf_op jit(solution)/shard_map/pallas_call | solution.py:230
  1.8 0.3 %copy-done = bf16[512,3,2,512]{3,2,1,0:T(2,128)(2,1)S(1)} copy-done((bf16[512,3,2,512]{3,2,1,0:T(2,128)(2,1)S(1)}, bf16[512,3,2,512]{3,2,1,0:T(2,128)(2,1)}, u32[]{:S(2)}) %copy-start) | copy-done | bytes 3145752
  2.1 0.9 %fusion.2 = f32[16,512]{1,0:T(8,128)S(1)} fusion(bf16[512,3,2,512]{3,2,1,0:T(2,128)(2,1)S(1)} %copy-done, bf16[16,3,2,512]{3,2,1,0:T(2,128)(2,1)S(1)} %get-tuple-element.8), kind=kOutput, calls=%fused_computation.2 | convolution fusion | flops 50331648 | bytes 3276800 | tf_op jit(solution)/shard_map/dot_general | solution.py:303
  3.0 0.7 %collective-permute-start = (f32[128,128]{1,0:T(8,128)S(1)}, f32[128,128]{1,0:T(8,128)S(1)}, u32[]{:S(2)}, u32[]{:S(2)}) collective-permute-start(f32[128,128]{1,0:T(8,128)S(1)} %pad_maximum_fusion), channel_id=1, source_target_pairs={{0,1},{1,0},{2,3},{3,2},{4,5},{5,4},{6,7},{7,6},{8,9},{9,8},{10,11... | collective-permute-start | bytes 196616 | tf_op jit(solution)/shard_map/ppermute | solution.py:273
  3.8 0.9 %collective-permute-done = f32[128,128]{1,0:T(8,128)S(1)} collective-permute-done((f32[128,128]{1,0:T(8,128)S(1)}, f32[128,128]{1,0:T(8,128)S(1)}, u32[]{:S(2)}, u32[]{:S(2)}) %collective-permute-start) | collective-permute-done | bytes 65568 | tf_op jit(solution)/shard_map/ppermute | solution.py:273
  4.7 0.5 %collective-permute-start.1 = (f32[32,128]{1,0:T(8,128)S(1)}, f32[32,128]{1,0:T(8,128)S(1)}, u32[]{:S(2)}, u32[]{:S(2)}) collective-permute-start(f32[32,128]{1,0:T(8,128)S(1)} %slice_select_fusion.2), channel_id=1, source_target_pairs={{0,17},{1,16},{2,19},{3,18},{4,21},{5,20},{6,23},{7,22},{8,25},{9,... | collective-permute-start | bytes 49160 | tf_op jit(solution)/shard_map/ppermute | solution.py:273
  5.2 0.1 fusion.9
  5.3 0.1 pad_maximum_fusion.2
  5.4 2.5 %collective-permute-done.1 = f32[32,128]{1,0:T(8,128)S(1)} collective-permute-done((f32[32,128]{1,0:T(8,128)S(1)}, f32[32,128]{1,0:T(8,128)S(1)}, u32[]{:S(2)}, u32[]{:S(2)}) %collective-permute-start.1) | collective-permute-done | bytes 16416 | tf_op jit(solution)/shard_map/ppermute | solution.py:273
  7.9 0.6 %collective-permute-start.2 = (f32[16,128]{1,0:T(8,128)S(1)}, f32[16,128]{1,0:T(8,128)S(1)}, u32[]{:S(2)}, u32[]{:S(2)}) collective-permute-start(f32[16,128]{1,0:T(8,128)S(1)} %slice_select_fusion.3), channel_id=1, source_target_pairs={{0,9},{1,8},{2,11},{3,10},{4,13},{5,12},{6,15},{7,14},{8,1},{9,0},... | collective-permute-start | bytes 24584 | tf_op jit(solution)/shard_map/ppermute | solution.py:273
  8.5 2.6 %collective-permute-done.2 = f32[16,128]{1,0:T(8,128)S(1)} collective-permute-done((f32[16,128]{1,0:T(8,128)S(1)}, f32[16,128]{1,0:T(8,128)S(1)}, u32[]{:S(2)}, u32[]{:S(2)}) %collective-permute-start.2) | collective-permute-done | bytes 8224 | tf_op jit(solution)/shard_map/ppermute | solution.py:273
  11.1 0.5 %collective-permute-start.3 = (f32[80,128]{1,0:T(8,128)S(1)}, f32[80,128]{1,0:T(8,128)S(1)}, u32[]{:S(2)}, u32[]{:S(2)}) collective-permute-start(f32[80,128]{1,0:T(8,128)S(1)} %pad_maximum_fusion.3), channel_id=1, source_target_pairs={{0,3},{1,2},{2,1},{3,0},{4,7},{5,6},{6,5},{7,4},{8,11},{9,10},{10,... | collective-permute-start | bytes 122888 | tf_op jit(solution)/shard_map/ppermute | solution.py:273
  11.6 3.1 %collective-permute-done.3 = f32[80,128]{1,0:T(8,128)S(1)} collective-permute-done((f32[80,128]{1,0:T(8,128)S(1)}, f32[80,128]{1,0:T(8,128)S(1)}, u32[]{:S(2)}, u32[]{:S(2)}) %collective-permute-start.3) | collective-permute-done | bytes 40992 | tf_op jit(solution)/shard_map/ppermute | solution.py:273
  14.7 0.4 %collective-permute-start.4 = (f32[80,128]{1,0:T(8,128)S(1)}, f32[80,128]{1,0:T(8,128)S(1)}, u32[]{:S(2)}, u32[]{:S(2)}) collective-permute-start(f32[80,128]{1,0:T(8,128)S(1)} %pad_maximum_fusion.4), channel_id=1, source_target_pairs={{0,5},{1,4},{2,7},{3,6},{4,1},{5,0},{6,3},{7,2},{8,13},{9,12},{10,... | collective-permute-start | bytes 122888 | tf_op jit(solution)/shard_map/ppermute | solution.py:273
  15.1 5.2 %collective-permute-done.4.got_ref = f32[80,128]{1,0:T(8,128)S(1)} collective-permute-done((f32[80,128]{1,0:T(8,128)S(1)}, f32[80,128]{1,0:T(8,128)S(1)}, u32[]{:S(2)}, u32[]{:S(2)}) %collective-permute-start.4) | collective-permute-done | bytes 40992 | tf_op jit(solution)/shard_map/ppermute | solution.py:273
  20.3 0.8 %shard_map.83 = f32[4,32]{1,0:T(4,128)} custom-call(f32[16,128]{1,0:T(8,128)S(1)} %slice_add_fusion.1.sums_ref, f32[80,128]{1,0:T(8,128)S(1)} %collective-permute-done.4.got_ref, f32[64,128]{1,0:T(8,128)S(1)} %bitcast.28), custom_call_target="tpu_custom_call" | custom-call | tf_op jit(solution)/shard_map/pallas_call | solution.py:349
  (15 shorter events, 0.1 us)
Async XLA Ops:
  0.0 2.1 %copy-start = (bf16[512,3,2,512]{3,2,1,0:T(2,128)(2,1)S(1)}, bf16[512,3,2,512]{3,2,1,0:T(2,128)(2,1)}, u32[]{:S(2)}) copy-start(bf16[512,3,2,512]{3,2,1,0:T(2,128)(2,1)} %param.11) | copy-start | bytes 9437188
  3.0 1.6 %collective-permute-start = (f32[128,128]{1,0:T(8,128)S(1)}, f32[128,128]{1,0:T(8,128)S(1)}, u32[]{:S(2)}, u32[]{:S(2)}) collective-permute-start(f32[128,128]{1,0:T(8,128)S(1)} %pad_maximum_fusion), channel_id=1, source_target_pairs={{0,1},{1,0},{2,3},{3,2},{4,5},{5,4},{6,7},{7,6},{8,9},{9,8},{10,11... | collective-permute-start | bytes 196616 | tf_op jit(solution)/shard_map/ppermute | solution.py:273
  4.7 3.2 %collective-permute-start.1 = (f32[32,128]{1,0:T(8,128)S(1)}, f32[32,128]{1,0:T(8,128)S(1)}, u32[]{:S(2)}, u32[]{:S(2)}) collective-permute-start(f32[32,128]{1,0:T(8,128)S(1)} %slice_select_fusion.2), channel_id=1, source_target_pairs={{0,17},{1,16},{2,19},{3,18},{4,21},{5,20},{6,23},{7,22},{8,25},{9,... | collective-permute-start | bytes 49160 | tf_op jit(solution)/shard_map/ppermute | solution.py:273
  7.9 3.1 %collective-permute-start.2 = (f32[16,128]{1,0:T(8,128)S(1)}, f32[16,128]{1,0:T(8,128)S(1)}, u32[]{:S(2)}, u32[]{:S(2)}) collective-permute-start(f32[16,128]{1,0:T(8,128)S(1)} %slice_select_fusion.3), channel_id=1, source_target_pairs={{0,9},{1,8},{2,11},{3,10},{4,13},{5,12},{6,15},{7,14},{8,1},{9,0},... | collective-permute-start | bytes 24584 | tf_op jit(solution)/shard_map/ppermute | solution.py:273
  11.1 3.6 %collective-permute-start.3 = (f32[80,128]{1,0:T(8,128)S(1)}, f32[80,128]{1,0:T(8,128)S(1)}, u32[]{:S(2)}, u32[]{:S(2)}) collective-permute-start(f32[80,128]{1,0:T(8,128)S(1)} %pad_maximum_fusion.3), channel_id=1, source_target_pairs={{0,3},{1,2},{2,1},{3,0},{4,7},{5,6},{6,5},{7,4},{8,11},{9,10},{10,... | collective-permute-start | bytes 122888 | tf_op jit(solution)/shard_map/ppermute | solution.py:273
  14.7 5.5 %collective-permute-start.4 = (f32[80,128]{1,0:T(8,128)S(1)}, f32[80,128]{1,0:T(8,128)S(1)}, u32[]{:S(2)}, u32[]{:S(2)}) collective-permute-start(f32[80,128]{1,0:T(8,128)S(1)} %pad_maximum_fusion.4), channel_id=1, source_target_pairs={{0,5},{1,4},{2,7},{3,6},{4,1},{5,0},{6,3},{7,2},{8,13},{9,12},{10,... | collective-permute-start | bytes 122888 | tf_op jit(solution)/shard_map/ppermute | solution.py:273

commit v7 on v6

--- a/solution.py
+++ b/solution.py
@@ -93,19 +93,6 @@
     for elem in range(1, elements):
         spread = jnp.where(turn == elem, rows[elem : elem + 1], spread)
     return spread
-
-
-def parity(chip):
-    return bin(chip).count("1") & 1
-
-
-def odd_block(block, blocks):
-    odd, rest = block & 1, blocks // 2
-    while rest > 1:
-        block = block >> 1
-        odd = odd ^ (block & 1)
-        rest //= 2
-    return odd
 
 
 def stored_kernel(
@@ -210,12 +197,13 @@
         jnp.dot(piece, selector, preferred_element_type=jnp.float32) for piece in halves_of(eigvecs_ref[...])
     ).T
     cols, chips = mode_count // blocks, blocks // 2
-    odd = odd_block(lax.axis_index("blk"), blocks)
+    block = lax.axis_index("blk")
+    core = block & 1
     half = mode_count // 4
     for chip in range(chips):
-        even = parity(chip)
-        keep = columns_ref[pl.ds((2 * chip + (even ^ odd)) * cols, cols), :]
-        send = columns_ref[pl.ds((2 * chip + (even ^ 1 ^ odd)) * cols, cols), :]
+        kept = jnp.where(chip == block // 2, core, 1 - core)
+        keep = columns_ref[pl.ds((2 * chip + kept) * cols, cols), :]
+        send = columns_ref[pl.ds((2 * chip + 1 - kept) * cols, cols), :]
         keep_ref[chip * cols : (chip + 1) * cols, :] = keep
         row, lane = chip * cols % half, chip * cols // half * own
         send_ref[row : row + cols, lane : lane + own] = send
@@ -273,17 +261,19 @@
     return lax.ppermute(block, ("sec", "blk"), pairs)
 
 
-def share_kernel(factor, chips, sums_ref, got_ref, held_ref, out_ref, total_ref):
-    count = sums_ref.shape[0]
-    fields, cols = out_ref.shape
-    total_ref[...] = sums_ref[...] + got_ref[:count, :]
+def share_kernel(factor, others, sums_ref, held_ref, *refs):
+    *got_refs, out_ref, total_ref = refs
+    count, chips = sums_ref.shape[0], len(others) + 1
+    fields = out_ref.shape[0]
+    total = sums_ref[...]
+    for got_ref in got_refs:
+        total += got_ref[:count, :]
+    total_ref[...] = total
     chip = lax.axis_index("blk") // 2
-    left = jnp.concatenate(
-        [total_ref[pl.ds(chip ^ n, fields, stride=chips), :] for n in range(chips)], axis=1
-    )
-    right = [ref[start + n * cols : start + (n + 1) * cols, :] for ref, start in ((held_ref, 0), (got_ref, count)) for n in range(chips // 2)]
+    left = [total_ref[pl.ds(chip ^ other, fields, stride=chips), :] for other in (0, *others)]
+    right = [held_ref[...]] + [got_ref[count:, :] for got_ref in got_refs]
     out_ref[...] = factor * lax.dot_general(
-        left,
+        jnp.concatenate(left, axis=1),
         jnp.concatenate(right, axis=1),
         (((1,), (1,)), ((), ())),
         precision=lax.Precision.HIGHEST,
@@ -313,7 +303,7 @@
     second = (block & 1) != 0
     held = jnp.concatenate(
         [jnp.where(second, arrived, keep), jnp.where(second, keep, arrived)], axis=1
-    ).reshape(chips, 1, cols, pair)
+    ).reshape(chips, cols, pair)
 
     step = sections // 2
     while step:
@@ -323,36 +313,29 @@
         sums = jnp.where(upper, high, low) + exchange(jnp.where(upper, low, high), step, 1)
         step //= 2
 
-    step = 1
-    while step < chips:
-        halves = held.reshape((held.shape[0] // 2, 2) + held.shape[1:])
-        upper = (block & (2 * step)) != 0
-        held = jnp.where(upper, halves[:, 1], halves[:, 0])
-        send = jnp.where(upper, halves[:, 0], halves[:, 1])
-        got = exchange(jnp.concatenate([sums, send.reshape(-1, pair)], axis=0), 0, (2 * step) | 1)
-        step *= 2
-        if step < chips:
-            held = jnp.concatenate([held, got[count:].reshape(held.shape)], axis=1)
-            sums = sums + got[:count]
-
-    held = held.reshape(-1, pair)
+    others = [n for n in (2,3,1) if n < chips] + list(range(4, chips))
+    chip = block // 2
+    got = []
+    for other in others:
+        packet = jnp.concatenate([sums, lax.dynamic_index_in_dim(held, chip ^ other, 0, keepdims=False)], axis=0)
+        got.append(exchange(packet, 0, 2 * other + 1))
+    held = lax.dynamic_index_in_dim(held, chip, 0, keepdims=False)
     if pair % LANES:
-        total = (sums + got[:count]).reshape(count // chips, chips, pair)
-        order = (block // 2) ^ jnp.arange(chips, dtype=jnp.int32)
+        total = sum((part[:count] for part in got), sums).reshape(count // chips, chips, pair)
         return factor * lax.dot_general(
-            jnp.take(total, order, axis=1),
-            jnp.concatenate([held, got[count:]], axis=0).reshape(chips, cols, pair),
+            jnp.take(total, chip ^ jnp.asarray([0, *others], jnp.int32), axis=1),
+            jnp.stack([held] + [part[count:] for part in got]),
             (((1, 2), (0, 2)), ((), ())),
             precision=lax.Precision.HIGHEST,
         )
     vmem = pl.BlockSpec(memory_space=pltpu.VMEM)
     return pl.pallas_call(
-        functools.partial(share_kernel, factor, chips),
+        functools.partial(share_kernel, factor, others),
         out_shape=jax.ShapeDtypeStruct((count // chips, cols), jnp.float32),
-        in_specs=[vmem] * 3,
+        in_specs=[vmem] * (2 + len(got)),
         out_specs=vmem,
         scratch_shapes=[pltpu.VMEM((count, pair), jnp.float32)],
-    )(*[pltpu.with_memory_space_constraint(array, pltpu.VMEM) for array in (sums, got, held)])
+    )(*[pltpu.with_memory_space_constraint(array, pltpu.VMEM) for array in (sums, held, *got)])
 
 
 def solution(mesh):

time: 21.2 us -> 20.7 us (0.976)
  the two profiles are of different devices: /device:TPU:31 before, /device:TPU:0 now
where the time goes in v7:
time: 20.7 us; the launch traced here: 20.6 us
  starting transfers between devices  9.36 us (45%)
  waiting for transfers between devices  7.16 us (35%)
  Pallas kernels  2.55 us (12%)
  matrix products  0.91 us (4%)
  local copies, waits for them, and re-layouts  0.37 us (2%)
    ppermute x6, starting transfers between devices, exchange(): return lax.ppermute(block, ('sec', 'blk'), pairs)  9.36 us
    ppermute x6, waiting for transfers between devices, exchange(): return lax.ppermute(block, ('sec', 'blk'), pairs)  7.16 us
    pallas_call x1, Pallas kernels, stored_vorticity(): pl.pallas_call(functools.partial(stored_kernel, blocks), out_shape=(pltpu...  1.79 us
    dot_general x1, matrix products, shards(): lax.dot_general(stored.reshape(fields, -1), snapshots.reshape(snapshots.s...  0.91 us
    pallas_call x1, Pallas kernels, shards(): pl.pallas_call(functools.partial(share_kernel, factor, others), out_shape...  0.76 us
  transfers between devices with their start and end apart: 6, of which 4 were waited for; matrix products, arithmetic and copies ran while one was open for 1% of the time, Pallas kernels for 0%

profile of v7, /device:TPU:0, one launch (start us, length us, event | category | flops | bytes accessed | tf_op | source)
XLA Modules:
  0.0 20.6 jit_solution(16440957305915215836)
XLA Ops:
  0.0 0.0 copy-start
  0.0 1.8 %shard_map.82 = (bf16[16,3,2,512]{3,2,1,0:T(2,128)(2,1)S(1)}, f32[64,128]{1,0:T(8,128)S(1)}, f32[128,64]{1,0:T(8,128)S(1)}) custom-call(s32[2]{0:T(128)} %map_hbm.1, s32[1,256]{1,0:T(1,128)} %bitcast.15, bf16[16,3,2,512]{3,2,1,0:T(2,128)(2,1)} %velocity_hbm.1, f32[9,2,512]{2,1,0:T(2,128)} %geometry_hbm.1, f32[2,512]{1,0:T(2,128)} %mass_hbm.1, ...), custom_call_target="tpu_custom_call" | custom-call | tf_op jit(solution)/shard_map/pallas_call | solution.py:218
  1.8 0.3 %copy-done = bf16[512,3,2,512]{3,2,1,0:T(2,128)(2,1)S(1)} copy-done((bf16[512,3,2,512]{3,2,1,0:T(2,128)(2,1)S(1)}, bf16[512,3,2,512]{3,2,1,0:T(2,128)(2,1)}, u32[]{:S(2)}) %copy-start) | copy-done | bytes 3145752
  2.1 0.9 %fusion.2 = f32[16,512]{1,0:T(8,128)S(1)} fusion(bf16[512,3,2,512]{3,2,1,0:T(2,128)(2,1)S(1)} %copy-done, bf16[16,3,2,512]{3,2,1,0:T(2,128)(2,1)S(1)} %get-tuple-element.8), kind=kOutput, calls=%fused_computation.2 | convolution fusion | flops 50331648 | bytes 3276800 | tf_op jit(solution)/shard_map/dot_general | solution.py:293
  3.0 0.5 %collective-permute-start = (f32[128,128]{1,0:T(8,128)S(1)}, f32[128,128]{1,0:T(8,128)S(1)}, u32[]{:S(2)}, u32[]{:S(2)}) collective-permute-start(f32[128,128]{1,0:T(8,128)S(1)} %pad_maximum_fusion), channel_id=1, source_target_pairs={{0,1},{1,0},{2,3},{3,2},{4,5},{5,4},{6,7},{7,6},{8,9},{9,8},{10,11... | collective-permute-start | bytes 196616 | tf_op jit(solution)/shard_map/ppermute | solution.py:261
  3.5 0.9 %collective-permute-done = f32[128,128]{1,0:T(8,128)S(1)} collective-permute-done((f32[128,128]{1,0:T(8,128)S(1)}, f32[128,128]{1,0:T(8,128)S(1)}, u32[]{:S(2)}, u32[]{:S(2)}) %collective-permute-start) | collective-permute-done | bytes 65568 | tf_op jit(solution)/shard_map/ppermute | solution.py:261
  4.5 2.7 %collective-permute-start.1 = (f32[32,128]{1,0:T(8,128)S(1)}, f32[32,128]{1,0:T(8,128)S(1)}, u32[]{:S(2)}, u32[]{:S(2)}) collective-permute-start(f32[32,128]{1,0:T(8,128)S(1)} %slice_select_fusion), channel_id=1, source_target_pairs={{0,17},{1,16},{2,19},{3,18},{4,21},{5,20},{6,23},{7,22},{8,25},{9,... | collective-permute-start | bytes 49160 | tf_op jit(solution)/shard_map/ppermute | solution.py:261
  7.2 0.1 fusion.8
  7.3 0.1 pad_maximum_fusion.2
  7.3 1.3 %collective-permute-done.1 = f32[32,128]{1,0:T(8,128)S(1)} collective-permute-done((f32[32,128]{1,0:T(8,128)S(1)}, f32[32,128]{1,0:T(8,128)S(1)}, u32[]{:S(2)}, u32[]{:S(2)}) %collective-permute-start.1) | collective-permute-done | bytes 16416 | tf_op jit(solution)/shard_map/ppermute | solution.py:261
  8.6 1.8 %collective-permute-start.2 = (f32[16,128]{1,0:T(8,128)S(1)}, f32[16,128]{1,0:T(8,128)S(1)}, u32[]{:S(2)}, u32[]{:S(2)}) collective-permute-start(f32[16,128]{1,0:T(8,128)S(1)} %slice_select_fusion.1), channel_id=1, source_target_pairs={{0,9},{1,8},{2,11},{3,10},{4,13},{5,12},{6,15},{7,14},{8,1},{9,0},... | collective-permute-start | bytes 24584 | tf_op jit(solution)/shard_map/ppermute | solution.py:261
  10.4 1.4 %collective-permute-done.2 = f32[16,128]{1,0:T(8,128)S(1)} collective-permute-done((f32[16,128]{1,0:T(8,128)S(1)}, f32[16,128]{1,0:T(8,128)S(1)}, u32[]{:S(2)}, u32[]{:S(2)}) %collective-permute-start.2) | collective-permute-done | bytes 8224 | tf_op jit(solution)/shard_map/ppermute | solution.py:261
  11.8 2.9 %collective-permute-start.3 = (f32[48,128]{1,0:T(8,128)S(1)}, f32[48,128]{1,0:T(8,128)S(1)}, u32[]{:S(2)}, u32[]{:S(2)}) collective-permute-start(f32[48,128]{1,0:T(8,128)S(1)} %get-tuple-element.21), channel_id=1, source_target_pairs={{0,5},{1,4},{2,7},{3,6},{4,1},{5,0},{6,3},{7,2},{8,13},{9,12},{10,... | collective-permute-start | bytes 73736 | tf_op jit(solution)/shard_map/ppermute | solution.py:261
  14.6 1.3 %collective-permute-start.4 = (f32[48,128]{1,0:T(8,128)S(1)}, f32[48,128]{1,0:T(8,128)S(1)}, u32[]{:S(2)}, u32[]{:S(2)}) collective-permute-start(f32[48,128]{1,0:T(8,128)S(1)} %get-tuple-element.20), channel_id=1, source_target_pairs={{0,7},{1,6},{2,5},{3,4},{4,3},{5,2},{6,1},{7,0},{8,15},{9,14},{10,... | collective-permute-start | bytes 73736 | tf_op jit(solution)/shard_map/ppermute | solution.py:261
  15.9 0.2 %collective-permute-start.5 = (f32[48,128]{1,0:T(8,128)S(1)}, f32[48,128]{1,0:T(8,128)S(1)}, u32[]{:S(2)}, u32[]{:S(2)}) collective-permute-start(f32[48,128]{1,0:T(8,128)S(1)} %get-tuple-element.19), channel_id=1, source_target_pairs={{0,3},{1,2},{2,1},{3,0},{4,7},{5,6},{6,5},{7,4},{8,11},{9,10},{10,... | collective-permute-start | bytes 73736 | tf_op jit(solution)/shard_map/ppermute | solution.py:261
  16.2 0.0 collective-permute-done.3.refs_0_
  16.2 3.6 %collective-permute-done.4.refs_1_ = f32[48,128]{1,0:T(8,128)S(1)} collective-permute-done((f32[48,128]{1,0:T(8,128)S(1)}, f32[48,128]{1,0:T(8,128)S(1)}, u32[]{:S(2)}, u32[]{:S(2)}) %collective-permute-start.4) | collective-permute-done | bytes 24608 | tf_op jit(solution)/shard_map/ppermute | solution.py:261
  19.8 0.0 collective-permute-done.5.refs_2_
  19.8 0.8 %shard_map.83 = f32[4,32]{1,0:T(4,128)} custom-call(f32[16,128]{1,0:T(8,128)S(1)} %select_add_fusion.1.sums_ref, f32[32,128]{1,0:T(8,128)S(1)} %get-tuple-element.16.held_ref, f32[48,128]{1,0:T(8,128)S(1)} %collective-permute-done.3.refs_0_, f32[48,128]{1,0:T(8,128)S(1)} %collective-permute-done.4.refs_1_, f32[48,128]{1,0:T(8,128)S(1)} %collective-permute-done.5.refs_2_), custom_call_target="tpu_custom_call" | custom-call | tf_op jit(solution)/shard_map/pallas_call | solution.py:332
  (10 shorter events, 0.1 us)
Async XLA Ops:
  0.0 2.1 %copy-start = (bf16[512,3,2,512]{3,2,1,0:T(2,128)(2,1)S(1)}, bf16[512,3,2,512]{3,2,1,0:T(2,128)(2,1)}, u32[]{:S(2)}) copy-start(bf16[512,3,2,512]{3,2,1,0:T(2,128)(2,1)} %param.11) | copy-start | bytes 9437188
  3.0 1.4 %collective-permute-start = (f32[128,128]{1,0:T(8,128)S(1)}, f32[128,128]{1,0:T(8,128)S(1)}, u32[]{:S(2)}, u32[]{:S(2)}) collective-permute-start(f32[128,128]{1,0:T(8,128)S(1)} %pad_maximum_fusion), channel_id=1, source_target_pairs={{0,1},{1,0},{2,3},{3,2},{4,5},{5,4},{6,7},{7,6},{8,9},{9,8},{10,11... | collective-permute-start | bytes 196616 | tf_op jit(solution)/shard_map/ppermute | solution.py:261
  4.5 4.1 %collective-permute-start.1 = (f32[32,128]{1,0:T(8,128)S(1)}, f32[32,128]{1,0:T(8,128)S(1)}, u32[]{:S(2)}, u32[]{:S(2)}) collective-permute-start(f32[32,128]{1,0:T(8,128)S(1)} %slice_select_fusion), channel_id=1, source_target_pairs={{0,17},{1,16},{2,19},{3,18},{4,21},{5,20},{6,23},{7,22},{8,25},{9,... | collective-permute-start | bytes 49160 | tf_op jit(solution)/shard_map/ppermute | solution.py:261
  8.6 3.1 %collective-permute-start.2 = (f32[16,128]{1,0:T(8,128)S(1)}, f32[16,128]{1,0:T(8,128)S(1)}, u32[]{:S(2)}, u32[]{:S(2)}) collective-permute-start(f32[16,128]{1,0:T(8,128)S(1)} %slice_select_fusion.1), channel_id=1, source_target_pairs={{0,9},{1,8},{2,11},{3,10},{4,13},{5,12},{6,15},{7,14},{8,1},{9,0},... | collective-permute-start | bytes 24584 | tf_op jit(solution)/shard_map/ppermute | solution.py:261
  11.8 4.4 %collective-permute-start.3 = (f32[48,128]{1,0:T(8,128)S(1)}, f32[48,128]{1,0:T(8,128)S(1)}, u32[]{:S(2)}, u32[]{:S(2)}) collective-permute-start(f32[48,128]{1,0:T(8,128)S(1)} %get-tuple-element.21), channel_id=1, source_target_pairs={{0,5},{1,4},{2,7},{3,6},{4,1},{5,0},{6,3},{7,2},{8,13},{9,12},{10,... | collective-permute-start | bytes 73736 | tf_op jit(solution)/shard_map/ppermute | solution.py:261
  14.6 5.2 %collective-permute-start.4 = (f32[48,128]{1,0:T(8,128)S(1)}, f32[48,128]{1,0:T(8,128)S(1)}, u32[]{:S(2)}, u32[]{:S(2)}) collective-permute-start(f32[48,128]{1,0:T(8,128)S(1)} %get-tuple-element.20), channel_id=1, source_target_pairs={{0,7},{1,6},{2,5},{3,4},{4,3},{5,2},{6,1},{7,0},{8,15},{9,14},{10,... | collective-permute-start | bytes 73736 | tf_op jit(solution)/shard_map/ppermute | solution.py:261
  15.9 3.9 %collective-permute-start.5 = (f32[48,128]{1,0:T(8,128)S(1)}, f32[48,128]{1,0:T(8,128)S(1)}, u32[]{:S(2)}, u32[]{:S(2)}) collective-permute-start(f32[48,128]{1,0:T(8,128)S(1)} %get-tuple-element.19), channel_id=1, source_target_pairs={{0,3},{1,2},{2,1},{3,0},{4,7},{5,6},{6,5},{7,4},{8,11},{9,10},{10,... | collective-permute-start | bytes 73736 | tf_op jit(solution)/shard_map/ppermute | solution.py:261

commit v8 on v7

--- a/solution.py
+++ b/solution.py
@@ -305,13 +305,12 @@
         [jnp.where(second, arrived, keep), jnp.where(second, keep, arrived)], axis=1
     ).reshape(chips, cols, pair)
 
-    step = sections // 2
-    while step:
-        count //= 2
-        upper = (section & step) != 0
-        low, high = sums[:count], sums[count:]
-        sums = jnp.where(upper, high, low) + exchange(jnp.where(upper, low, high), step, 1)
-        step //= 2
+    count //= sections
+    parts = sums.reshape(sections, count, pair)
+    sums = lax.dynamic_index_in_dim(parts, section, 0, keepdims=False)
+    for other in [n for n in (2,3,1) if n < sections] + list(range(4, sections)):
+        part = lax.dynamic_index_in_dim(parts, section ^ other, 0, keepdims=False)
+        sums = sums + exchange(part, other, 1)
 
     others = [n for n in (2,3,1) if n < chips] + list(range(4, chips))
     chip = block // 2

time: 20.7 us -> 20.2 us (0.976)
  starting transfers between devices: 9.36 us -> 8.67 us
    ppermute x6 -> x7, starting transfers between devices: 9.36 us -> 8.67 us  [exchange(): return lax.ppermute(block, ('sec', 'blk'), pairs)]
    ppermute x6 -> x7, waiting for transfers between devices: 7.16 us -> 7.35 us  [exchange(): return lax.ppermute(block, ('sec', 'blk'), pairs)]
  transfers between devices with their start and end apart: 6 -> 7, of which waited for: 4 -> 5; matrix products, arithmetic and copies ran while one was open for 1% -> 1% of each run, Pallas kernels for 0% -> 0%
where the time goes in v8:
time: 20.2 us; the launch traced here: 20.1 us
  starting transfers between devices  8.67 us (43%)
  waiting for transfers between devices  7.35 us (36%)
  Pallas kernels  2.55 us (13%)
  matrix products  0.91 us (5%)
  local copies, waits for them, and re-layouts  0.39 us (2%)
    ppermute x7, starting transfers between devices, exchange(): return lax.ppermute(block, ('sec', 'blk'), pairs)  8.67 us
    ppermute x7, waiting for transfers between devices, exchange(): return lax.ppermute(block, ('sec', 'blk'), pairs)  7.35 us
    pallas_call x1, Pallas kernels, stored_vorticity(): pl.pallas_call(functools.partial(stored_kernel, blocks), out_shape=(pltpu...  1.79 us
    dot_general x1, matrix products, shards(): lax.dot_general(stored.reshape(fields, -1), snapshots.reshape(snapshots.s...  0.91 us
    pallas_call x1, Pallas kernels, shards(): pl.pallas_call(functools.partial(share_kernel, factor, others), out_shape...  0.76 us
  transfers between devices with their start and end apart: 7, of which 5 were waited for; matrix products, arithmetic and copies ran while one was open for 1% of the time, Pallas kernels for 0%

profile of v8, /device:TPU:0, one launch (start us, length us, event | category | flops | bytes accessed | tf_op | source)
XLA Modules:
  0.0 20.1 jit_solution(8641151864382451470)
XLA Ops:
  0.0 0.0 copy-start
  0.0 1.8 %shard_map.82 = (bf16[16,3,2,512]{3,2,1,0:T(2,128)(2,1)S(1)}, f32[64,128]{1,0:T(8,128)S(1)}, f32[128,64]{1,0:T(8,128)S(1)}) custom-call(s32[2]{0:T(128)} %map_hbm.1, s32[1,256]{1,0:T(1,128)} %bitcast.30, bf16[16,3,2,512]{3,2,1,0:T(2,128)(2,1)} %velocity_hbm.1, f32[9,2,512]{2,1,0:T(2,128)} %geometry_hbm.1, f32[2,512]{1,0:T(2,128)} %mass_hbm.1, ...), custom_call_target="tpu_custom_call" | custom-call | tf_op jit(solution)/shard_map/pallas_call | solution.py:218
  1.8 0.3 %copy-done = bf16[512,3,2,512]{3,2,1,0:T(2,128)(2,1)S(1)} copy-done((bf16[512,3,2,512]{3,2,1,0:T(2,128)(2,1)S(1)}, bf16[512,3,2,512]{3,2,1,0:T(2,128)(2,1)}, u32[]{:S(2)}) %copy-start) | copy-done | bytes 3145752
  2.1 0.9 %fusion.2 = f32[16,512]{1,0:T(8,128)S(1)} fusion(bf16[512,3,2,512]{3,2,1,0:T(2,128)(2,1)S(1)} %copy-done, bf16[16,3,2,512]{3,2,1,0:T(2,128)(2,1)S(1)} %get-tuple-element.8), kind=kOutput, calls=%fused_computation.2 | convolution fusion | flops 50331648 | bytes 3276800 | tf_op jit(solution)/shard_map/dot_general | solution.py:293
  3.0 0.5 %collective-permute-start = (f32[128,128]{1,0:T(8,128)S(1)}, f32[128,128]{1,0:T(8,128)S(1)}, u32[]{:S(2)}, u32[]{:S(2)}) collective-permute-start(f32[128,128]{1,0:T(8,128)S(1)} %pad_maximum_fusion), channel_id=1, source_target_pairs={{0,1},{1,0},{2,3},{3,2},{4,5},{5,4},{6,7},{7,6},{8,9},{9,8},{10,11... | collective-permute-start | bytes 196616 | tf_op jit(solution)/shard_map/ppermute | solution.py:261
  3.5 0.9 %collective-permute-done = f32[128,128]{1,0:T(8,128)S(1)} collective-permute-done((f32[128,128]{1,0:T(8,128)S(1)}, f32[128,128]{1,0:T(8,128)S(1)}, u32[]{:S(2)}, u32[]{:S(2)}) %collective-permute-start) | collective-permute-done | bytes 65568 | tf_op jit(solution)/shard_map/ppermute | solution.py:261
  4.5 2.7 %collective-permute-start.3 = (f32[16,128]{1,0:T(8,128)S(1)}, f32[16,128]{1,0:T(8,128)S(1)}, u32[]{:S(2)}, u32[]{:S(2)}) collective-permute-start(f32[16,128]{1,0:T(8,128)S(1)} %get-tuple-element.20), channel_id=1, source_target_pairs={{0,9},{1,8},{2,11},{3,10},{4,13},{5,12},{6,15},{7,14},{8,1},{9,0},... | collective-permute-start | bytes 24584 | tf_op jit(solution)/shard_map/ppermute | solution.py:261
  7.1 1.4 %collective-permute-start.2 = (f32[16,128]{1,0:T(8,128)S(1)}, f32[16,128]{1,0:T(8,128)S(1)}, u32[]{:S(2)}, u32[]{:S(2)}) collective-permute-start(f32[16,128]{1,0:T(8,128)S(1)} %get-tuple-element.21), channel_id=1, source_target_pairs={{0,25},{1,24},{2,27},{3,26},{4,29},{5,28},{6,31},{7,30},{8,17},{9,... | collective-permute-start | bytes 24584 | tf_op jit(solution)/shard_map/ppermute | solution.py:261
  8.6 0.1 collective-permute-start.1
  8.6 0.1 fusion.10
  8.7 0.1 pad_maximum_fusion.2
  8.8 0.0 collective-permute-done.3
  8.8 2.3 %collective-permute-done.2 = f32[16,128]{1,0:T(8,128)S(1)} collective-permute-done((f32[16,128]{1,0:T(8,128)S(1)}, f32[16,128]{1,0:T(8,128)S(1)}, u32[]{:S(2)}, u32[]{:S(2)}) %collective-permute-start.2) | collective-permute-done | bytes 8224 | tf_op jit(solution)/shard_map/ppermute | solution.py:261
  11.1 0.6 %collective-permute-done.1 = f32[16,128]{1,0:T(8,128)S(1)} collective-permute-done((f32[16,128]{1,0:T(8,128)S(1)}, f32[16,128]{1,0:T(8,128)S(1)}, u32[]{:S(2)}, u32[]{:S(2)}) %collective-permute-start.1) | collective-permute-done | bytes 8224 | tf_op jit(solution)/shard_map/ppermute | solution.py:261
  11.7 2.4 %collective-permute-start.4 = (f32[48,128]{1,0:T(8,128)S(1)}, f32[48,128]{1,0:T(8,128)S(1)}, u32[]{:S(2)}, u32[]{:S(2)}) collective-permute-start(f32[48,128]{1,0:T(8,128)S(1)} %get-tuple-element.24), channel_id=1, source_target_pairs={{0,5},{1,4},{2,7},{3,6},{4,1},{5,0},{6,3},{7,2},{8,13},{9,12},{10,... | collective-permute-start | bytes 73736 | tf_op jit(solution)/shard_map/ppermute | solution.py:261
  14.1 1.3 %collective-permute-start.5 = (f32[48,128]{1,0:T(8,128)S(1)}, f32[48,128]{1,0:T(8,128)S(1)}, u32[]{:S(2)}, u32[]{:S(2)}) collective-permute-start(f32[48,128]{1,0:T(8,128)S(1)} %get-tuple-element.23), channel_id=1, source_target_pairs={{0,7},{1,6},{2,5},{3,4},{4,3},{5,2},{6,1},{7,0},{8,15},{9,14},{10,... | collective-permute-start | bytes 73736 | tf_op jit(solution)/shard_map/ppermute | solution.py:261
  15.5 0.3 %collective-permute-start.6 = (f32[48,128]{1,0:T(8,128)S(1)}, f32[48,128]{1,0:T(8,128)S(1)}, u32[]{:S(2)}, u32[]{:S(2)}) collective-permute-start(f32[48,128]{1,0:T(8,128)S(1)} %get-tuple-element.22), channel_id=1, source_target_pairs={{0,3},{1,2},{2,1},{3,0},{4,7},{5,6},{6,5},{7,4},{8,11},{9,10},{10,... | collective-permute-start | bytes 73736 | tf_op jit(solution)/shard_map/ppermute | solution.py:261
  15.7 0.2 %collective-permute-done.4.refs_0_ = f32[48,128]{1,0:T(8,128)S(1)} collective-permute-done((f32[48,128]{1,0:T(8,128)S(1)}, f32[48,128]{1,0:T(8,128)S(1)}, u32[]{:S(2)}, u32[]{:S(2)}) %collective-permute-start.4) | collective-permute-done | bytes 24608 | tf_op jit(solution)/shard_map/ppermute | solution.py:261
  16.0 3.3 %collective-permute-done.5.refs_1_ = f32[48,128]{1,0:T(8,128)S(1)} collective-permute-done((f32[48,128]{1,0:T(8,128)S(1)}, f32[48,128]{1,0:T(8,128)S(1)}, u32[]{:S(2)}, u32[]{:S(2)}) %collective-permute-start.5) | collective-permute-done | bytes 24608 | tf_op jit(solution)/shard_map/ppermute | solution.py:261
  19.3 0.0 collective-permute-done.6.refs_2_
  19.3 0.8 %shard_map.83 = f32[4,32]{1,0:T(4,128)} custom-call(f32[16,128]{1,0:T(8,128)S(1)} %fusion.9.sums_ref, f32[32,128]{1,0:T(8,128)S(1)} %get-tuple-element.16.held_ref, f32[48,128]{1,0:T(8,128)S(1)} %collective-permute-done.4.refs_0_, f32[48,128]{1,0:T(8,128)S(1)} %collective-permute-done.5.refs_1_, f32[48,128]{1,0:T(8,128)S(1)} %collective-permute-done.6.refs_2_), custom_call_target="tpu_custom_call" | custom-call | tf_op jit(solution)/shard_map/pallas_call | solution.py:331
  (8 shorter events, 0.1 us)
Async XLA Ops:
  0.0 2.1 %copy-start = (bf16[512,3,2,512]{3,2,1,0:T(2,128)(2,1)S(1)}, bf16[512,3,2,512]{3,2,1,0:T(2,128)(2,1)}, u32[]{:S(2)}) copy-start(bf16[512,3,2,512]{3,2,1,0:T(2,128)(2,1)} %param.11) | copy-start | bytes 9437188
  3.0 1.4 %collective-permute-start = (f32[128,128]{1,0:T(8,128)S(1)}, f32[128,128]{1,0:T(8,128)S(1)}, u32[]{:S(2)}, u32[]{:S(2)}) collective-permute-start(f32[128,128]{1,0:T(8,128)S(1)} %pad_maximum_fusion), channel_id=1, source_target_pairs={{0,1},{1,0},{2,3},{3,2},{4,5},{5,4},{6,7},{7,6},{8,9},{9,8},{10,11... | collective-permute-start | bytes 196616 | tf_op jit(solution)/shard_map/ppermute | solution.py:261
  4.5 4.4 %collective-permute-start.3 = (f32[16,128]{1,0:T(8,128)S(1)}, f32[16,128]{1,0:T(8,128)S(1)}, u32[]{:S(2)}, u32[]{:S(2)}) collective-permute-start(f32[16,128]{1,0:T(8,128)S(1)} %get-tuple-element.20), channel_id=1, source_target_pairs={{0,9},{1,8},{2,11},{3,10},{4,13},{5,12},{6,15},{7,14},{8,1},{9,0},... | collective-permute-start | bytes 24584 | tf_op jit(solution)/shard_map/ppermute | solution.py:261
  7.1 4.0 %collective-permute-start.2 = (f32[16,128]{1,0:T(8,128)S(1)}, f32[16,128]{1,0:T(8,128)S(1)}, u32[]{:S(2)}, u32[]{:S(2)}) collective-permute-start(f32[16,128]{1,0:T(8,128)S(1)} %get-tuple-element.21), channel_id=1, source_target_pairs={{0,25},{1,24},{2,27},{3,26},{4,29},{5,28},{6,31},{7,30},{8,17},{9,... | collective-permute-start | bytes 24584 | tf_op jit(solution)/shard_map/ppermute | solution.py:261
  8.6 3.1 %collective-permute-start.1 = (f32[16,128]{1,0:T(8,128)S(1)}, f32[16,128]{1,0:T(8,128)S(1)}, u32[]{:S(2)}, u32[]{:S(2)}) collective-permute-start(f32[16,128]{1,0:T(8,128)S(1)} %get-tuple-element.19), channel_id=1, source_target_pairs={{0,17},{1,16},{2,19},{3,18},{4,21},{5,20},{6,23},{7,22},{8,25},{9,... | collective-permute-start | bytes 24584 | tf_op jit(solution)/shard_map/ppermute | solution.py:261
  11.7 4.2 %collective-permute-start.4 = (f32[48,128]{1,0:T(8,128)S(1)}, f32[48,128]{1,0:T(8,128)S(1)}, u32[]{:S(2)}, u32[]{:S(2)}) collective-permute-start(f32[48,128]{1,0:T(8,128)S(1)} %get-tuple-element.24), channel_id=1, source_target_pairs={{0,5},{1,4},{2,7},{3,6},{4,1},{5,0},{6,3},{7,2},{8,13},{9,12},{10,... | collective-permute-start | bytes 73736 | tf_op jit(solution)/shard_map/ppermute | solution.py:261
  14.1 5.2 %collective-permute-start.5 = (f32[48,128]{1,0:T(8,128)S(1)}, f32[48,128]{1,0:T(8,128)S(1)}, u32[]{:S(2)}, u32[]{:S(2)}) collective-permute-start(f32[48,128]{1,0:T(8,128)S(1)} %get-tuple-element.23), channel_id=1, source_target_pairs={{0,7},{1,6},{2,5},{3,4},{4,3},{5,2},{6,1},{7,0},{8,15},{9,14},{10,... | collective-permute-start | bytes 73736 | tf_op jit(solution)/shard_map/ppermute | solution.py:261
  15.5 3.8 %collective-permute-start.6 = (f32[48,128]{1,0:T(8,128)S(1)}, f32[48,128]{1,0:T(8,128)S(1)}, u32[]{:S(2)}, u32[]{:S(2)}) collective-permute-start(f32[48,128]{1,0:T(8,128)S(1)} %get-tuple-element.22), channel_id=1, source_target_pairs={{0,3},{1,2},{2,1},{3,0},{4,7},{5,6},{6,5},{7,4},{8,11},{9,10},{10,... | collective-permute-start | bytes 73736 | tf_op jit(solution)/shard_map/ppermute | solution.py:261

commit v9 on v8

--- a/solution.py
+++ b/solution.py
@@ -81,9 +81,12 @@
     ).astype(np.float32)
 
 
-def halves_of(values):
-    high = values.astype(jnp.bfloat16)
-    return high, (values - high.astype(jnp.float32)).astype(jnp.bfloat16)
+def pieces_of(values):
+    pieces = []
+    for _ in range(3):
+        pieces.append(values.astype(jnp.bfloat16))
+        values = values - pieces[-1].astype(jnp.float32)
+    return pieces
 
 
 def pair_rows(rows, height):
@@ -144,10 +147,10 @@
         velocity_ref[:, c, :, p * LANES : (p + 1) * LANES].reshape(rows, LANES) for c, p in chunks
     ]
     stacked = jnp.concatenate(packed, axis=0)
-    st_high, st_low = halves_of(jnp.concatenate([table_ref[:LANES, :], table_ref[LANES : 2 * LANES, :]], axis=1))
+    st = pieces_of(jnp.concatenate([table_ref[:LANES, :], table_ref[LANES : 2 * LANES, :]], axis=1))
     along_st = jnp.dot(
-        jnp.concatenate([stacked, stacked], axis=1),
-        jnp.concatenate([st_high, st_low], axis=0),
+        jnp.concatenate([stacked] * len(st), axis=1),
+        jnp.concatenate(st, axis=0),
         preferred_element_type=jnp.float32,
     )
     point_row = table_hbm.shape[0] - parts
@@ -194,7 +197,7 @@
         lax.broadcasted_iota(jnp.int32, (mode_count, mode_count), 0) == order_ref[...]
     ).astype(jnp.bfloat16)
     columns_ref[...] = sum(
-        jnp.dot(piece, selector, preferred_element_type=jnp.float32) for piece in halves_of(eigvecs_ref[...])
+        jnp.dot(piece, selector, preferred_element_type=jnp.float32) for piece in pieces_of(eigvecs_ref[...])
     ).T
     cols, chips = mode_count // blocks, blocks // 2
     block = lax.axis_index("blk")

time: 20.2 us -> 20.2 us (level)
  no operation moved by 1% of the time
where the time goes in v9:
time: 20.2 us; the launch traced here: 20.1 us
  starting transfers between devices  8.67 us (43%)
  waiting for transfers between devices  7.35 us (36%)
  Pallas kernels  2.62 us (13%)
  matrix products  0.91 us (5%)
  local copies, waits for them, and re-layouts  0.32 us (2%)
    ppermute x7, starting transfers between devices, exchange(): return lax.ppermute(block, ('sec', 'blk'), pairs)  8.67 us
    ppermute x7, waiting for transfers between devices, exchange(): return lax.ppermute(block, ('sec', 'blk'), pairs)  7.35 us
    pallas_call x1, Pallas kernels, stored_vorticity(): pl.pallas_call(functools.partial(stored_kernel, blocks), out_shape=(pltpu...  1.86 us
    dot_general x1, matrix products, shards(): lax.dot_general(stored.reshape(fields, -1), snapshots.reshape(snapshots.s...  0.91 us
    pallas_call x1, Pallas kernels, shards(): pl.pallas_call(functools.partial(share_kernel, factor, others), out_shape...  0.76 us
  transfers between devices with their start and end apart: 7, of which 5 were waited for; matrix products, arithmetic and copies ran while one was open for 1% of the time, Pallas kernels for 0%

profile of v9, /device:TPU:0, one launch (start us, length us, event | category | flops | bytes accessed | tf_op | source)
XLA Modules:
  0.0 20.1 jit_solution(17403788030101004274)
XLA Ops:
  0.0 0.0 copy-start
  0.0 1.9 %shard_map.82 = (bf16[16,3,2,512]{3,2,1,0:T(2,128)(2,1)S(1)}, f32[64,128]{1,0:T(8,128)S(1)}, f32[128,64]{1,0:T(8,128)S(1)}) custom-call(s32[2]{0:T(128)} %map_hbm.1, s32[1,256]{1,0:T(1,128)} %bitcast.30, bf16[16,3,2,512]{3,2,1,0:T(2,128)(2,1)} %velocity_hbm.1, f32[9,2,512]{2,1,0:T(2,128)} %geometry_hbm.1, f32[2,512]{1,0:T(2,128)} %mass_hbm.1, ...), custom_call_target="tpu_custom_call" | custom-call | tf_op jit(solution)/shard_map/pallas_call | solution.py:221
  1.9 0.2 %copy-done = bf16[512,3,2,512]{3,2,1,0:T(2,128)(2,1)S(1)} copy-done((bf16[512,3,2,512]{3,2,1,0:T(2,128)(2,1)S(1)}, bf16[512,3,2,512]{3,2,1,0:T(2,128)(2,1)}, u32[]{:S(2)}) %copy-start) | copy-done | bytes 3145752
  2.1 0.9 %fusion.2 = f32[16,512]{1,0:T(8,128)S(1)} fusion(bf16[512,3,2,512]{3,2,1,0:T(2,128)(2,1)S(1)} %copy-done, bf16[16,3,2,512]{3,2,1,0:T(2,128)(2,1)S(1)} %get-tuple-element.8), kind=kOutput, calls=%fused_computation.2 | convolution fusion | flops 50331648 | bytes 3276800 | tf_op jit(solution)/shard_map/dot_general | solution.py:296
  3.0 0.5 %collective-permute-start = (f32[128,128]{1,0:T(8,128)S(1)}, f32[128,128]{1,0:T(8,128)S(1)}, u32[]{:S(2)}, u32[]{:S(2)}) collective-permute-start(f32[128,128]{1,0:T(8,128)S(1)} %pad_maximum_fusion), channel_id=1, source_target_pairs={{0,1},{1,0},{2,3},{3,2},{4,5},{5,4},{6,7},{7,6},{8,9},{9,8},{10,11... | collective-permute-start | bytes 196616 | tf_op jit(solution)/shard_map/ppermute | solution.py:264
  3.5 0.9 %collective-permute-done = f32[128,128]{1,0:T(8,128)S(1)} collective-permute-done((f32[128,128]{1,0:T(8,128)S(1)}, f32[128,128]{1,0:T(8,128)S(1)}, u32[]{:S(2)}, u32[]{:S(2)}) %collective-permute-start) | collective-permute-done | bytes 65568 | tf_op jit(solution)/shard_map/ppermute | solution.py:264
  4.5 2.7 %collective-permute-start.3 = (f32[16,128]{1,0:T(8,128)S(1)}, f32[16,128]{1,0:T(8,128)S(1)}, u32[]{:S(2)}, u32[]{:S(2)}) collective-permute-start(f32[16,128]{1,0:T(8,128)S(1)} %get-tuple-element.20), channel_id=1, source_target_pairs={{0,9},{1,8},{2,11},{3,10},{4,13},{5,12},{6,15},{7,14},{8,1},{9,0},... | collective-permute-start | bytes 24584 | tf_op jit(solution)/shard_map/ppermute | solution.py:264
  7.1 1.4 %collective-permute-start.2 = (f32[16,128]{1,0:T(8,128)S(1)}, f32[16,128]{1,0:T(8,128)S(1)}, u32[]{:S(2)}, u32[]{:S(2)}) collective-permute-start(f32[16,128]{1,0:T(8,128)S(1)} %get-tuple-element.21), channel_id=1, source_target_pairs={{0,25},{1,24},{2,27},{3,26},{4,29},{5,28},{6,31},{7,30},{8,17},{9,... | collective-permute-start | bytes 24584 | tf_op jit(solution)/shard_map/ppermute | solution.py:264
  8.6 0.1 collective-permute-start.1
  8.6 0.1 fusion.10
  8.7 0.1 pad_maximum_fusion.2
  8.8 0.0 collective-permute-done.3
  8.8 2.3 %collective-permute-done.2 = f32[16,128]{1,0:T(8,128)S(1)} collective-permute-done((f32[16,128]{1,0:T(8,128)S(1)}, f32[16,128]{1,0:T(8,128)S(1)}, u32[]{:S(2)}, u32[]{:S(2)}) %collective-permute-start.2) | collective-permute-done | bytes 8224 | tf_op jit(solution)/shard_map/ppermute | solution.py:264
  11.1 0.6 %collective-permute-done.1 = f32[16,128]{1,0:T(8,128)S(1)} collective-permute-done((f32[16,128]{1,0:T(8,128)S(1)}, f32[16,128]{1,0:T(8,128)S(1)}, u32[]{:S(2)}, u32[]{:S(2)}) %collective-permute-start.1) | collective-permute-done | bytes 8224 | tf_op jit(solution)/shard_map/ppermute | solution.py:264
  11.7 2.4 %collective-permute-start.4 = (f32[48,128]{1,0:T(8,128)S(1)}, f32[48,128]{1,0:T(8,128)S(1)}, u32[]{:S(2)}, u32[]{:S(2)}) collective-permute-start(f32[48,128]{1,0:T(8,128)S(1)} %get-tuple-element.24), channel_id=1, source_target_pairs={{0,5},{1,4},{2,7},{3,6},{4,1},{5,0},{6,3},{7,2},{8,13},{9,12},{10,... | collective-permute-start | bytes 73736 | tf_op jit(solution)/shard_map/ppermute | solution.py:264
  14.1 1.3 %collective-permute-start.5 = (f32[48,128]{1,0:T(8,128)S(1)}, f32[48,128]{1,0:T(8,128)S(1)}, u32[]{:S(2)}, u32[]{:S(2)}) collective-permute-start(f32[48,128]{1,0:T(8,128)S(1)} %get-tuple-element.23), channel_id=1, source_target_pairs={{0,7},{1,6},{2,5},{3,4},{4,3},{5,2},{6,1},{7,0},{8,15},{9,14},{10,... | collective-permute-start | bytes 73736 | tf_op jit(solution)/shard_map/ppermute | solution.py:264
  15.5 0.3 %collective-permute-start.6 = (f32[48,128]{1,0:T(8,128)S(1)}, f32[48,128]{1,0:T(8,128)S(1)}, u32[]{:S(2)}, u32[]{:S(2)}) collective-permute-start(f32[48,128]{1,0:T(8,128)S(1)} %get-tuple-element.22), channel_id=1, source_target_pairs={{0,3},{1,2},{2,1},{3,0},{4,7},{5,6},{6,5},{7,4},{8,11},{9,10},{10,... | collective-permute-start | bytes 73736 | tf_op jit(solution)/shard_map/ppermute | solution.py:264
  15.7 0.2 %collective-permute-done.4.refs_0_ = f32[48,128]{1,0:T(8,128)S(1)} collective-permute-done((f32[48,128]{1,0:T(8,128)S(1)}, f32[48,128]{1,0:T(8,128)S(1)}, u32[]{:S(2)}, u32[]{:S(2)}) %collective-permute-start.4) | collective-permute-done | bytes 24608 | tf_op jit(solution)/shard_map/ppermute | solution.py:264
  16.0 3.3 %collective-permute-done.5.refs_1_ = f32[48,128]{1,0:T(8,128)S(1)} collective-permute-done((f32[48,128]{1,0:T(8,128)S(1)}, f32[48,128]{1,0:T(8,128)S(1)}, u32[]{:S(2)}, u32[]{:S(2)}) %collective-permute-start.5) | collective-permute-done | bytes 24608 | tf_op jit(solution)/shard_map/ppermute | solution.py:264
  19.3 0.0 collective-permute-done.6.refs_2_
  19.3 0.8 %shard_map.83 = f32[4,32]{1,0:T(4,128)} custom-call(f32[16,128]{1,0:T(8,128)S(1)} %fusion.9.sums_ref, f32[32,128]{1,0:T(8,128)S(1)} %get-tuple-element.16.held_ref, f32[48,128]{1,0:T(8,128)S(1)} %collective-permute-done.4.refs_0_, f32[48,128]{1,0:T(8,128)S(1)} %collective-permute-done.5.refs_1_, f32[48,128]{1,0:T(8,128)S(1)} %collective-permute-done.6.refs_2_), custom_call_target="tpu_custom_call" | custom-call | tf_op jit(solution)/shard_map/pallas_call | solution.py:334
  (8 shorter events, 0.1 us)
Async XLA Ops:
  0.0 2.1 %copy-start = (bf16[512,3,2,512]{3,2,1,0:T(2,128)(2,1)S(1)}, bf16[512,3,2,512]{3,2,1,0:T(2,128)(2,1)}, u32[]{:S(2)}) copy-start(bf16[512,3,2,512]{3,2,1,0:T(2,128)(2,1)} %param.11) | copy-start | bytes 9437188
  3.0 1.4 %collective-permute-start = (f32[128,128]{1,0:T(8,128)S(1)}, f32[128,128]{1,0:T(8,128)S(1)}, u32[]{:S(2)}, u32[]{:S(2)}) collective-permute-start(f32[128,128]{1,0:T(8,128)S(1)} %pad_maximum_fusion), channel_id=1, source_target_pairs={{0,1},{1,0},{2,3},{3,2},{4,5},{5,4},{6,7},{7,6},{8,9},{9,8},{10,11... | collective-permute-start | bytes 196616 | tf_op jit(solution)/shard_map/ppermute | solution.py:264
  4.5 4.4 %collective-permute-start.3 = (f32[16,128]{1,0:T(8,128)S(1)}, f32[16,128]{1,0:T(8,128)S(1)}, u32[]{:S(2)}, u32[]{:S(2)}) collective-permute-start(f32[16,128]{1,0:T(8,128)S(1)} %get-tuple-element.20), channel_id=1, source_target_pairs={{0,9},{1,8},{2,11},{3,10},{4,13},{5,12},{6,15},{7,14},{8,1},{9,0},... | collective-permute-start | bytes 24584 | tf_op jit(solution)/shard_map/ppermute | solution.py:264
  7.1 4.0 %collective-permute-start.2 = (f32[16,128]{1,0:T(8,128)S(1)}, f32[16,128]{1,0:T(8,128)S(1)}, u32[]{:S(2)}, u32[]{:S(2)}) collective-permute-start(f32[16,128]{1,0:T(8,128)S(1)} %get-tuple-element.21), channel_id=1, source_target_pairs={{0,25},{1,24},{2,27},{3,26},{4,29},{5,28},{6,31},{7,30},{8,17},{9,... | collective-permute-start | bytes 24584 | tf_op jit(solution)/shard_map/ppermute | solution.py:264
  8.6 3.1 %collective-permute-start.1 = (f32[16,128]{1,0:T(8,128)S(1)}, f32[16,128]{1,0:T(8,128)S(1)}, u32[]{:S(2)}, u32[]{:S(2)}) collective-permute-start(f32[16,128]{1,0:T(8,128)S(1)} %get-tuple-element.19), channel_id=1, source_target_pairs={{0,17},{1,16},{2,19},{3,18},{4,21},{5,20},{6,23},{7,22},{8,25},{9,... | collective-permute-start | bytes 24584 | tf_op jit(solution)/shard_map/ppermute | solution.py:264
  11.7 4.2 %collective-permute-start.4 = (f32[48,128]{1,0:T(8,128)S(1)}, f32[48,128]{1,0:T(8,128)S(1)}, u32[]{:S(2)}, u32[]{:S(2)}) collective-permute-start(f32[48,128]{1,0:T(8,128)S(1)} %get-tuple-element.24), channel_id=1, source_target_pairs={{0,5},{1,4},{2,7},{3,6},{4,1},{5,0},{6,3},{7,2},{8,13},{9,12},{10,... | collective-permute-start | bytes 73736 | tf_op jit(solution)/shard_map/ppermute | solution.py:264
  14.1 5.2 %collective-permute-start.5 = (f32[48,128]{1,0:T(8,128)S(1)}, f32[48,128]{1,0:T(8,128)S(1)}, u32[]{:S(2)}, u32[]{:S(2)}) collective-permute-start(f32[48,128]{1,0:T(8,128)S(1)} %get-tuple-element.23), channel_id=1, source_target_pairs={{0,7},{1,6},{2,5},{3,4},{4,3},{5,2},{6,1},{7,0},{8,15},{9,14},{10,... | collective-permute-start | bytes 73736 | tf_op jit(solution)/shard_map/ppermute | solution.py:264
  15.5 3.8 %collective-permute-start.6 = (f32[48,128]{1,0:T(8,128)S(1)}, f32[48,128]{1,0:T(8,128)S(1)}, u32[]{:S(2)}, u32[]{:S(2)}) collective-permute-start(f32[48,128]{1,0:T(8,128)S(1)} %get-tuple-element.22), channel_id=1, source_target_pairs={{0,3},{1,2},{2,1},{3,0},{4,7},{5,6},{6,5},{7,4},{8,11},{9,10},{10,... | collective-permute-start | bytes 73736 | tf_op jit(solution)/shard_map/ppermute | solution.py:264

commit v10 on v9

--- a/solution.py
+++ b/solution.py
@@ -264,6 +264,16 @@
     return lax.ppermute(block, ("sec", "blk"), pairs)
 
 
+def pass_on(block, distance):
+    sections, blocks = lax.axis_size("sec"), lax.axis_size("blk")
+    pairs = [
+        (s * blocks + b, s * blocks + ((b + 2 * distance) % blocks ^ 1))
+        for s in range(sections)
+        for b in range(blocks)
+    ]
+    return lax.ppermute(block, ("sec", "blk"), pairs)
+
+
 def share_kernel(factor, others, sums_ref, held_ref, *refs):
     *got_refs, out_ref, total_ref = refs
     count, chips = sums_ref.shape[0], len(others) + 1
@@ -273,7 +283,7 @@
         total += got_ref[:count, :]
     total_ref[...] = total
     chip = lax.axis_index("blk") // 2
-    left = [total_ref[pl.ds(chip ^ other, fields, stride=chips), :] for other in (0, *others)]
+    left = [total_ref[pl.ds((chip + chips - other) % chips, fields, stride=chips), :] for other in (0, *others)]
     right = [held_ref[...]] + [got_ref[count:, :] for got_ref in got_refs]
     out_ref[...] = factor * lax.dot_general(
         jnp.concatenate(left, axis=1),
@@ -315,17 +325,17 @@
         part = lax.dynamic_index_in_dim(parts, section ^ other, 0, keepdims=False)
         sums = sums + exchange(part, other, 1)
 
-    others = [n for n in (2,3,1) if n < chips] + list(range(4, chips))
+    others = [n for n in (1,2,3) if n < chips] + list(range(4, chips))
     chip = block // 2
     got = []
     for other in others:
-        packet = jnp.concatenate([sums, lax.dynamic_index_in_dim(held, chip ^ other, 0, keepdims=False)], axis=0)
-        got.append(exchange(packet, 0, 2 * other + 1))
+        away = lax.dynamic_index_in_dim(held, (chip + other) % chips, 0, keepdims=False)
+        got.append(pass_on(jnp.concatenate([sums, away], axis=0), other))
     held = lax.dynamic_index_in_dim(held, chip, 0, keepdims=False)
     if pair % LANES:
         total = sum((part[:count] for part in got), sums).reshape(count // chips, chips, pair)
         return factor * lax.dot_general(
-            jnp.take(total, chip ^ jnp.asarray([0, *others], jnp.int32), axis=1),
+            jnp.take(total, (chip - jnp.asarray([0, *others], jnp.int32)) % chips, axis=1),
             jnp.stack([held] + [part[count:] for part in got]),
             (((1, 2), (0, 2)), ((), ())),
             precision=lax.Precision.HIGHEST,

time: 20.2 us -> 19.9 us (0.985)
  waiting for transfers between devices: 7.35 us -> 6 us
  starting transfers between devices: 8.67 us -> 9.69 us
    ppermute x0 -> x3, starting transfers between devices: none -> 5 us  [pass_on(): return lax.ppermute(block, ('sec', 'blk'), pairs)]
    ppermute x7 -> x4, starting transfers between devices: 8.67 us -> 4.68 us  [exchange(): return lax.ppermute(block, ('sec', 'blk'), pairs)]
    ppermute x7 -> x4, waiting for transfers between devices: 7.35 us -> 3.78 us  [exchange(): return lax.ppermute(block, ('sec', 'blk'), pairs)]
    ppermute x0 -> x3, waiting for transfers between devices: none -> 2.22 us  [pass_on(): return lax.ppermute(block, ('sec', 'blk'), pairs)]
  transfers between devices with their start and end apart: 7 -> 7, of which waited for: 5 -> 6; matrix products, arithmetic and copies ran while one was open for 1% -> 1% of each run, Pallas kernels for 0% -> 0%
where the time goes in v10:
time: 19.9 us; the launch traced here: 19.7 us
  starting transfers between devices  9.69 us (49%)
  waiting for transfers between devices  6 us (30%)
  Pallas kernels  2.63 us (13%)
  matrix products  0.91 us (5%)
  local copies, waits for them, and re-layouts  0.32 us (2%)
    ppermute x3, starting transfers between devices, pass_on(): return lax.ppermute(block, ('sec', 'blk'), pairs)  5 us
    ppermute x4, starting transfers between devices, exchange(): return lax.ppermute(block, ('sec', 'blk'), pairs)  4.68 us
    ppermute x4, waiting for transfers between devices, exchange(): return lax.ppermute(block, ('sec', 'blk'), pairs)  3.78 us
    ppermute x3, waiting for transfers between devices, pass_on(): return lax.ppermute(block, ('sec', 'blk'), pairs)  2.22 us
    pallas_call x1, Pallas kernels, stored_vorticity(): pl.pallas_call(functools.partial(stored_kernel, blocks), out_shape=(pltpu...  1.86 us
    dot_general x1, matrix products, shards(): lax.dot_general(stored.reshape(fields, -1), snapshots.reshape(snapshots.s...  0.91 us
    pallas_call x1, Pallas kernels, shards(): pl.pallas_call(functools.partial(share_kernel, factor, others), out_shape...  0.77 us
  transfers between devices with their start and end apart: 7, of which 6 were waited for; matrix products, arithmetic and copies ran while one was open for 1% of the time, Pallas kernels for 0%

profile of v10, /device:TPU:0, one launch (start us, length us, event | category | flops | bytes accessed | tf_op | source)
XLA Modules:
  0.0 19.7 jit_solution(7628183466625734379)
XLA Ops:
  0.0 0.0 copy-start
  0.0 1.9 %shard_map.82 = (bf16[16,3,2,512]{3,2,1,0:T(2,128)(2,1)S(1)}, f32[64,128]{1,0:T(8,128)S(1)}, f32[128,64]{1,0:T(8,128)S(1)}) custom-call(s32[2]{0:T(128)} %map_hbm.1, s32[1,256]{1,0:T(1,128)} %bitcast.30, bf16[16,3,2,512]{3,2,1,0:T(2,128)(2,1)} %velocity_hbm.1, f32[9,2,512]{2,1,0:T(2,128)} %geometry_hbm.1, f32[2,512]{1,0:T(2,128)} %mass_hbm.1, ...), custom_call_target="tpu_custom_call" | custom-call | tf_op jit(solution)/shard_map/pallas_call | solution.py:221
  1.9 0.2 %copy-done = bf16[512,3,2,512]{3,2,1,0:T(2,128)(2,1)S(1)} copy-done((bf16[512,3,2,512]{3,2,1,0:T(2,128)(2,1)S(1)}, bf16[512,3,2,512]{3,2,1,0:T(2,128)(2,1)}, u32[]{:S(2)}) %copy-start) | copy-done | bytes 3145752
  2.1 0.9 %fusion.2 = f32[16,512]{1,0:T(8,128)S(1)} fusion(bf16[512,3,2,512]{3,2,1,0:T(2,128)(2,1)S(1)} %copy-done, bf16[16,3,2,512]{3,2,1,0:T(2,128)(2,1)S(1)} %get-tuple-element.8), kind=kOutput, calls=%fused_computation.2 | convolution fusion | flops 50331648 | bytes 3276800 | tf_op jit(solution)/shard_map/dot_general | solution.py:306
  3.0 0.5 %collective-permute-start = (f32[128,128]{1,0:T(8,128)S(1)}, f32[128,128]{1,0:T(8,128)S(1)}, u32[]{:S(2)}, u32[]{:S(2)}) collective-permute-start(f32[128,128]{1,0:T(8,128)S(1)} %pad_maximum_fusion), channel_id=1, source_target_pairs={{0,1},{1,0},{2,3},{3,2},{4,5},{5,4},{6,7},{7,6},{8,9},{9,8},{10,11... | collective-permute-start | bytes 196616 | tf_op jit(solution)/shard_map/ppermute | solution.py:264
  3.5 0.9 %collective-permute-done = f32[128,128]{1,0:T(8,128)S(1)} collective-permute-done((f32[128,128]{1,0:T(8,128)S(1)}, f32[128,128]{1,0:T(8,128)S(1)}, u32[]{:S(2)}, u32[]{:S(2)}) %collective-permute-start) | collective-permute-done | bytes 65568 | tf_op jit(solution)/shard_map/ppermute | solution.py:264
  4.5 2.7 %collective-permute-start.3 = (f32[16,128]{1,0:T(8,128)S(1)}, f32[16,128]{1,0:T(8,128)S(1)}, u32[]{:S(2)}, u32[]{:S(2)}) collective-permute-start(f32[16,128]{1,0:T(8,128)S(1)} %get-tuple-element.20), channel_id=1, source_target_pairs={{0,9},{1,8},{2,11},{3,10},{4,13},{5,12},{6,15},{7,14},{8,1},{9,0},... | collective-permute-start | bytes 24584 | tf_op jit(solution)/shard_map/ppermute | solution.py:264
  7.1 1.4 %collective-permute-start.2 = (f32[16,128]{1,0:T(8,128)S(1)}, f32[16,128]{1,0:T(8,128)S(1)}, u32[]{:S(2)}, u32[]{:S(2)}) collective-permute-start(f32[16,128]{1,0:T(8,128)S(1)} %get-tuple-element.21), channel_id=1, source_target_pairs={{0,25},{1,24},{2,27},{3,26},{4,29},{5,28},{6,31},{7,30},{8,17},{9,... | collective-permute-start | bytes 24584 | tf_op jit(solution)/shard_map/ppermute | solution.py:264
  8.6 0.1 collective-permute-start.1
  8.6 0.1 fusion.10
  8.7 0.1 pad_maximum_fusion.2
  8.8 0.0 collective-permute-done.3
  8.8 2.3 %collective-permute-done.2 = f32[16,128]{1,0:T(8,128)S(1)} collective-permute-done((f32[16,128]{1,0:T(8,128)S(1)}, f32[16,128]{1,0:T(8,128)S(1)}, u32[]{:S(2)}, u32[]{:S(2)}) %collective-permute-start.2) | collective-permute-done | bytes 8224 | tf_op jit(solution)/shard_map/ppermute | solution.py:264
  11.1 0.6 %collective-permute-done.1 = f32[16,128]{1,0:T(8,128)S(1)} collective-permute-done((f32[16,128]{1,0:T(8,128)S(1)}, f32[16,128]{1,0:T(8,128)S(1)}, u32[]{:S(2)}, u32[]{:S(2)}) %collective-permute-start.1) | collective-permute-done | bytes 8224 | tf_op jit(solution)/shard_map/ppermute | solution.py:264
  11.7 1.3 %collective-permute-start.4 = (f32[48,128]{1,0:T(8,128)S(1)}, f32[48,128]{1,0:T(8,128)S(1)}, u32[]{:S(2)}, u32[]{:S(2)}) collective-permute-start(f32[48,128]{1,0:T(8,128)S(1)} %get-tuple-element.24), channel_id=1, source_target_pairs={{0,3},{1,2},{2,5},{3,4},{4,7},{5,6},{6,1},{7,0},{8,11},{9,10},{10,... | collective-permute-start | bytes 73736 | tf_op jit(solution)/shard_map/ppermute | solution.py:274
  13.1 2.6 %collective-permute-start.5 = (f32[48,128]{1,0:T(8,128)S(1)}, f32[48,128]{1,0:T(8,128)S(1)}, u32[]{:S(2)}, u32[]{:S(2)}) collective-permute-start(f32[48,128]{1,0:T(8,128)S(1)} %get-tuple-element.23), channel_id=1, source_target_pairs={{0,5},{1,4},{2,7},{3,6},{4,1},{5,0},{6,3},{7,2},{8,13},{9,12},{10,... | collective-permute-start | bytes 73736 | tf_op jit(solution)/shard_map/ppermute | solution.py:274
  15.7 1.0 %collective-permute-start.6 = (f32[48,128]{1,0:T(8,128)S(1)}, f32[48,128]{1,0:T(8,128)S(1)}, u32[]{:S(2)}, u32[]{:S(2)}) collective-permute-start(f32[48,128]{1,0:T(8,128)S(1)} %get-tuple-element.22), channel_id=1, source_target_pairs={{0,7},{1,6},{2,1},{3,0},{4,3},{5,2},{6,5},{7,4},{8,15},{9,14},{10,... | collective-permute-start | bytes 73736 | tf_op jit(solution)/shard_map/ppermute | solution.py:274
  16.7 0.1 collective-permute-done.4.refs_0_
  16.8 0.6 %collective-permute-done.5.refs_1_ = f32[48,128]{1,0:T(8,128)S(1)} collective-permute-done((f32[48,128]{1,0:T(8,128)S(1)}, f32[48,128]{1,0:T(8,128)S(1)}, u32[]{:S(2)}, u32[]{:S(2)}) %collective-permute-start.5) | collective-permute-done | bytes 24608 | tf_op jit(solution)/shard_map/ppermute | solution.py:274
  17.5 1.5 %collective-permute-done.6.refs_2_ = f32[48,128]{1,0:T(8,128)S(1)} collective-permute-done((f32[48,128]{1,0:T(8,128)S(1)}, f32[48,128]{1,0:T(8,128)S(1)}, u32[]{:S(2)}, u32[]{:S(2)}) %collective-permute-start.6) | collective-permute-done | bytes 24608 | tf_op jit(solution)/shard_map/ppermute | solution.py:274
  19.0 0.8 %shard_map.83 = f32[4,32]{1,0:T(4,128)} custom-call(f32[16,128]{1,0:T(8,128)S(1)} %fusion.9.sums_ref, f32[32,128]{1,0:T(8,128)S(1)} %get-tuple-element.16.held_ref, f32[48,128]{1,0:T(8,128)S(1)} %collective-permute-done.4.refs_0_, f32[48,128]{1,0:T(8,128)S(1)} %collective-permute-done.5.refs_1_, f32[48,128]{1,0:T(8,128)S(1)} %collective-permute-done.6.refs_2_), custom_call_target="tpu_custom_call" | custom-call | tf_op jit(solution)/shard_map/pallas_call | solution.py:344
  (8 shorter events, 0.1 us)
Async XLA Ops:
  0.0 2.1 %copy-start = (bf16[512,3,2,512]{3,2,1,0:T(2,128)(2,1)S(1)}, bf16[512,3,2,512]{3,2,1,0:T(2,128)(2,1)}, u32[]{:S(2)}) copy-start(bf16[512,3,2,512]{3,2,1,0:T(2,128)(2,1)} %param.11) | copy-start | bytes 9437188
  3.0 1.4 %collective-permute-start = (f32[128,128]{1,0:T(8,128)S(1)}, f32[128,128]{1,0:T(8,128)S(1)}, u32[]{:S(2)}, u32[]{:S(2)}) collective-permute-start(f32[128,128]{1,0:T(8,128)S(1)} %pad_maximum_fusion), channel_id=1, source_target_pairs={{0,1},{1,0},{2,3},{3,2},{4,5},{5,4},{6,7},{7,6},{8,9},{9,8},{10,11... | collective-permute-start | bytes 196616 | tf_op jit(solution)/shard_map/ppermute | solution.py:264
  4.5 4.4 %collective-permute-start.3 = (f32[16,128]{1,0:T(8,128)S(1)}, f32[16,128]{1,0:T(8,128)S(1)}, u32[]{:S(2)}, u32[]{:S(2)}) collective-permute-start(f32[16,128]{1,0:T(8,128)S(1)} %get-tuple-element.20), channel_id=1, source_target_pairs={{0,9},{1,8},{2,11},{3,10},{4,13},{5,12},{6,15},{7,14},{8,1},{9,0},... | collective-permute-start | bytes 24584 | tf_op jit(solution)/shard_map/ppermute | solution.py:264
  7.1 4.0 %collective-permute-start.2 = (f32[16,128]{1,0:T(8,128)S(1)}, f32[16,128]{1,0:T(8,128)S(1)}, u32[]{:S(2)}, u32[]{:S(2)}) collective-permute-start(f32[16,128]{1,0:T(8,128)S(1)} %get-tuple-element.21), channel_id=1, source_target_pairs={{0,25},{1,24},{2,27},{3,26},{4,29},{5,28},{6,31},{7,30},{8,17},{9,... | collective-permute-start | bytes 24584 | tf_op jit(solution)/shard_map/ppermute | solution.py:264
  8.6 3.1 %collective-permute-start.1 = (f32[16,128]{1,0:T(8,128)S(1)}, f32[16,128]{1,0:T(8,128)S(1)}, u32[]{:S(2)}, u32[]{:S(2)}) collective-permute-start(f32[16,128]{1,0:T(8,128)S(1)} %get-tuple-element.19), channel_id=1, source_target_pairs={{0,17},{1,16},{2,19},{3,18},{4,21},{5,20},{6,23},{7,22},{8,25},{9,... | collective-permute-start | bytes 24584 | tf_op jit(solution)/shard_map/ppermute | solution.py:264
  11.7 5.1 %collective-permute-start.4 = (f32[48,128]{1,0:T(8,128)S(1)}, f32[48,128]{1,0:T(8,128)S(1)}, u32[]{:S(2)}, u32[]{:S(2)}) collective-permute-start(f32[48,128]{1,0:T(8,128)S(1)} %get-tuple-element.24), channel_id=1, source_target_pairs={{0,3},{1,2},{2,5},{3,4},{4,7},{5,6},{6,1},{7,0},{8,11},{9,10},{10,... | collective-permute-start | bytes 73736 | tf_op jit(solution)/shard_map/ppermute | solution.py:274
  13.1 4.4 %collective-permute-start.5 = (f32[48,128]{1,0:T(8,128)S(1)}, f32[48,128]{1,0:T(8,128)S(1)}, u32[]{:S(2)}, u32[]{:S(2)}) collective-permute-start(f32[48,128]{1,0:T(8,128)S(1)} %get-tuple-element.23), channel_id=1, source_target_pairs={{0,5},{1,4},{2,7},{3,6},{4,1},{5,0},{6,3},{7,2},{8,13},{9,12},{10,... | collective-permute-start | bytes 73736 | tf_op jit(solution)/shard_map/ppermute | solution.py:274
  15.7 3.3 %collective-permute-start.6 = (f32[48,128]{1,0:T(8,128)S(1)}, f32[48,128]{1,0:T(8,128)S(1)}, u32[]{:S(2)}, u32[]{:S(2)}) collective-permute-start(f32[48,128]{1,0:T(8,128)S(1)} %get-tuple-element.22), channel_id=1, source_target_pairs={{0,7},{1,6},{2,1},{3,0},{4,3},{5,2},{6,5},{7,4},{8,15},{9,14},{10,... | collective-permute-start | bytes 73736 | tf_op jit(solution)/shard_map/ppermute | solution.py:274

commit v11 on v10

--- a/solution.py
+++ b/solution.py
@@ -264,6 +264,25 @@
     return lax.ppermute(block, ("sec", "blk"), pairs)
 
 
+def ring_place(section, sections):
+    place, shift = section, 1
+    while shift < sections:
+        place = place ^ (section >> shift)
+        shift += 1
+    return place
+
+
+def pass_round(part, distance):
+    sections, blocks = lax.axis_size("sec"), lax.axis_size("blk")
+    ring = [n ^ (n >> 1) for n in range(sections)]
+    pairs = [
+        (ring[n] * blocks + b, ring[(n + distance) % sections] * blocks + (b ^ 1))
+        for n in range(sections)
+        for b in range(blocks)
+    ]
+    return lax.ppermute(part, ("sec", "blk"), pairs)
+
+
 def pass_on(block, distance):
     sections, blocks = lax.axis_size("sec"), lax.axis_size("blk")
     pairs = [
@@ -321,9 +340,11 @@
     count //= sections
     parts = sums.reshape(sections, count, pair)
     sums = lax.dynamic_index_in_dim(parts, section, 0, keepdims=False)
-    for other in [n for n in (2,3,1) if n < sections] + list(range(4, sections)):
-        part = lax.dynamic_index_in_dim(parts, section ^ other, 0, keepdims=False)
-        sums = sums + exchange(part, other, 1)
+    place = ring_place(section, sections)
+    for other in [n for n in (2,1,3) if n < sections] + list(range(4, sections)):
+        target = (place + other) % sections
+        part = lax.dynamic_index_in_dim(parts, target ^ (target >> 1), 0, keepdims=False)
+        sums = sums + pass_round(part, other)
 
     others = [n for n in (1,2,3) if n < chips] + list(range(4, chips))
     chip = block // 2

time: 19.9 us -> 19.7 us (0.990)
  waiting for transfers between devices: 6 us -> 4.24 us
  starting transfers between devices: 9.69 us -> 11.3 us
    ppermute x0 -> x3, starting transfers between devices: none -> 5.35 us  [pass_round(): return lax.ppermute(part, ('sec', 'blk'), pairs)]
    ppermute x4 -> x1, starting transfers between devices: 4.68 us -> 0.52 us  [exchange(): return lax.ppermute(block, ('sec', 'blk'), pairs)]
    ppermute x4 -> x1, waiting for transfers between devices: 3.78 us -> 0.9 us  [exchange(): return lax.ppermute(block, ('sec', 'blk'), pairs)]
    ppermute x0 -> x3, waiting for transfers between devices: none -> 1.2 us  [pass_round(): return lax.ppermute(part, ('sec', 'blk'), pairs)]
    ppermute x3, starting transfers between devices: 5 us -> 5.4 us  [pass_on(): return lax.ppermute(block, ('sec', 'blk'), pairs)]
  transfers between devices with their start and end apart: 7 -> 7, of which waited for: 6 -> 5; matrix products, arithmetic and copies ran while one was open for 1% -> 1% of each run, Pallas kernels for 0% -> 0%
where the time goes in v11:
time: 19.7 us; the launch traced here: 19.6 us
  starting transfers between devices  11.3 us (57%)
  waiting for transfers between devices  4.24 us (22%)
  Pallas kernels  2.63 us (13%)
  matrix products  0.91 us (5%)
  local copies, waits for them, and re-layouts  0.32 us (2%)
    ppermute x3, starting transfers between devices, pass_on(): return lax.ppermute(block, ('sec', 'blk'), pairs)  5.4 us
    ppermute x3, starting transfers between devices, pass_round(): return lax.ppermute(part, ('sec', 'blk'), pairs)  5.35 us
    ppermute x3, waiting for transfers between devices, pass_on(): return lax.ppermute(block, ('sec', 'blk'), pairs)  2.14 us
    pallas_call x1, Pallas kernels, stored_vorticity(): pl.pallas_call(functools.partial(stored_kernel, blocks), out_shape=(pltpu...  1.86 us
    ppermute x3, waiting for transfers between devices, pass_round(): return lax.ppermute(part, ('sec', 'blk'), pairs)  1.2 us
    dot_general x1, matrix products, shards(): lax.dot_general(stored.reshape(fields, -1), snapshots.reshape(snapshots.s...  0.91 us
    ppermute x1, waiting for transfers between devices, exchange(): return lax.ppermute(block, ('sec', 'blk'), pairs)  0.9 us
    pallas_call x1, Pallas kernels, shards(): pl.pallas_call(functools.partial(share_kernel, factor, others), out_shape...  0.77 us
  transfers between devices with their start and end apart: 7, of which 5 were waited for; matrix products, arithmetic and copies ran while one was open for 1% of the time, Pallas kernels for 0%

profile of v11, /device:TPU:0, one launch (start us, length us, event | category | flops | bytes accessed | tf_op | source)
XLA Modules:
  0.0 19.6 jit_solution(16662429677596776299)
XLA Ops:
  0.0 0.0 copy-start
  0.0 1.9 %shard_map.82 = (bf16[16,3,2,512]{3,2,1,0:T(2,128)(2,1)S(1)}, f32[64,128]{1,0:T(8,128)S(1)}, f32[128,64]{1,0:T(8,128)S(1)}) custom-call(s32[2]{0:T(128)} %map_hbm.1, s32[1,256]{1,0:T(1,128)} %bitcast.30, bf16[16,3,2,512]{3,2,1,0:T(2,128)(2,1)} %velocity_hbm.1, f32[9,2,512]{2,1,0:T(2,128)} %geometry_hbm.1, f32[2,512]{1,0:T(2,128)} %mass_hbm.1, ...), custom_call_target="tpu_custom_call" | custom-call | tf_op jit(solution)/shard_map/pallas_call | solution.py:221
  1.9 0.2 %copy-done = bf16[512,3,2,512]{3,2,1,0:T(2,128)(2,1)S(1)} copy-done((bf16[512,3,2,512]{3,2,1,0:T(2,128)(2,1)S(1)}, bf16[512,3,2,512]{3,2,1,0:T(2,128)(2,1)}, u32[]{:S(2)}) %copy-start) | copy-done | bytes 3145752
  2.1 0.9 %fusion.2 = f32[16,512]{1,0:T(8,128)S(1)} fusion(bf16[512,3,2,512]{3,2,1,0:T(2,128)(2,1)S(1)} %copy-done, bf16[16,3,2,512]{3,2,1,0:T(2,128)(2,1)S(1)} %get-tuple-element.8), kind=kOutput, calls=%fused_computation.2 | convolution fusion | flops 50331648 | bytes 3276800 | tf_op jit(solution)/shard_map/dot_general | solution.py:325
  3.0 0.5 %collective-permute-start = (f32[128,128]{1,0:T(8,128)S(1)}, f32[128,128]{1,0:T(8,128)S(1)}, u32[]{:S(2)}, u32[]{:S(2)}) collective-permute-start(f32[128,128]{1,0:T(8,128)S(1)} %pad_maximum_fusion), channel_id=1, source_target_pairs={{0,1},{1,0},{2,3},{3,2},{4,5},{5,4},{6,7},{7,6},{8,9},{9,8},{10,11... | collective-permute-start | bytes 196616 | tf_op jit(solution)/shard_map/ppermute | solution.py:264
  3.5 0.9 %collective-permute-done = f32[128,128]{1,0:T(8,128)S(1)} collective-permute-done((f32[128,128]{1,0:T(8,128)S(1)}, f32[128,128]{1,0:T(8,128)S(1)}, u32[]{:S(2)}, u32[]{:S(2)}) %collective-permute-start) | collective-permute-done | bytes 65568 | tf_op jit(solution)/shard_map/ppermute | solution.py:264
  4.5 2.7 %collective-permute-start.3 = (f32[16,128]{1,0:T(8,128)S(1)}, f32[16,128]{1,0:T(8,128)S(1)}, u32[]{:S(2)}, u32[]{:S(2)}) collective-permute-start(f32[16,128]{1,0:T(8,128)S(1)} %get-tuple-element.20), channel_id=1, source_target_pairs={{0,17},{1,16},{2,19},{3,18},{4,21},{5,20},{6,23},{7,22},{8,1},{9,0... | collective-permute-start | bytes 24584 | tf_op jit(solution)/shard_map/ppermute | solution.py:283
  7.1 0.0 collective-permute-start.2
  7.2 2.6 %collective-permute-start.1 = (f32[16,128]{1,0:T(8,128)S(1)}, f32[16,128]{1,0:T(8,128)S(1)}, u32[]{:S(2)}, u32[]{:S(2)}) collective-permute-start(f32[16,128]{1,0:T(8,128)S(1)} %get-tuple-element.19), channel_id=1, source_target_pairs={{0,25},{1,24},{2,27},{3,26},{4,29},{5,28},{6,31},{7,30},{8,17},{9,... | collective-permute-start | bytes 24584 | tf_op jit(solution)/shard_map/ppermute | solution.py:283
  9.8 0.1 fusion.10
  9.9 0.1 pad_maximum_fusion.2
  10.0 0.0 collective-permute-done.3
  10.0 0.2 collective-permute-done.2
  10.2 1.0 %collective-permute-done.1 = f32[16,128]{1,0:T(8,128)S(1)} collective-permute-done((f32[16,128]{1,0:T(8,128)S(1)}, f32[16,128]{1,0:T(8,128)S(1)}, u32[]{:S(2)}, u32[]{:S(2)}) %collective-permute-start.1) | collective-permute-done | bytes 8224 | tf_op jit(solution)/shard_map/ppermute | solution.py:283
  11.3 1.7 %collective-permute-start.4 = (f32[48,128]{1,0:T(8,128)S(1)}, f32[48,128]{1,0:T(8,128)S(1)}, u32[]{:S(2)}, u32[]{:S(2)}) collective-permute-start(f32[48,128]{1,0:T(8,128)S(1)} %get-tuple-element.24), channel_id=1, source_target_pairs={{0,3},{1,2},{2,5},{3,4},{4,7},{5,6},{6,1},{7,0},{8,11},{9,10},{10,... | collective-permute-start | bytes 73736 | tf_op jit(solution)/shard_map/ppermute | solution.py:293
  13.0 2.5 %collective-permute-start.5 = (f32[48,128]{1,0:T(8,128)S(1)}, f32[48,128]{1,0:T(8,128)S(1)}, u32[]{:S(2)}, u32[]{:S(2)}) collective-permute-start(f32[48,128]{1,0:T(8,128)S(1)} %get-tuple-element.23), channel_id=1, source_target_pairs={{0,5},{1,4},{2,7},{3,6},{4,1},{5,0},{6,3},{7,2},{8,13},{9,12},{10,... | collective-permute-start | bytes 73736 | tf_op jit(solution)/shard_map/ppermute | solution.py:293
  15.5 1.1 %collective-permute-start.6 = (f32[48,128]{1,0:T(8,128)S(1)}, f32[48,128]{1,0:T(8,128)S(1)}, u32[]{:S(2)}, u32[]{:S(2)}) collective-permute-start(f32[48,128]{1,0:T(8,128)S(1)} %get-tuple-element.22), channel_id=1, source_target_pairs={{0,7},{1,6},{2,1},{3,0},{4,3},{5,2},{6,5},{7,4},{8,15},{9,14},{10,... | collective-permute-start | bytes 73736 | tf_op jit(solution)/shard_map/ppermute | solution.py:293
  16.7 0.0 collective-permute-done.4.refs_0_
  16.7 0.7 %collective-permute-done.5.refs_1_ = f32[48,128]{1,0:T(8,128)S(1)} collective-permute-done((f32[48,128]{1,0:T(8,128)S(1)}, f32[48,128]{1,0:T(8,128)S(1)}, u32[]{:S(2)}, u32[]{:S(2)}) %collective-permute-start.5) | collective-permute-done | bytes 24608 | tf_op jit(solution)/shard_map/ppermute | solution.py:293
  17.3 1.5 %collective-permute-done.6.refs_2_ = f32[48,128]{1,0:T(8,128)S(1)} collective-permute-done((f32[48,128]{1,0:T(8,128)S(1)}, f32[48,128]{1,0:T(8,128)S(1)}, u32[]{:S(2)}, u32[]{:S(2)}) %collective-permute-start.6) | collective-permute-done | bytes 24608 | tf_op jit(solution)/shard_map/ppermute | solution.py:293
  18.8 0.8 %shard_map.83 = f32[4,32]{1,0:T(4,128)} custom-call(f32[16,128]{1,0:T(8,128)S(1)} %fusion.9.sums_ref, f32[32,128]{1,0:T(8,128)S(1)} %get-tuple-element.16.held_ref, f32[48,128]{1,0:T(8,128)S(1)} %collective-permute-done.4.refs_0_, f32[48,128]{1,0:T(8,128)S(1)} %collective-permute-done.5.refs_1_, f32[48,128]{1,0:T(8,128)S(1)} %collective-permute-done.6.refs_2_), custom_call_target="tpu_custom_call" | custom-call | tf_op jit(solution)/shard_map/pallas_call | solution.py:365
  (8 shorter events, 0.1 us)
Async XLA Ops:
  0.0 2.1 %copy-start = (bf16[512,3,2,512]{3,2,1,0:T(2,128)(2,1)S(1)}, bf16[512,3,2,512]{3,2,1,0:T(2,128)(2,1)}, u32[]{:S(2)}) copy-start(bf16[512,3,2,512]{3,2,1,0:T(2,128)(2,1)} %param.11) | copy-start | bytes 9437188
  3.0 1.4 %collective-permute-start = (f32[128,128]{1,0:T(8,128)S(1)}, f32[128,128]{1,0:T(8,128)S(1)}, u32[]{:S(2)}, u32[]{:S(2)}) collective-permute-start(f32[128,128]{1,0:T(8,128)S(1)} %pad_maximum_fusion), channel_id=1, source_target_pairs={{0,1},{1,0},{2,3},{3,2},{4,5},{5,4},{6,7},{7,6},{8,9},{9,8},{10,11... | collective-permute-start | bytes 196616 | tf_op jit(solution)/shard_map/ppermute | solution.py:264
  4.5 5.6 %collective-permute-start.3 = (f32[16,128]{1,0:T(8,128)S(1)}, f32[16,128]{1,0:T(8,128)S(1)}, u32[]{:S(2)}, u32[]{:S(2)}) collective-permute-start(f32[16,128]{1,0:T(8,128)S(1)} %get-tuple-element.20), channel_id=1, source_target_pairs={{0,17},{1,16},{2,19},{3,18},{4,21},{5,20},{6,23},{7,22},{8,1},{9,0... | collective-permute-start | bytes 24584 | tf_op jit(solution)/shard_map/ppermute | solution.py:283
  7.1 3.1 %collective-permute-start.2 = (f32[16,128]{1,0:T(8,128)S(1)}, f32[16,128]{1,0:T(8,128)S(1)}, u32[]{:S(2)}, u32[]{:S(2)}) collective-permute-start(f32[16,128]{1,0:T(8,128)S(1)} %get-tuple-element.21), channel_id=1, source_target_pairs={{0,9},{1,8},{2,11},{3,10},{4,13},{5,12},{6,15},{7,14},{8,25},{9,24... | collective-permute-start | bytes 24584 | tf_op jit(solution)/shard_map/ppermute | solution.py:283
  7.2 4.1 %collective-permute-start.1 = (f32[16,128]{1,0:T(8,128)S(1)}, f32[16,128]{1,0:T(8,128)S(1)}, u32[]{:S(2)}, u32[]{:S(2)}) collective-permute-start(f32[16,128]{1,0:T(8,128)S(1)} %get-tuple-element.19), channel_id=1, source_target_pairs={{0,25},{1,24},{2,27},{3,26},{4,29},{5,28},{6,31},{7,30},{8,17},{9,... | collective-permute-start | bytes 24584 | tf_op jit(solution)/shard_map/ppermute | solution.py:283
  11.3 5.4 %collective-permute-start.4 = (f32[48,128]{1,0:T(8,128)S(1)}, f32[48,128]{1,0:T(8,128)S(1)}, u32[]{:S(2)}, u32[]{:S(2)}) collective-permute-start(f32[48,128]{1,0:T(8,128)S(1)} %get-tuple-element.24), channel_id=1, source_target_pairs={{0,3},{1,2},{2,5},{3,4},{4,7},{5,6},{6,1},{7,0},{8,11},{9,10},{10,... | collective-permute-start | bytes 73736 | tf_op jit(solution)/shard_map/ppermute | solution.py:293
  13.0 4.3 %collective-permute-start.5 = (f32[48,128]{1,0:T(8,128)S(1)}, f32[48,128]{1,0:T(8,128)S(1)}, u32[]{:S(2)}, u32[]{:S(2)}) collective-permute-start(f32[48,128]{1,0:T(8,128)S(1)} %get-tuple-element.23), channel_id=1, source_target_pairs={{0,5},{1,4},{2,7},{3,6},{4,1},{5,0},{6,3},{7,2},{8,13},{9,12},{10,... | collective-permute-start | bytes 73736 | tf_op jit(solution)/shard_map/ppermute | solution.py:293
  15.5 3.3 %collective-permute-start.6 = (f32[48,128]{1,0:T(8,128)S(1)}, f32[48,128]{1,0:T(8,128)S(1)}, u32[]{:S(2)}, u32[]{:S(2)}) collective-permute-start(f32[48,128]{1,0:T(8,128)S(1)} %get-tuple-element.22), channel_id=1, source_target_pairs={{0,7},{1,6},{2,1},{3,0},{4,3},{5,2},{6,5},{7,4},{8,15},{9,14},{10,... | collective-permute-start | bytes 73736 | tf_op jit(solution)/shard_map/ppermute | solution.py:293

commit v12 on v11

--- a/solution.py
+++ b/solution.py
@@ -304,12 +304,11 @@
     chip = lax.axis_index("blk") // 2
     left = [total_ref[pl.ds((chip + chips - other) % chips, fields, stride=chips), :] for other in (0, *others)]
     right = [held_ref[...]] + [got_ref[count:, :] for got_ref in got_refs]
-    out_ref[...] = factor * lax.dot_general(
-        jnp.concatenate(left, axis=1),
-        jnp.concatenate(right, axis=1),
-        (((1,), (1,)), ((), ())),
-        precision=lax.Precision.HIGHEST,
-        preferred_element_type=jnp.float32,
+    left = pieces_of(jnp.concatenate(left, axis=1))
+    right = pieces_of(jnp.concatenate(right, axis=1))
+    out_ref[...] = factor * sum(
+        lax.dot_general(left[i], right[j], (((1,), (1,)), ((), ())), preferred_element_type=jnp.float32)
+        for i, j in ((1, 0), (0, 1), (0, 0))
     )
 
 

time: 19.7 us -> 19.7 us (level)
  no operation moved by 1% of the time
where the time goes in v12:
time: 19.7 us; the launch traced here: 19.5 us
  starting transfers between devices  11.3 us (57%)
  waiting for transfers between devices  4.24 us (22%)
  Pallas kernels  2.6 us (13%)
  matrix products  0.91 us (5%)
  local copies, waits for them, and re-layouts  0.32 us (2%)
    ppermute x3, starting transfers between devices, pass_on(): return lax.ppermute(block, ('sec', 'blk'), pairs)  5.4 us
    ppermute x3, starting transfers between devices, pass_round(): return lax.ppermute(part, ('sec', 'blk'), pairs)  5.35 us
    ppermute x3, waiting for transfers between devices, pass_on(): return lax.ppermute(block, ('sec', 'blk'), pairs)  2.14 us
    pallas_call x1, Pallas kernels, stored_vorticity(): pl.pallas_call(functools.partial(stored_kernel, blocks), out_shape=(pltpu...  1.86 us
    ppermute x3, waiting for transfers between devices, pass_round(): return lax.ppermute(part, ('sec', 'blk'), pairs)  1.2 us
    dot_general x1, matrix products, shards(): lax.dot_general(stored.reshape(fields, -1), snapshots.reshape(snapshots.s...  0.91 us
    ppermute x1, waiting for transfers between devices, exchange(): return lax.ppermute(block, ('sec', 'blk'), pairs)  0.9 us
    pallas_call x1, Pallas kernels, shards(): pl.pallas_call(functools.partial(share_kernel, factor, others), out_shape...  0.74 us
  transfers between devices with their start and end apart: 7, of which 5 were waited for; matrix products, arithmetic and copies ran while one was open for 1% of the time, Pallas kernels for 0%

profile of v12, /device:TPU:0, one launch (start us, length us, event | category | flops | bytes accessed | tf_op | source)
XLA Modules:
  0.0 19.5 jit_solution(8440600711069626021)
XLA Ops:
  0.0 0.0 copy-start
  0.0 1.9 %shard_map.82 = (bf16[16,3,2,512]{3,2,1,0:T(2,128)(2,1)S(1)}, f32[64,128]{1,0:T(8,128)S(1)}, f32[128,64]{1,0:T(8,128)S(1)}) custom-call(s32[2]{0:T(128)} %map_hbm.1, s32[1,256]{1,0:T(1,128)} %bitcast.30, bf16[16,3,2,512]{3,2,1,0:T(2,128)(2,1)} %velocity_hbm.1, f32[9,2,512]{2,1,0:T(2,128)} %geometry_hbm.1, f32[2,512]{1,0:T(2,128)} %mass_hbm.1, ...), custom_call_target="tpu_custom_call" | custom-call | tf_op jit(solution)/shard_map/pallas_call | solution.py:221
  1.9 0.2 %copy-done = bf16[512,3,2,512]{3,2,1,0:T(2,128)(2,1)S(1)} copy-done((bf16[512,3,2,512]{3,2,1,0:T(2,128)(2,1)S(1)}, bf16[512,3,2,512]{3,2,1,0:T(2,128)(2,1)}, u32[]{:S(2)}) %copy-start) | copy-done | bytes 3145752
  2.1 0.9 %fusion.2 = f32[16,512]{1,0:T(8,128)S(1)} fusion(bf16[512,3,2,512]{3,2,1,0:T(2,128)(2,1)S(1)} %copy-done, bf16[16,3,2,512]{3,2,1,0:T(2,128)(2,1)S(1)} %get-tuple-element.8), kind=kOutput, calls=%fused_computation.2 | convolution fusion | flops 50331648 | bytes 3276800 | tf_op jit(solution)/shard_map/dot_general | solution.py:324
  3.0 0.5 %collective-permute-start = (f32[128,128]{1,0:T(8,128)S(1)}, f32[128,128]{1,0:T(8,128)S(1)}, u32[]{:S(2)}, u32[]{:S(2)}) collective-permute-start(f32[128,128]{1,0:T(8,128)S(1)} %pad_maximum_fusion), channel_id=1, source_target_pairs={{0,1},{1,0},{2,3},{3,2},{4,5},{5,4},{6,7},{7,6},{8,9},{9,8},{10,11... | collective-permute-start | bytes 196616 | tf_op jit(solution)/shard_map/ppermute | solution.py:264
  3.5 0.9 %collective-permute-done = f32[128,128]{1,0:T(8,128)S(1)} collective-permute-done((f32[128,128]{1,0:T(8,128)S(1)}, f32[128,128]{1,0:T(8,128)S(1)}, u32[]{:S(2)}, u32[]{:S(2)}) %collective-permute-start) | collective-permute-done | bytes 65568 | tf_op jit(solution)/shard_map/ppermute | solution.py:264
  4.5 2.7 %collective-permute-start.3 = (f32[16,128]{1,0:T(8,128)S(1)}, f32[16,128]{1,0:T(8,128)S(1)}, u32[]{:S(2)}, u32[]{:S(2)}) collective-permute-start(f32[16,128]{1,0:T(8,128)S(1)} %get-tuple-element.20), channel_id=1, source_target_pairs={{0,17},{1,16},{2,19},{3,18},{4,21},{5,20},{6,23},{7,22},{8,1},{9,0... | collective-permute-start | bytes 24584 | tf_op jit(solution)/shard_map/ppermute | solution.py:283
  7.1 0.0 collective-permute-start.2
  7.2 2.6 %collective-permute-start.1 = (f32[16,128]{1,0:T(8,128)S(1)}, f32[16,128]{1,0:T(8,128)S(1)}, u32[]{:S(2)}, u32[]{:S(2)}) collective-permute-start(f32[16,128]{1,0:T(8,128)S(1)} %get-tuple-element.19), channel_id=1, source_target_pairs={{0,25},{1,24},{2,27},{3,26},{4,29},{5,28},{6,31},{7,30},{8,17},{9,... | collective-permute-start | bytes 24584 | tf_op jit(solution)/shard_map/ppermute | solution.py:283
  9.8 0.1 fusion.10
  9.9 0.1 pad_maximum_fusion.2
  10.0 0.0 collective-permute-done.3
  10.0 0.2 collective-permute-done.2
  10.2 1.0 %collective-permute-done.1 = f32[16,128]{1,0:T(8,128)S(1)} collective-permute-done((f32[16,128]{1,0:T(8,128)S(1)}, f32[16,128]{1,0:T(8,128)S(1)}, u32[]{:S(2)}, u32[]{:S(2)}) %collective-permute-start.1) | collective-permute-done | bytes 8224 | tf_op jit(solution)/shard_map/ppermute | solution.py:283
  11.3 1.7 %collective-permute-start.4 = (f32[48,128]{1,0:T(8,128)S(1)}, f32[48,128]{1,0:T(8,128)S(1)}, u32[]{:S(2)}, u32[]{:S(2)}) collective-permute-start(f32[48,128]{1,0:T(8,128)S(1)} %get-tuple-element.24), channel_id=1, source_target_pairs={{0,3},{1,2},{2,5},{3,4},{4,7},{5,6},{6,1},{7,0},{8,11},{9,10},{10,... | collective-permute-start | bytes 73736 | tf_op jit(solution)/shard_map/ppermute | solution.py:293
  13.0 2.5 %collective-permute-start.5 = (f32[48,128]{1,0:T(8,128)S(1)}, f32[48,128]{1,0:T(8,128)S(1)}, u32[]{:S(2)}, u32[]{:S(2)}) collective-permute-start(f32[48,128]{1,0:T(8,128)S(1)} %get-tuple-element.23), channel_id=1, source_target_pairs={{0,5},{1,4},{2,7},{3,6},{4,1},{5,0},{6,3},{7,2},{8,13},{9,12},{10,... | collective-permute-start | bytes 73736 | tf_op jit(solution)/shard_map/ppermute | solution.py:293
  15.5 1.1 %collective-permute-start.6 = (f32[48,128]{1,0:T(8,128)S(1)}, f32[48,128]{1,0:T(8,128)S(1)}, u32[]{:S(2)}, u32[]{:S(2)}) collective-permute-start(f32[48,128]{1,0:T(8,128)S(1)} %get-tuple-element.22), channel_id=1, source_target_pairs={{0,7},{1,6},{2,1},{3,0},{4,3},{5,2},{6,5},{7,4},{8,15},{9,14},{10,... | collective-permute-start | bytes 73736 | tf_op jit(solution)/shard_map/ppermute | solution.py:293
  16.7 0.0 collective-permute-done.4.refs_0_
  16.7 0.7 %collective-permute-done.5.refs_1_ = f32[48,128]{1,0:T(8,128)S(1)} collective-permute-done((f32[48,128]{1,0:T(8,128)S(1)}, f32[48,128]{1,0:T(8,128)S(1)}, u32[]{:S(2)}, u32[]{:S(2)}) %collective-permute-start.5) | collective-permute-done | bytes 24608 | tf_op jit(solution)/shard_map/ppermute | solution.py:293
  17.3 1.5 %collective-permute-done.6.refs_2_ = f32[48,128]{1,0:T(8,128)S(1)} collective-permute-done((f32[48,128]{1,0:T(8,128)S(1)}, f32[48,128]{1,0:T(8,128)S(1)}, u32[]{:S(2)}, u32[]{:S(2)}) %collective-permute-start.6) | collective-permute-done | bytes 24608 | tf_op jit(solution)/shard_map/ppermute | solution.py:293
  18.8 0.7 %shard_map.83 = f32[4,32]{1,0:T(4,128)} custom-call(f32[16,128]{1,0:T(8,128)S(1)} %fusion.9.sums_ref, f32[32,128]{1,0:T(8,128)S(1)} %get-tuple-element.16.held_ref, f32[48,128]{1,0:T(8,128)S(1)} %collective-permute-done.4.refs_0_, f32[48,128]{1,0:T(8,128)S(1)} %collective-permute-done.5.refs_1_, f32[48,128]{1,0:T(8,128)S(1)} %collective-permute-done.6.refs_2_), custom_call_target="tpu_custom_call" | custom-call | tf_op jit(solution)/shard_map/pallas_call | solution.py:364
  (8 shorter events, 0.1 us)
Async XLA Ops:
  0.0 2.1 %copy-start = (bf16[512,3,2,512]{3,2,1,0:T(2,128)(2,1)S(1)}, bf16[512,3,2,512]{3,2,1,0:T(2,128)(2,1)}, u32[]{:S(2)}) copy-start(bf16[512,3,2,512]{3,2,1,0:T(2,128)(2,1)} %param.11) | copy-start | bytes 9437188
  3.0 1.4 %collective-permute-start = (f32[128,128]{1,0:T(8,128)S(1)}, f32[128,128]{1,0:T(8,128)S(1)}, u32[]{:S(2)}, u32[]{:S(2)}) collective-permute-start(f32[128,128]{1,0:T(8,128)S(1)} %pad_maximum_fusion), channel_id=1, source_target_pairs={{0,1},{1,0},{2,3},{3,2},{4,5},{5,4},{6,7},{7,6},{8,9},{9,8},{10,11... | collective-permute-start | bytes 196616 | tf_op jit(solution)/shard_map/ppermute | solution.py:264
  4.5 5.6 %collective-permute-start.3 = (f32[16,128]{1,0:T(8,128)S(1)}, f32[16,128]{1,0:T(8,128)S(1)}, u32[]{:S(2)}, u32[]{:S(2)}) collective-permute-start(f32[16,128]{1,0:T(8,128)S(1)} %get-tuple-element.20), channel_id=1, source_target_pairs={{0,17},{1,16},{2,19},{3,18},{4,21},{5,20},{6,23},{7,22},{8,1},{9,0... | collective-permute-start | bytes 24584 | tf_op jit(solution)/shard_map/ppermute | solution.py:283
  7.1 3.1 %collective-permute-start.2 = (f32[16,128]{1,0:T(8,128)S(1)}, f32[16,128]{1,0:T(8,128)S(1)}, u32[]{:S(2)}, u32[]{:S(2)}) collective-permute-start(f32[16,128]{1,0:T(8,128)S(1)} %get-tuple-element.21), channel_id=1, source_target_pairs={{0,9},{1,8},{2,11},{3,10},{4,13},{5,12},{6,15},{7,14},{8,25},{9,24... | collective-permute-start | bytes 24584 | tf_op jit(solution)/shard_map/ppermute | solution.py:283
  7.2 4.1 %collective-permute-start.1 = (f32[16,128]{1,0:T(8,128)S(1)}, f32[16,128]{1,0:T(8,128)S(1)}, u32[]{:S(2)}, u32[]{:S(2)}) collective-permute-start(f32[16,128]{1,0:T(8,128)S(1)} %get-tuple-element.19), channel_id=1, source_target_pairs={{0,25},{1,24},{2,27},{3,26},{4,29},{5,28},{6,31},{7,30},{8,17},{9,... | collective-permute-start | bytes 24584 | tf_op jit(solution)/shard_map/ppermute | solution.py:283
  11.3 5.4 %collective-permute-start.4 = (f32[48,128]{1,0:T(8,128)S(1)}, f32[48,128]{1,0:T(8,128)S(1)}, u32[]{:S(2)}, u32[]{:S(2)}) collective-permute-start(f32[48,128]{1,0:T(8,128)S(1)} %get-tuple-element.24), channel_id=1, source_target_pairs={{0,3},{1,2},{2,5},{3,4},{4,7},{5,6},{6,1},{7,0},{8,11},{9,10},{10,... | collective-permute-start | bytes 73736 | tf_op jit(solution)/shard_map/ppermute | solution.py:293
  13.0 4.3 %collective-permute-start.5 = (f32[48,128]{1,0:T(8,128)S(1)}, f32[48,128]{1,0:T(8,128)S(1)}, u32[]{:S(2)}, u32[]{:S(2)}) collective-permute-start(f32[48,128]{1,0:T(8,128)S(1)} %get-tuple-element.23), channel_id=1, source_target_pairs={{0,5},{1,4},{2,7},{3,6},{4,1},{5,0},{6,3},{7,2},{8,13},{9,12},{10,... | collective-permute-start | bytes 73736 | tf_op jit(solution)/shard_map/ppermute | solution.py:293
  15.5 3.3 %collective-permute-start.6 = (f32[48,128]{1,0:T(8,128)S(1)}, f32[48,128]{1,0:T(8,128)S(1)}, u32[]{:S(2)}, u32[]{:S(2)}) collective-permute-start(f32[48,128]{1,0:T(8,128)S(1)} %get-tuple-element.22), channel_id=1, source_target_pairs={{0,7},{1,6},{2,1},{3,0},{4,3},{5,2},{6,5},{7,4},{8,15},{9,14},{10,... | collective-permute-start | bytes 73736 | tf_op jit(solution)/shard_map/ppermute | solution.py:293
